TPU v7x, 32 devices: a whole 2x2x4 slice. The times are simulated.
32 devices in a mesh: pipe: 4 (over y, x), expert: 8 (over z, core).
Axes of the slice: x: 2, y: 2, z: 4, core: 2. Of those that a mesh axis runs over, the one named last changes fastest.
Arguments:
- out_grad: bfloat16 [4, 1024, 3840], P('pipe', 'expert'), may hold values from -1.5 to 1.5
- routes: int32 [4, 2, 1024, 2], P('pipe', None, 'expert'), may hold values from 0 to 127, as said below
- positions: int32 [4, 2, 1024, 2], P('pipe', None, 'expert'), may hold values from -1 to 1, as said below
- route_probs: bfloat16 [4, 2, 1024, 2], P('pipe', None, 'expert'), may hold values from 0.049804688 to 0.94921875
- saved_acts: bfloat16 [4, 2, 16, 2, 1024], P('pipe', None, None, None, 'expert'), may hold values from -6 to 6
- w_gate: bfloat16 [4, 3840, 1024], P('pipe', None, 'expert'), may hold values from -0.09375 to 0.09375
- w_up: bfloat16 [4, 3840, 1024], P('pipe', None, 'expert'), may hold values from -0.09375 to 0.09375
- w_down: bfloat16 [4, 1024, 3840], P('pipe', 'expert'), may hold values from -0.375 to 0.375
Outputs:
- in_grad: bfloat16 [4, 1024, 3840], P('pipe', 'expert')
- prob_grad: float32 [4, 2, 1024, 2], P('pipe', None, 'expert')
Inputs may be any that keep to these rules, and one draw needn't show every extreme that they name: `routes`: each row names two different experts. In every aligned block of 128 rows (one device's tokens for one section and step), each of the experts 0 to 3 is named by 1 to 2 rows, and at every section and step one of them is named by exactly 2 rows in every block. positions[p, t, i, k] is -1 exactly where routes[p, t, i, k] >= 4; otherwise, within the row's block, the pairs that name one expert hold the positions 0 to their count - 1, each once.
All inputs are finite; a program needn't handle non-finite values.
Results may differ from a plain program's by a relative error of at most 0.0034.
Values may be sent and summed in bfloat16 or wider, within the bound.
No kernel may reach another device: no remote copies, remote signals or barrier semaphores. Data moves between devices by JAX's collectives and lax.ppermute only.
A program may use at most 64 MiB of HBM per device.

v0:
```python
import jax
import jax.numpy as jnp
from jax import lax
from jax.sharding import PartitionSpec as P

E_FLY = 4
MOST = 2
STEPS = 2


def shifted(block, axis, distance):
    devices = range(lax.axis_size(axis))
    route = [(i - distance, i) for i in devices if i - distance in devices]
    return lax.ppermute(block, axis, route)


def pair_table(route_part, place_part):
    labels = jnp.arange(E_FLY * MOST, dtype=jnp.int32)
    pair_keys = jnp.where(place_part >= 0, route_part * MOST + place_part, -1)
    return (pair_keys.T[:, None, :] == labels[None, :, None]).astype(jnp.float32)


def assemble(current, onehot, contrib):
    select = (onehot[0] + onehot[1]).astype(jnp.bfloat16)
    delta = lax.dot_general(
        select, contrib, (((0,), (0,)), ((), ())), preferred_element_type=jnp.float32
    )
    return (current.astype(jnp.float32) + delta).astype(jnp.bfloat16)


def expert_back(slot_rows, slot_rates, stored, gate_weight, up_weight, down_weight):
    downward = lax.dot_general(
        slot_rows, down_weight, (((1,), (1,)), ((), ())), preferred_element_type=jnp.float32
    )
    gate_pre = stored[:, 0, :].astype(jnp.float32)
    upward = stored[:, 1, :].astype(jnp.float32)
    sigmoid_gate = jax.nn.sigmoid(gate_pre)
    active = gate_pre * sigmoid_gate
    hidden = active * upward
    scaled = slot_rates.astype(jnp.float32)[:, None] * downward
    grad_gate = (scaled * upward * sigmoid_gate * (1.0 + gate_pre * (1.0 - sigmoid_gate))).astype(
        jnp.bfloat16
    )
    grad_up = (scaled * active).astype(jnp.bfloat16)
    prob_terms = jnp.sum(hidden * downward, axis=1)
    back_rows = lax.dot_general(
        grad_gate, gate_weight, (((1,), (1,)), ((), ())), preferred_element_type=jnp.float32
    )
    back_rows = back_rows + lax.dot_general(
        grad_up, up_weight, (((1,), (1,)), ((), ())), preferred_element_type=jnp.float32
    )
    return (back_rows, prob_terms)


def local(out_grad, routes, positions, route_probs, saved_acts, w_gate, w_up, w_down):
    devices = lax.axis_size("expert")
    members = devices // E_FLY
    pair_count = E_FLY * MOST
    gate_weight = w_gate[0]
    up_weight = w_up[0]
    down_weight = w_down[0]
    current_grad = out_grad[0]
    features = current_grad.shape[1]
    final_grad = current_grad
    prob_rows = []
    for step_index in range(STEPS):
        route_part = routes[0, step_index]
        place_part = positions[0, step_index]
        rate_part = route_probs[0, step_index]
        onehot = pair_table(route_part, place_part)
        select = (onehot[0] + onehot[1]).astype(jnp.bfloat16)
        send_rows = jnp.dot(select, current_grad, preferred_element_type=jnp.float32).astype(
            jnp.bfloat16
        )
        send_rates = jnp.sum(
            onehot * rate_part.T.astype(jnp.float32)[:, None, :], axis=(0, 2)
        ).astype(jnp.bfloat16)
        out_rows = jnp.broadcast_to(
            send_rows.reshape(E_FLY, 1, MOST, features), (E_FLY, members, MOST, features)
        ).reshape(devices, MOST, features)
        out_rates = jnp.broadcast_to(
            send_rates.reshape(E_FLY, 1, MOST), (E_FLY, members, MOST)
        ).reshape(devices, MOST)
        got_rows, got_rates = (
            lax.all_to_all(out_rows, "expert", split_axis=0, concat_axis=0, tiled=True),
            lax.all_to_all(out_rates, "expert", split_axis=0, concat_axis=0, tiled=True),
        )
        back_rows, prob_terms = expert_back(
            got_rows.reshape(devices * MOST, features),
            got_rates.reshape(devices * MOST),
            saved_acts[0, step_index],
            gate_weight,
            up_weight,
            down_weight,
        )
        back_rows = back_rows.reshape(devices, MOST, features)
        prob_terms = prob_terms.reshape(devices, MOST)
        came_rows, came_terms = (
            lax.all_to_all(back_rows, "expert", split_axis=0, concat_axis=0, tiled=True),
            lax.all_to_all(prob_terms, "expert", split_axis=0, concat_axis=0, tiled=True),
        )
        contrib = (
            jnp.sum(came_rows.reshape(E_FLY, members, MOST, features), axis=1)
            .astype(jnp.bfloat16)
            .reshape(pair_count, features)
        )
        slot_terms = jnp.sum(came_terms.reshape(E_FLY, members, MOST), axis=1).reshape(pair_count)
        prob_rows.append(jnp.sum(onehot * slot_terms[None, :, None], axis=1).T)
        if step_index + 1 < STEPS:
            current_grad = shifted(assemble(current_grad, onehot, contrib), "pipe", -1)
        else:
            final_grad = assemble(current_grad, onehot, contrib)
    return (final_grad[None], jnp.stack(prob_rows, axis=0)[None])


def solution(mesh):
    in_specs = (
        P("pipe", "expert", None),
        P("pipe", None, "expert", None),
        P("pipe", None, "expert", None),
        P("pipe", None, "expert", None),
        P("pipe", None, None, None, "expert"),
        P("pipe", None, "expert"),
        P("pipe", None, "expert"),
        P("pipe", "expert", None),
    )
    out_specs = (P("pipe", "expert", None), P("pipe", None, "expert", None))
    return jax.shard_map(local, mesh=mesh, in_specs=in_specs, out_specs=out_specs, check_vma=False)
```

profile of v0, /device:TPU:0, one launch (start us, length us, event | category | flops | bytes accessed | tf_op | source)
XLA Modules:
  0.0 118.4 jit_solution(11239997940693848940)
XLA Ops:
  0.7 0.9 fusion.45
  1.6 1.4 %convolution_convert_fusion.1 = bf16[8,3840]{1,0:T(8,128)(2,1)S(1)} fusion(bf16[8,128]{1,0:T(8,128)(2,1)S(1)} %fusion.43, bf16[1,128,3840]{2,1,0:T(8,128)(2,1)} %param.8), kind=kOutput, calls=%fused_computation.5 | convolution fusion | flops 7895040 | bytes 1046528 | tf_op jit(solution)/shard_map/dot_general | solution.py:72
  3.0 0.7 broadcast_in_dim.46
  3.8 6.3 %all-to-all-start.1 = ((bf16[8,2,3840]{2,1,0:T(2,128)(2,1)}), bf16[8,2,3840]{2,1,0:T(2,128)(2,1)S(1)}, u32[]{:S(2)}, u32[]{:S(2)}) async-start(bf16[8,2,3840]{2,1,0:T(2,128)(2,1)} %bitcast.6), calls=%async_computation.1 | async-start | bytes 245760 | tf_op jit(solution)/shard_map/all_to_all | solution.py:85
  10.1 6.6 %all-to-all-done.1 = bf16[8,2,3840]{2,1,0:T(2,128)(2,1)S(1)} async-done(((bf16[8,2,3840]{2,1,0:T(2,128)(2,1)}), bf16[8,2,3840]{2,1,0:T(2,128)(2,1)S(1)}, u32[]{:S(2)}, u32[]{:S(2)}) %all-to-all-start.1) | async-done | bytes 122912 | tf_op jit(solution)/shard_map/all_to_all | solution.py:85
  16.8 0.5 fusion.17
  17.3 0.7 all_to_all.44
  18.0 3.3 %all-to-all-start.6 = ((f32[8,1,2]{2,1,0:T(1,128)}), f32[8,1,2]{2,1,0:T(1,128)S(1)}, u32[]{:S(2)}, u32[]{:S(2)}) async-start(f32[8,1,2]{2,1,0:T(1,128)} %bitcast.28), calls=%async_computation.6 | async-start | bytes 8192 | tf_op jit(solution)/shard_map/all_to_all | solution.py:100
  21.3 5.4 %all-to-all-done.6 = f32[8,1,2]{2,1,0:T(1,128)S(1)} async-done(((f32[8,1,2]{2,1,0:T(1,128)}), f32[8,1,2]{2,1,0:T(1,128)S(1)}, u32[]{:S(2)}, u32[]{:S(2)}) %all-to-all-start.6) | async-done | bytes 96 | tf_op jit(solution)/shard_map/all_to_all | solution.py:100
  26.8 0.1 mul.132
  26.8 0.1 select_reduce_fusion.1
  27.0 0.1 convert_element_type.168
  27.1 0.1 copy.38
  27.2 0.1 all_to_all.36
  27.3 0.1 copy.39
  27.4 7.9 %all_to_all.56 = bf16[8,1,2]{2,1,0:T(2,128)(2,1)S(1)} all-to-all(bf16[8,1,2]{2,1,0:T(2,128)(2,1)S(1)} %copy.39), channel_id=1, replica_groups=mesh['pipe'=4,'expert'=8] {'expert'}, dimensions={0} | all-to-all | bytes 64 | tf_op jit(solution)/shard_map/all_to_all | solution.py:86
  35.4 0.1 reshape.153
  35.5 0.4 fusion.6
  35.9 0.4 convolution_add_fusion.2
  36.3 0.2 reshape.145
  36.5 11.9 %all_to_all.57 = f32[8,2,3840]{2,1,0:T(2,128)S(1)} all-to-all(f32[8,2,3840]{2,1,0:T(2,128)S(1)} %reshape.145), channel_id=1, replica_groups=mesh['pipe'=4,'expert'=8] {'expert'}, dimensions={0} | all-to-all | bytes 491520 | tf_op jit(solution)/shard_map/all_to_all | solution.py:99
  48.4 0.1 bitcast_reduce_fusion.1
  48.6 0.5 fusion
  49.0 1.3 %collective-permute-start = (bf16[128,3840]{1,0:T(8,128)(2,1)S(1)}, bf16[128,3840]{1,0:T(8,128)(2,1)S(1)}, u32[]{:S(2)}, u32[]{:S(2)}) collective-permute-start(bf16[128,3840]{1,0:T(8,128)(2,1)S(1)} %fusion), channel_id=1, source_target_pairs={{8,0},{16,8},{24,16},{9,1},{17,9},{25,17},{10,2},{18,10},{26,18},{... | collective-permute-start | bytes 2949128 | tf_op jit(solution)/shard_map/ppermute | solution.py:14
  50.3 23.7 %collective-permute-done = bf16[128,3840]{1,0:T(8,128)(2,1)S(1)} collective-permute-done((bf16[128,3840]{1,0:T(8,128)(2,1)S(1)}, bf16[128,3840]{1,0:T(8,128)(2,1)S(1)}, u32[]{:S(2)}, u32[]{:S(2)}) %collective-permute-start) | collective-permute-done | bytes 983072 | tf_op jit(solution)/shard_map/ppermute | solution.py:14
  74.1 0.2 convolution_convert_fusion
  74.3 0.7 broadcast_in_dim.49
  75.1 3.4 %all-to-all-start.4 = ((bf16[8,2,3840]{2,1,0:T(2,128)(2,1)}), bf16[8,2,3840]{2,1,0:T(2,128)(2,1)S(1)}, u32[]{:S(2)}, u32[]{:S(2)}) async-start(bf16[8,2,3840]{2,1,0:T(2,128)(2,1)} %bitcast.20), calls=%async_computation.4 | async-start | bytes 245760 | tf_op jit(solution)/shard_map/all_to_all | solution.py:85
  78.5 6.6 %all-to-all-done.4 = bf16[8,2,3840]{2,1,0:T(2,128)(2,1)S(1)} async-done(((bf16[8,2,3840]{2,1,0:T(2,128)(2,1)}), bf16[8,2,3840]{2,1,0:T(2,128)(2,1)S(1)}, u32[]{:S(2)}, u32[]{:S(2)}) %all-to-all-start.4) | async-done | bytes 122912 | tf_op jit(solution)/shard_map/all_to_all | solution.py:85
  85.1 0.5 fusion.22
  85.6 0.1 all_to_all.46
  85.7 8.1 %all_to_all.58 = f32[8,1,2]{2,1,0:T(1,128)S(1)} all-to-all(f32[8,1,2]{2,1,0:T(1,128)S(1)} %bitcast.132), channel_id=1, replica_groups=mesh['pipe'=4,'expert'=8] {'expert'}, dimensions={0} | all-to-all | bytes 128 | tf_op jit(solution)/shard_map/all_to_all | solution.py:100
  93.8 0.1 mul.137
  93.9 0.1 select_reduce_fusion
  94.0 0.1 convert_element_type.189
  94.1 0.1 copy.41
  94.3 0.1 all_to_all.40
  94.3 0.1 copy.42
  94.4 7.9 %all_to_all.59 = bf16[8,1,2]{2,1,0:T(2,128)(2,1)S(1)} all-to-all(bf16[8,1,2]{2,1,0:T(2,128)(2,1)S(1)} %copy.42), channel_id=1, replica_groups=mesh['pipe'=4,'expert'=8] {'expert'}, dimensions={0} | all-to-all | bytes 64 | tf_op jit(solution)/shard_map/all_to_all | solution.py:86
  102.4 0.1 reshape.156
  102.5 0.4 fusion.4
  102.9 0.4 convolution_add_fusion.1
  103.3 0.9 reshape.149
  104.2 3.4 %all-to-all-start.5 = ((f32[8,2,3840]{2,1,0:T(2,128)}), f32[8,2,3840]{2,1,0:T(2,128)S(1)}, u32[]{:S(2)}, u32[]{:S(2)}) async-start(f32[8,2,3840]{2,1,0:T(2,128)} %reshape.149), calls=%async_computation.5 | async-start | bytes 491520 | tf_op jit(solution)/shard_map/all_to_all | solution.py:99
  107.6 0.6 maximum_bitcast_fusion
  108.2 8.7 %all-to-all-done.5 = f32[8,2,3840]{2,1,0:T(2,128)S(1)} async-done(((f32[8,2,3840]{2,1,0:T(2,128)}), f32[8,2,3840]{2,1,0:T(2,128)S(1)}, u32[]{:S(2)}, u32[]{:S(2)}) %all-to-all-start.5) | async-done | bytes 245792 | tf_op jit(solution)/shard_map/all_to_all | solution.py:99
  116.9 0.1 bitcast_reduce_fusion
  117.0 1.4 %fusion.1 = bf16[1,128,3840]{2,1,0:T(8,128)(2,1)} fusion(bf16[128,3840]{1,0:T(8,128)(2,1)S(1)} %collective-permute-done, bf16[8,128]{1,0:T(8,128)(2,1)S(1)} %fusion.44, bf16[8,3840]{1,0:T(8,128)(2,1)S(1)} %convert_element_type.200), kind=kOutput, calls=%fused_computation.7 | convolution fusion | flops 9338880 | bytes 2029568 | tf_op jit(solution)/shard_map/dot_general | solution.py:25
  (34 shorter events, 0.5 us)
Async XLA Ops:
  0.6 34.8 %copy-start = (bf16[1,3840,128]{2,1,0:T(8,128)(2,1)S(1)}, bf16[1,3840,128]{2,1,0:T(8,128)(2,1)}, u32[]{:S(2)}) copy-start(bf16[1,3840,128]{2,1,0:T(8,128)(2,1)} %param.13) | copy-start | bytes 2949124
  0.6 9.4 %copy-start.5 = (bf16[1,2,16,2,128]{4,3,2,1,0:T(2,128)(2,1)S(1)}, bf16[1,2,16,2,128]{4,3,2,1,0:T(2,128)(2,1)}, u32[]{:S(2)}) copy-start(bf16[1,2,16,2,128]{4,3,2,1,0:T(2,128)(2,1)} %param.12) | copy-start | bytes 49156
  0.7 16.2 %copy-start.2 = (bf16[1,128,3840]{2,1,0:T(8,128)(2,1)S(1)}, bf16[1,128,3840]{2,1,0:T(8,128)(2,1)}, u32[]{:S(2)}) copy-start(bf16[1,128,3840]{2,1,0:T(8,128)(2,1)} %param.15) | copy-start | bytes 2949124
  3.0 18.3 %copy-start.6 = (bf16[1,2,128,2]{2,3,1,0:T(2,128)(2,1)S(1)}, bf16[1,2,128,2]{2,3,1,0:T(2,128)(2,1)}, u32[]{:S(2)}) copy-start(bf16[1,2,128,2]{2,3,1,0:T(2,128)(2,1)} %param.11) | copy-start | bytes 3076
  3.8 13.0 %all-to-all-start.1 = ((bf16[8,2,3840]{2,1,0:T(2,128)(2,1)}), bf16[8,2,3840]{2,1,0:T(2,128)(2,1)S(1)}, u32[]{:S(2)}, u32[]{:S(2)}) async-start(bf16[8,2,3840]{2,1,0:T(2,128)(2,1)} %bitcast.6), calls=%async_computation.1 | async-start | bytes 245760 | tf_op jit(solution)/shard_map/all_to_all | solution.py:85
  16.8 19.1 %copy-start.3 = (bf16[1,3840,128]{2,1,0:T(8,128)(2,1)S(1)}, bf16[1,3840,128]{2,1,0:T(8,128)(2,1)}, u32[]{:S(2)}) copy-start(bf16[1,3840,128]{2,1,0:T(8,128)(2,1)} %param.14) | copy-start | bytes 2949124
  18.0 8.7 %all-to-all-start.6 = ((f32[8,1,2]{2,1,0:T(1,128)}), f32[8,1,2]{2,1,0:T(1,128)S(1)}, u32[]{:S(2)}, u32[]{:S(2)}) async-start(f32[8,1,2]{2,1,0:T(1,128)} %bitcast.28), calls=%async_computation.6 | async-start | bytes 8192 | tf_op jit(solution)/shard_map/all_to_all | solution.py:100
  36.3 12.2 %copy-start.1 = (bf16[1,128,3840]{2,1,0:T(8,128)(2,1)S(1)}, bf16[1,128,3840]{2,1,0:T(8,128)(2,1)}, u32[]{:S(2)}) copy-start(bf16[1,128,3840]{2,1,0:T(8,128)(2,1)} %param.8) | copy-start | bytes 2949124
  49.0 25.0 %collective-permute-start = (bf16[128,3840]{1,0:T(8,128)(2,1)S(1)}, bf16[128,3840]{1,0:T(8,128)(2,1)S(1)}, u32[]{:S(2)}, u32[]{:S(2)}) collective-permute-start(bf16[128,3840]{1,0:T(8,128)(2,1)S(1)} %fusion), channel_id=1, source_target_pairs={{8,0},{16,8},{24,16},{9,1},{17,9},{25,17},{10,2},{18,10},{26,18},{... | collective-permute-start | bytes 2949128 | tf_op jit(solution)/shard_map/ppermute | solution.py:14
  75.1 10.0 %all-to-all-start.4 = ((bf16[8,2,3840]{2,1,0:T(2,128)(2,1)}), bf16[8,2,3840]{2,1,0:T(2,128)(2,1)S(1)}, u32[]{:S(2)}, u32[]{:S(2)}) async-start(bf16[8,2,3840]{2,1,0:T(2,128)(2,1)} %bitcast.20), calls=%async_computation.4 | async-start | bytes 245760 | tf_op jit(solution)/shard_map/all_to_all | solution.py:85
  85.6 17.3 %copy-start.4 = (bf16[1,3840,128]{2,1,0:T(8,128)(2,1)S(1)}, bf16[1,3840,128]{2,1,0:T(8,128)(2,1)}, u32[]{:S(2)}) copy-start(bf16[1,3840,128]{2,1,0:T(8,128)(2,1)} %param.14) | copy-start | bytes 2949124
  104.2 12.7 %all-to-all-start.5 = ((f32[8,2,3840]{2,1,0:T(2,128)}), f32[8,2,3840]{2,1,0:T(2,128)S(1)}, u32[]{:S(2)}, u32[]{:S(2)}) async-start(f32[8,2,3840]{2,1,0:T(2,128)} %reshape.149), calls=%async_computation.5 | async-start | bytes 491520 | tf_op jit(solution)/shard_map/all_to_all | solution.py:99
where the time goes:
time: 119 us; the launch traced here: 118 us
  waiting for transfers between devices  51.1 us (43%)
  blocking collectives  35.9 us (30%)
  starting transfers between devices  17.7 us (15%)
  matrix products  6.2 us (5%)
  local copies, waits for them, and re-layouts  4.74 us (4%)
  other arithmetic  2 us (2%)
    ppermute x1, waiting for transfers between devices, shifted(): return lax.ppermute(block, axis, route)  23.7 us
    all_to_all x2, blocking collectives, local(): lax.all_to_all(out_rates, 'expert', split_axis=0, concat_axis=0, tiled=True)  15.9 us
    all_to_all x2, waiting for transfers between devices, local(): lax.all_to_all(out_rows, 'expert', split_axis=0, concat_axis=0, tiled=True)  13.2 us
    all_to_all x1, blocking collectives, local(): lax.all_to_all(back_rows, 'expert', split_axis=0, concat_axis=0, tiled=True)  11.9 us
    all_to_all x2, starting transfers between devices, local(): lax.all_to_all(out_rows, 'expert', split_axis=0, concat_axis=0, tiled=True)  9.69 us
    all_to_all x1, waiting for transfers between devices, local(): lax.all_to_all(back_rows, 'expert', split_axis=0, concat_axis=0, tiled=True)  8.73 us
    all_to_all x1, blocking collectives, local(): lax.all_to_all(prob_terms, 'expert', split_axis=0, concat_axis=0, tiled=T...  8.07 us
    all_to_all x1, waiting for transfers between devices, local(): lax.all_to_all(prob_terms, 'expert', split_axis=0, concat_axis=0, tiled=T...  5.39 us
  transfers between devices with their start and end apart: 5, of which 5 were waited for; matrix products, arithmetic and copies ran while one was open for 1% of the time, Pallas kernels for 0%

commit v1 on v0

--- a/solution.py
+++ b/solution.py
@@ -1,11 +1,313 @@
+import functools
+
 import jax
 import jax.numpy as jnp
 from jax import lax
+from jax.experimental import pallas as pl
+from jax.experimental.pallas import tpu as pltpu
 from jax.sharding import PartitionSpec as P
 
 E_FLY = 4
 MOST = 2
 STEPS = 2
+PAIRS = E_FLY * MOST
+META = 128
+CHUNK = 256
+F32 = jnp.float32
+BF16 = jnp.bfloat16
+NT = (((1,), (1,)), ((), ()))
+TN = (((0,), (0,)), ((), ()))
+
+
+def call(kernel, name, out_shape, scratch=()):
+    return pl.pallas_call(
+        kernel,
+        name=name,
+        out_shape=out_shape,
+        scratch_shapes=list(scratch),
+        compiler_params=pltpu.CompilerParams(vmem_limit_bytes=24 * 2**20),
+    )
+
+
+def place():
+    at = lax.axis_index("expert")
+    return lax.axis_index("pipe"), at // 2, at % 2
+
+
+def keys_of(routes, positions, step):
+    return jnp.where(positions[step] >= 0, routes[step] * MOST + positions[step], -1)
+
+
+def labels(rows, expert_of):
+    row = lax.broadcasted_iota(jnp.int32, (rows, 1), 0)
+    return expert_of(row // MOST) * MOST + row % MOST
+
+
+def hits(keys, label):
+    return keys[0:1] == label, keys[1:2] == label
+
+
+def one_hot(keys, label):
+    first, second = hits(keys, label)
+    return jnp.where(first | second, 1.0, 0.0).astype(F32)
+
+
+def rates_of(keys, rates, label):
+    first, second = hits(keys, label)
+    picked = jnp.where(first, rates[0:1], 0.0) + jnp.where(second, rates[1:2], 0.0)
+    return jnp.sum(picked, axis=1, keepdims=True)
+
+
+def first_lanes(columns):
+    lane = lax.broadcasted_iota(jnp.int32, (columns[0].shape[0], META), 1)
+    out = jnp.zeros(lane.shape, F32)
+    for index, column in enumerate(columns):
+        out = jnp.where(lane == index, column, out)
+    return out
+
+
+def put_rows(outs, rows, meta):
+    width = rows.shape[1]
+    for k, out in enumerate(outs):
+        out[:, :width] = rows[MOST * k:MOST * (k + 1)].astype(BF16)
+        out[:, width:] = meta[MOST * k:MOST * (k + 1)].astype(BF16)
+
+
+def take_rows(scratch, refs):
+    for k, ref in enumerate(refs):
+        scratch[MOST * k:MOST * (k + 1), :] = ref[...].astype(F32)
+
+
+def pick_kernel(grad, routes, positions, probs, *outs):
+    _, z, _ = place()
+    keys = keys_of(routes, positions, 0)
+    label = labels(PAIRS, lambda k: (z + k) % E_FLY)
+    select = one_hot(keys, label)
+    rows = jnp.dot(select.astype(BF16), grad[...], preferred_element_type=F32)
+    rate = rates_of(keys, probs[0].astype(F32), label)
+    put_rows(outs[:E_FLY], rows, first_lanes([rate]))
+    table = outs[E_FLY]
+    table[0:2] = keys_of(routes, positions, 1).astype(F32)
+    table[2:4] = probs[1].astype(F32)
+
+
+def ahead_kernel(grad, routes, positions, table, acts, acts_other, *refs):
+    outs, factors, gate_at, up_at = refs[:E_FLY], *refs[E_FLY:]
+    p, z, c = place()
+    keys0 = keys_of(routes, positions, 0)
+    keys1 = table[0:2].astype(jnp.int32)
+    keys1 = jnp.where(p == 0, -1, keys1)
+    label = labels(PAIRS, lambda k: (z + k) % E_FLY)
+    select = one_hot(keys1, label)
+    rows = jnp.dot(select.astype(BF16), grad[...], preferred_element_type=F32)
+    rate = rates_of(keys1, table[2:4], label)
+    lane = lax.broadcasted_iota(jnp.int32, (PAIRS, META), 1)
+    meta = jnp.where(lane == E_FLY * PAIRS, rate, 0.0)
+    column = lax.broadcasted_iota(jnp.int32, (META, 1), 0)
+    source, block, spot = column // PAIRS, column // MOST % E_FLY, column % MOST
+    row = lax.broadcasted_iota(jnp.int32, (PAIRS, 1), 0)
+    for k in range(E_FLY):
+        expert = (z + k + E_FLY - source) % E_FLY
+        own = (source < E_FLY) & ((source + block) % E_FLY == k)
+        step0 = one_hot(keys0, jnp.where(own, expert * MOST + spot, -2))
+        match = lax.dot_general(
+            select.astype(BF16), step0.astype(BF16), NT, preferred_element_type=F32
+        )
+        meta = meta + jnp.where(row // MOST == k, match, 0.0)
+    put_rows(outs, rows, meta)
+    for step in range(STEPS):
+        for k in range(E_FLY):
+            first = (2 * ((z + E_FLY - k) % E_FLY) + c) * MOST
+            for spot_at in range(MOST):
+                at = MOST * k + spot_at
+                for half, ref in enumerate((acts, acts_other)):
+                    pair = ref[step, first + spot_at].astype(F32)
+                    width = pair.shape[1]
+                    gate_at[at:at + 1, half * width:(half + 1) * width] = pair[0:1]
+                    up_at[at:at + 1, half * width:(half + 1) * width] = pair[1:2]
+        gate, up = gate_at[...], up_at[...]
+        sigmoid = 1.0 / (1.0 + jnp.exp(-gate))
+        active = gate * sigmoid
+        factors[step, 0] = up * sigmoid * (1.0 + gate * (1.0 - sigmoid))
+        factors[step, 1] = active
+        factors[step, 2] = active * up
+
+
+def expert_rows(rows, rate, factors, step, weights):
+    down, down_other, gate, gate_other, up, up_other = weights
+    features = rows.shape[1]
+    v = jnp.zeros((rows.shape[0], 2 * down.shape[0]), F32)
+    for at in range(0, features, CHUNK):
+        part = slice(at, at + CHUNK)
+        both = jnp.concatenate([down[:, part], down_other[:, part]], axis=0)
+        v = v + lax.dot_general(rows[:, part], both, NT, preferred_element_type=F32)
+    scaled = rate * v
+    grad_gate = (scaled * factors[step, 0]).astype(BF16)
+    grad_up = (scaled * factors[step, 1]).astype(BF16)
+    terms = jnp.sum(factors[step, 2] * v, axis=1, keepdims=True)
+    grads = jnp.concatenate([grad_gate, grad_up], axis=1)
+
+    def back(part):
+        wide = jnp.concatenate(
+            [gate[part], gate_other[part], up[part], up_other[part]], axis=1
+        )
+        return lax.dot_general(grads, wide, NT, preferred_element_type=F32)
+
+    return back, terms
+
+
+def step_zero_kernel(*refs):
+    got, ahead, (routes, positions, factors) = refs[:4], refs[4:8], refs[8:11]
+    weights, (rows_out, ahead_out, terms_out, rows_at) = refs[11:17], refs[17:]
+    p, z, _ = place()
+    take_rows(rows_at, got)
+    features = rows_at.shape[1] - META
+    rate = rows_at[:, features:features + 1]
+    back, terms = expert_rows(rows_at[:, :features].astype(BF16), rate, factors, 0, weights)
+    terms_out[...] = jnp.broadcast_to(terms, terms_out.shape)
+    for at in range(0, features, CHUNK):
+        rows_out[:, at:at + CHUNK] = back(slice(at, at + CHUNK)).astype(BF16)
+    keys = keys_of(routes, positions, 0)
+    keys = jnp.where(p == 0, -1, keys)
+    select = one_hot(keys, labels(PAIRS, lambda k: (z + k) % E_FLY))
+    rows_out[:, features:] = select.astype(BF16)
+    take_rows(rows_at, ahead)
+    ahead_out[...] = rows_at[...].astype(BF16)
+
+
+def split(value):
+    high = value.astype(BF16).astype(F32)
+    middle = (value - high).astype(BF16).astype(F32)
+    return [high, middle, value - high - middle]
+
+
+def step_one_kernel(*refs):
+    came, (ahead, factors, terms0) = refs[:4], refs[4:7]
+    weights, outs = refs[7:13], refs[13:17]
+    features = ahead.shape[1] - META
+    meta = ahead[:, features:]
+    rate = meta[:, E_FLY * PAIRS:E_FLY * PAIRS + 1].astype(F32)
+    match = meta[:, :E_FLY * PAIRS]
+    everything = jnp.concatenate([ref[:, :features] for ref in came], axis=0)
+    rows = ahead[:, :features].astype(F32) + jnp.dot(
+        match, everything, preferred_element_type=F32
+    )
+    back, terms = expert_rows(rows.astype(BF16), rate, factors, 1, weights)
+    for at in range(0, features, CHUNK):
+        part = back(slice(at, at + CHUNK))
+        for k, out in enumerate(outs):
+            out[:, at:at + CHUNK] = part[MOST * k:MOST * (k + 1)].astype(BF16)
+    meta = first_lanes(split(terms) + split(terms0[:, 0:1]))
+    for k, out in enumerate(outs):
+        out[:, features:] = meta[MOST * k:MOST * (k + 1)].astype(BF16)
+
+
+def final_kernel(*refs):
+    shifted, routes, positions = refs[:3]
+    came, got, (out, prob_out, rows_at, back_at) = refs[3:7], refs[7:11], refs[11:]
+    p, z, _ = place()
+    features = out.shape[1]
+    label = labels(PAIRS, lambda k: (z + k) % E_FLY)
+    for k in range(E_FLY):
+        rows = came[(E_FLY - k) % E_FLY][MOST * k:MOST * (k + 1), :features]
+        rows_at[MOST * k:MOST * (k + 1), :] = rows.astype(F32)
+    take_rows(back_at, got)
+    select0 = came[0][:, features:]
+    keys = [keys_of(routes, positions, step) for step in range(STEPS)]
+    select1 = one_hot(keys[1], label).astype(BF16)
+    last = p == lax.axis_size("pipe") - 1
+    for at in range(0, features, CHUNK):
+        part = slice(at, at + CHUNK)
+        base = shifted[:, part].astype(F32)
+        base = jnp.where(last, 0.0, base)
+        base = base + lax.dot_general(
+            select0, rows_at[:, part].astype(BF16), TN, preferred_element_type=F32
+        )
+        base = base.astype(BF16).astype(F32)
+        base = base + lax.dot_general(
+            select1, back_at[:, part].astype(BF16), TN, preferred_element_type=F32
+        )
+        out[:, part] = base.astype(BF16)
+    meta = back_at[:, features:]
+    for step in range(STEPS):
+        first = 3 * (STEPS - 1 - step)
+        terms = meta[:, first:first + 1] + (meta[:, first + 1:first + 2] + meta[:, first + 2:first + 3])
+        for choice, hit in enumerate(hits(keys[step], label)):
+            prob_out[step, choice:choice + 1] = jnp.sum(
+                jnp.where(hit, terms, 0.0), axis=0, keepdims=True
+            )
+
+
+def local_chip(out_grad, routes, positions, route_probs, saved_acts, w_gate, w_up, w_down):
+    sections = lax.axis_size("pipe")
+    devices = lax.axis_size("expert")
+    grad = out_grad[0]
+    tokens, features = grad.shape
+    width = features + META
+    routes = routes[0].transpose(0, 2, 1)
+    positions = positions[0].transpose(0, 2, 1)
+    probs = route_probs[0].transpose(0, 2, 1)
+    acts = saved_acts[0]
+    hidden = 2 * acts.shape[-1]
+
+    def across(block):
+        return lax.ppermute(block, "expert", [(i, i ^ 1) for i in range(devices)])
+
+    def along(block, k):
+        if k % E_FLY == 0:
+            return block
+        return lax.ppermute(
+            block, "expert", [(i, (i + 2 * k) % devices) for i in range(devices)]
+        )
+
+    def relay(block, distance):
+        route = [(i, (i + distance) % sections) for i in range(sections)]
+        return lax.ppermute(block, "pipe", route)
+
+    pair = jax.ShapeDtypeStruct((MOST, width), BF16)
+    block = jax.ShapeDtypeStruct((PAIRS, width), BF16)
+    row_scratch = pltpu.VMEM((PAIRS, width), F32)
+
+    picked = call(
+        pick_kernel, "pick_rows", [pair] * E_FLY + [jax.ShapeDtypeStruct((4, tokens), F32)]
+    )(grad, routes, positions, probs)
+    got = [along(picked[k], k) for k in range(E_FLY)]
+    table = relay(picked[E_FLY], 1)
+    weights = []
+    for array in (w_down[0], w_gate[0], w_up[0]):
+        weights += [array, across(array)]
+    acts_other = across(acts)
+    shifted = relay(grad, -1)
+    *ahead, factors = call(
+        ahead_kernel,
+        "rows_ahead",
+        [pair] * E_FLY + [jax.ShapeDtypeStruct((STEPS, 3, PAIRS, hidden), F32)],
+        [pltpu.VMEM((PAIRS, hidden), F32)] * 2,
+    )(grad, routes, positions, table, acts, acts_other)
+    ahead = [along(ahead[k], k) for k in range(E_FLY)]
+    rows, ahead_rows, terms0 = call(
+        step_zero_kernel,
+        "step_zero",
+        [block, block, jax.ShapeDtypeStruct((PAIRS, META), F32)],
+        [row_scratch],
+    )(*got, *ahead, routes, positions, factors, *weights)
+    came = relay(rows, -1)
+    ahead_rows = relay(ahead_rows, -1)
+    came = [along(came, j) for j in range(E_FLY)]
+    back = call(step_one_kernel, "step_one", [pair] * E_FLY)(
+        *came, ahead_rows, factors, terms0, *weights
+    )
+    back = [along(back[k], E_FLY - k) for k in range(E_FLY)]
+    result, prob = call(
+        final_kernel,
+        "final_sums",
+        [
+            jax.ShapeDtypeStruct((tokens, features), BF16),
+            jax.ShapeDtypeStruct((STEPS, 2, tokens), F32),
+        ],
+        [pltpu.VMEM((PAIRS, features), F32), row_scratch],
+    )(shifted, routes, positions, *came, *back)
+    return result[None], prob.transpose(0, 2, 1)[None]
 
 
 def shifted(block, axis, distance):
@@ -52,7 +354,7 @@
     return (back_rows, prob_terms)
 
 
-def local(out_grad, routes, positions, route_probs, saved_acts, w_gate, w_up, w_down):
+def local_general(out_grad, routes, positions, route_probs, saved_acts, w_gate, w_up, w_down):
     devices = lax.axis_size("expert")
     members = devices // E_FLY
     pair_count = E_FLY * MOST
@@ -125,4 +427,6 @@
         P("pipe", "expert", None),
     )
     out_specs = (P("pipe", "expert", None), P("pipe", None, "expert", None))
+    one_chip = mesh.shape["expert"] == 2 * E_FLY
+    local = local_chip if one_chip else local_general
     return jax.shard_map(local, mesh=mesh, in_specs=in_specs, out_specs=out_specs, check_vma=False)

time: 119 us -> 86.7 us (0.73)
  blocking collectives: 35.9 us -> 0 us
  Pallas kernels: 0 us -> 7.65 us
  matrix products: 6.2 us -> 0 us
  waiting for transfers between devices: 51.1 us -> 54.2 us
  starting transfers between devices: 17.7 us -> 20 us
  other arithmetic: 2 us -> 0 us
    all_to_all x4 -> x0, blocking collectives: 35.9 us -> none  [the longest x2 15.9 us: local(): lax.all_to_all(out_rates, 'expert', split_axis=0, concat_axis=0, tiled=True)]
    ppermute x1 -> x20, waiting for transfers between devices: 23.7 us -> 54.2 us  [the longest x12 29.7 us: along(): lax.ppermute(block, 'expert', [(i, (i + 2 * k) % devices) for i in range(...]
    all_to_all x4 -> x0, waiting for transfers between devices: 27.3 us -> none  [the longest x2 13.2 us: local(): lax.all_to_all(out_rows, 'expert', split_axis=0, concat_axis=0, tiled=True)]
    ppermute x1 -> x20, starting transfers between devices: 1.29 us -> 20 us  [the longest x12 13.6 us: along(): lax.ppermute(block, 'expert', [(i, (i + 2 * k) % devices) for i in range(...]
    all_to_all x4 -> x0, starting transfers between devices: 16.4 us -> none  [the longest x2 9.69 us: local(): lax.all_to_all(out_rows, 'expert', split_axis=0, concat_axis=0, tiled=True)]
    pallas_call x0 -> x5, Pallas kernels: none -> 7.65 us  [the longest x1 2.73 us: local_chip(): call(step_one_kernel, 'step_one', [pair] * E_FLY)]
    dot_general x10 -> x0, matrix products: 6.2 us -> none  [the longest x2 1.87 us: assemble(): lax.dot_general(select, contrib, (((0,), (0,)), ((), ())), preferred_elem...]
    unnamed x16 -> x18, local copies, waits for them, and re-layouts: 0.05 us -> 3.83 us
  transfers between devices with their start and end apart: 5 -> 20, of which waited for: 5 -> 15; matrix products, arithmetic and copies ran while one was open for 1% -> 0% of each run, Pallas kernels for 0% -> 7%
where the time goes in v1:
time: 86.7 us; the launch traced here: 86.4 us
  waiting for transfers between devices  54.2 us (63%)
  starting transfers between devices  20 us (23%)
  Pallas kernels  7.65 us (9%)
  local copies, waits for them, and re-layouts  3.83 us (4%)
    ppermute x12, waiting for transfers between devices, along(): lax.ppermute(block, 'expert', [(i, (i + 2 * k) % devices) for i in range(...  29.7 us
    ppermute x4, waiting for transfers between devices, relay(): return lax.ppermute(block, 'pipe', route)  23.1 us
    ppermute x12, starting transfers between devices, along(): lax.ppermute(block, 'expert', [(i, (i + 2 * k) % devices) for i in range(...  13.6 us
    ppermute x4, starting transfers between devices, relay(): return lax.ppermute(block, 'pipe', route)  5.41 us
    unnamed x18, local copies, waits for them, and re-layouts  3.83 us
    pallas_call x1, Pallas kernels, local_chip(): call(step_one_kernel, 'step_one', [pair] * E_FLY)  2.73 us
    pallas_call x1, Pallas kernels, local_chip(): call(step_zero_kernel, 'step_zero', [block, block, jax.ShapeDtypeStruct((...  2.68 us
  transfers between devices with their start and end apart: 20, of which 15 were waited for; matrix products, arithmetic and copies ran while one was open for 0% of the time, Pallas kernels for 7%

profile of v1, /device:TPU:0, one launch (start us, length us, event | category | flops | bytes accessed | tf_op | source)
XLA Modules:
  0.0 86.4 jit_solution(11014256128466528341)
XLA Ops:
  0.6 0.5 collective-permute-start.10
  1.1 0.1 collective-permute-start.11
  1.2 0.4 collective-permute-start.9
  1.7 3.5 %collective-permute-start = (bf16[128,3840]{1,0:T(8,128)(2,1)}, bf16[128,3840]{1,0:T(8,128)(2,1)S(1)}, u32[]{:S(2)}, u32[]{:S(2)}) collective-permute-start(bf16[128,3840]{1,0:T(8,128)(2,1)} %bitcast.27), channel_id=1, source_target_pairs={{0,24},{8,0},{16,8},{24,16},{1,25},{9,1},{17,9},{25,17},{2,26},{10... | collective-permute-start | bytes 2949128 | tf_op jit(solution)/shard_map/ppermute | solution.py:265
  5.2 0.7 copy-done.6
  5.9 0.0 copy-done.5
  5.9 0.0 copy-done.8
  5.9 1.2 %copy-done.4 = bf16[1,128,3840]{2,1,0:T(8,128)(2,1)S(1)} copy-done((bf16[1,128,3840]{2,1,0:T(8,128)(2,1)S(1)}, bf16[1,128,3840]{2,1,0:T(8,128)(2,1)}, u32[]{:S(2)}) %copy-start.4) | copy-done | bytes 983064
  7.1 0.2 pick_rows.1
  7.3 0.1 collective-permute-start.4
  7.4 20.6 %collective-permute-done.4.table = f32[4,128]{1,0:T(4,128)S(1)} collective-permute-done((f32[4,128]{1,0:T(4,128)S(1)}, f32[4,128]{1,0:T(4,128)S(1)}, u32[]{:S(2)}, u32[]{:S(2)}) %collective-permute-start.4) | collective-permute-done | bytes 2080 | tf_op jit(solution)/shard_map/ppermute | solution.py:265
  28.1 1.6 %collective-permute-start.1 = (bf16[2,3968]{1,0:T(2,128)(2,1)S(1)}, bf16[2,3968]{1,0:T(2,128)(2,1)S(1)}, u32[]{:S(2)}, u32[]{:S(2)}) collective-permute-start(bf16[2,3968]{1,0:T(2,128)(2,1)S(1)} %get-tuple-element.22), channel_id=1, source_target_pairs={{0,2},{1,3},{2,4},{3,5},{4,6},{5,7},{6,0},{7,1},{8,10},{9,11},{10,... | collective-permute-start | bytes 47624 | tf_op jit(solution)/shard_map/ppermute | solution.py:259
  29.6 4.0 %collective-permute-done.1.refs_1_ = bf16[2,3968]{1,0:T(2,128)(2,1)S(1)} collective-permute-done((bf16[2,3968]{1,0:T(2,128)(2,1)S(1)}, bf16[2,3968]{1,0:T(2,128)(2,1)S(1)}, u32[]{:S(2)}, u32[]{:S(2)}) %collective-permute-start.1) | collective-permute-done | bytes 15904 | tf_op jit(solution)/shard_map/ppermute | solution.py:259
  33.6 0.8 collective-permute-start.2
  34.4 3.8 %collective-permute-done.2.refs_2_ = bf16[2,3968]{1,0:T(2,128)(2,1)S(1)} collective-permute-done((bf16[2,3968]{1,0:T(2,128)(2,1)S(1)}, bf16[2,3968]{1,0:T(2,128)(2,1)S(1)}, u32[]{:S(2)}, u32[]{:S(2)}) %collective-permute-start.2) | collective-permute-done | bytes 15904 | tf_op jit(solution)/shard_map/ppermute | solution.py:259
  38.2 1.4 %collective-permute-done.5.acts_other = bf16[2,16,2,128]{3,2,1,0:T(2,128)(2,1)S(1)} collective-permute-done((bf16[2,16,2,128]{3,2,1,0:T(2,128)(2,1)}, bf16[2,16,2,128]{3,2,1,0:T(2,128)(2,1)S(1)}, u32[]{:S(2)}, u32[]{:S(2)}) %collective-permute-start.5) | collective-permute-done | bytes 16416 | tf_op jit(solution)/shard_map/ppermute | solution.py:254
  39.6 1.9 %collective-permute-start.3 = (bf16[2,3968]{1,0:T(2,128)(2,1)S(1)}, bf16[2,3968]{1,0:T(2,128)(2,1)S(1)}, u32[]{:S(2)}, u32[]{:S(2)}) collective-permute-start(bf16[2,3968]{1,0:T(2,128)(2,1)S(1)} %get-tuple-element.24), channel_id=1, source_target_pairs={{0,6},{1,7},{2,0},{3,1},{4,2},{5,3},{6,4},{7,5},{8,14},{9,15},{10,... | collective-permute-start | bytes 47624 | tf_op jit(solution)/shard_map/ppermute | solution.py:259
  41.5 0.7 copy-done.7
  42.2 0.3 rows_ahead.1
  42.5 0.8 collective-permute-done.3.refs_3_
  43.3 0.0 collective-permute-start.6
  43.3 5.5 %collective-permute-done.6.refs_5_ = bf16[2,3968]{1,0:T(2,128)(2,1)S(1)} collective-permute-done((bf16[2,3968]{1,0:T(2,128)(2,1)S(1)}, bf16[2,3968]{1,0:T(2,128)(2,1)S(1)}, u32[]{:S(2)}, u32[]{:S(2)}) %collective-permute-start.6) | collective-permute-done | bytes 15904 | tf_op jit(solution)/shard_map/ppermute | solution.py:259
  48.9 0.1 collective-permute-start.7
  49.0 4.5 %collective-permute-done.7.refs_6_ = bf16[2,3968]{1,0:T(2,128)(2,1)S(1)} collective-permute-done((bf16[2,3968]{1,0:T(2,128)(2,1)S(1)}, bf16[2,3968]{1,0:T(2,128)(2,1)S(1)}, u32[]{:S(2)}, u32[]{:S(2)}) %collective-permute-start.7) | collective-permute-done | bytes 15904 | tf_op jit(solution)/shard_map/ppermute | solution.py:259
  53.5 1.9 %collective-permute-start.8 = (bf16[2,3968]{1,0:T(2,128)(2,1)S(1)}, bf16[2,3968]{1,0:T(2,128)(2,1)S(1)}, u32[]{:S(2)}, u32[]{:S(2)}) collective-permute-start(bf16[2,3968]{1,0:T(2,128)(2,1)S(1)} %get-tuple-element.29), channel_id=1, source_target_pairs={{0,6},{1,7},{2,0},{3,1},{4,2},{5,3},{6,4},{7,5},{8,14},{9,15},{10,... | collective-permute-start | bytes 47624 | tf_op jit(solution)/shard_map/ppermute | solution.py:259
  55.4 1.9 %collective-permute-done.8.refs_7_ = bf16[2,3968]{1,0:T(2,128)(2,1)S(1)} collective-permute-done((bf16[2,3968]{1,0:T(2,128)(2,1)S(1)}, bf16[2,3968]{1,0:T(2,128)(2,1)S(1)}, u32[]{:S(2)}, u32[]{:S(2)}) %collective-permute-start.8) | collective-permute-done | bytes 15904 | tf_op jit(solution)/shard_map/ppermute | solution.py:259
  57.2 0.0 collective-permute-done.10.refs_14_.refs_10_
  57.2 0.0 collective-permute-done.11.refs_16_.refs_12_
  57.3 0.0 collective-permute-done.9.refs_12_.refs_8_
  57.3 0.0 copy-start.2
  57.3 1.2 %copy-done.2 = bf16[1,3840,128]{2,1,0:T(8,128)(2,1)S(1)} copy-done((bf16[1,3840,128]{2,1,0:T(8,128)(2,1)S(1)}, bf16[1,3840,128]{2,1,0:T(8,128)(2,1)}, u32[]{:S(2)}) %copy-start.2) | copy-done | bytes 983064
  58.5 2.7 %step_zero.1 = (bf16[8,3968]{1,0:T(8,128)(2,1)S(1)}, bf16[8,3968]{1,0:T(8,128)(2,1)S(1)}, f32[8,128]{1,0:T(8,128)S(1)}) custom-call(bf16[2,3968]{1,0:T(2,128)(2,1)S(1)} %get-tuple-element.21.refs_0_, bf16[2,3968]{1,0:T(2,128)(2,1)S(1)} %collective-permute-done.1.refs_1_, bf16[2,3968]{1,0:T(2,128)(2,1)S(1)} %collective-permute-done.2.refs_2_, ...), custom_call_target="tpu_custom_call" | custom-call | tf_op jit(solution)/shard_map/step_zero/pallas_call | solution.py:288
  61.2 1.5 %collective-permute-start.12 = (bf16[8,3968]{1,0:T(8,128)(2,1)S(1)}, bf16[8,3968]{1,0:T(8,128)(2,1)S(1)}, u32[]{:S(2)}, u32[]{:S(2)}) collective-permute-start(bf16[8,3968]{1,0:T(8,128)(2,1)S(1)} %get-tuple-element.31), channel_id=1, source_target_pairs={{0,24},{8,0},{16,8},{24,16},{1,25},{9,1},{17,9},{25,17},{2,26},{10... | collective-permute-start | bytes 190472 | tf_op jit(solution)/shard_map/ppermute | solution.py:265
  62.6 0.4 collective-permute-start.16
  63.0 2.4 %collective-permute-done.12.refs_0_.refs_3_ = bf16[8,3968]{1,0:T(8,128)(2,1)S(1)} collective-permute-done((bf16[8,3968]{1,0:T(8,128)(2,1)S(1)}, bf16[8,3968]{1,0:T(8,128)(2,1)S(1)}, u32[]{:S(2)}, u32[]{:S(2)}) %collective-permute-start.12) | collective-permute-done | bytes 63520 | tf_op jit(solution)/shard_map/ppermute | solution.py:265
  65.4 0.0 collective-permute-start.13
  65.4 4.2 %collective-permute-start.14 = (bf16[8,3968]{1,0:T(8,128)(2,1)S(1)}, bf16[8,3968]{1,0:T(8,128)(2,1)S(1)}, u32[]{:S(2)}, u32[]{:S(2)}) collective-permute-start(bf16[8,3968]{1,0:T(8,128)(2,1)S(1)} %collective-permute-done.12.refs_0_.refs_3_), channel_id=1, source_target_pairs={{0,4},{1,5},{2,6},{3,7},{4,0},{5,1},{6,2},{7,3},{8,12},{9,13},{10,... | collective-permute-start | bytes 190472 | tf_op jit(solution)/shard_map/ppermute | solution.py:259
  69.7 0.0 collective-permute-start.15
  69.7 1.8 %collective-permute-done.13.refs_1_.refs_4_ = bf16[8,3968]{1,0:T(8,128)(2,1)S(1)} collective-permute-done((bf16[8,3968]{1,0:T(8,128)(2,1)S(1)}, bf16[8,3968]{1,0:T(8,128)(2,1)S(1)}, u32[]{:S(2)}, u32[]{:S(2)}) %collective-permute-start.13) | collective-permute-done | bytes 63520 | tf_op jit(solution)/shard_map/ppermute | solution.py:259
  71.5 1.5 %collective-permute-done.14.refs_2_.refs_5_ = bf16[8,3968]{1,0:T(8,128)(2,1)S(1)} collective-permute-done((bf16[8,3968]{1,0:T(8,128)(2,1)S(1)}, bf16[8,3968]{1,0:T(8,128)(2,1)S(1)}, u32[]{:S(2)}, u32[]{:S(2)}) %collective-permute-start.14) | collective-permute-done | bytes 63520 | tf_op jit(solution)/shard_map/ppermute | solution.py:259
  73.0 0.9 %collective-permute-done.15.refs_3_.refs_6_ = bf16[8,3968]{1,0:T(8,128)(2,1)S(1)} collective-permute-done((bf16[8,3968]{1,0:T(8,128)(2,1)S(1)}, bf16[8,3968]{1,0:T(8,128)(2,1)S(1)}, u32[]{:S(2)}, u32[]{:S(2)}) %collective-permute-start.15) | collective-permute-done | bytes 63520 | tf_op jit(solution)/shard_map/ppermute | solution.py:259
  73.9 2.7 %step_one.1 = (bf16[2,3968]{1,0:T(2,128)(2,1)S(1)}, bf16[2,3968]{1,0:T(2,128)(2,1)S(1)}, bf16[2,3968]{1,0:T(2,128)(2,1)S(1)}, bf16[2,3968]{1,0:T(2,128)(2,1)S(1)}) custom-call(bf16[8,3968]{1,0:T(8,128)(2,1)S(1)} %collective-permute-done.12.refs_0_.refs_3_, bf16[8,3968]{1,0:T(8,128)(2,1)S(1)} %collective-permute-done.13.refs_1_.refs_4_, ...), custom_call_target="tpu_custom_call" | custom-call | tf_op jit(solution)/shard_map/step_one/pallas_call | solution.py:297
  76.6 2.6 %collective-permute-start.17 = (bf16[2,3968]{1,0:T(2,128)(2,1)S(1)}, bf16[2,3968]{1,0:T(2,128)(2,1)S(1)}, u32[]{:S(2)}, u32[]{:S(2)}) collective-permute-start(bf16[2,3968]{1,0:T(2,128)(2,1)S(1)} %get-tuple-element.35), channel_id=1, source_target_pairs={{0,6},{1,7},{2,0},{3,1},{4,2},{5,3},{6,4},{7,5},{8,14},{9,15},{10,... | collective-permute-start | bytes 47624 | tf_op jit(solution)/shard_map/ppermute | solution.py:259
  79.2 0.6 collective-permute-start.19
  79.8 0.9 collective-permute-done.17.refs_8_
  80.6 3.2 %collective-permute-done.18.refs_9_ = bf16[2,3968]{1,0:T(2,128)(2,1)S(1)} collective-permute-done((bf16[2,3968]{1,0:T(2,128)(2,1)S(1)}, bf16[2,3968]{1,0:T(2,128)(2,1)S(1)}, u32[]{:S(2)}, u32[]{:S(2)}) %collective-permute-start.18) | collective-permute-done | bytes 15904 | tf_op jit(solution)/shard_map/ppermute | solution.py:259
  83.8 0.9 %collective-permute-done.19.refs_10_ = bf16[2,3968]{1,0:T(2,128)(2,1)S(1)} collective-permute-done((bf16[2,3968]{1,0:T(2,128)(2,1)S(1)}, bf16[2,3968]{1,0:T(2,128)(2,1)S(1)}, u32[]{:S(2)}, u32[]{:S(2)}) %collective-permute-start.19) | collective-permute-done | bytes 15904 | tf_op jit(solution)/shard_map/ppermute | solution.py:259
  84.7 1.7 %final_sums.1 = (bf16[128,3840]{1,0:T(8,128)(2,1)}, f32[2,2,128]{2,1,0:T(2,128)}) custom-call(bf16[128,3840]{1,0:T(8,128)(2,1)S(1)} %collective-permute-done.refs_0_, s32[2,2,128]{2,1,0:T(2,128)S(1)} %bitcast.33, s32[2,2,128]{2,1,0:T(2,128)S(1)} %bitcast.37, bf16[8,3968]{1,0:T(8,128)(2,1)S(1)} %collective-permute-done.12.refs_0_.refs_3_, ...), custom_call_target="tpu_custom_call" | custom-call | tf_op jit(solution)/shard_map/final_sums/pallas_call | solution.py:301
  (15 shorter events, 0.0 us)
Async XLA Ops:
  0.6 56.6 %collective-permute-start.10 = (bf16[3840,128]{1,0:T(8,128)(2,1)}, bf16[3840,128]{1,0:T(8,128)(2,1)S(1)}, u32[]{:S(2)}, u32[]{:S(2)}) collective-permute-start(bf16[3840,128]{1,0:T(8,128)(2,1)} %bitcast.21), channel_id=1, source_target_pairs={{0,1},{1,0},{2,3},{3,2},{4,5},{5,4},{6,7},{7,6},{8,9},{9,8},{10,11... | collective-permute-start | bytes 2949128 | tf_op jit(solution)/shard_map/ppermute | solution.py:254
  1.1 56.1 %collective-permute-start.11 = (bf16[3840,128]{1,0:T(8,128)(2,1)}, bf16[3840,128]{1,0:T(8,128)(2,1)S(1)}, u32[]{:S(2)}, u32[]{:S(2)}) collective-permute-start(bf16[3840,128]{1,0:T(8,128)(2,1)} %bitcast.24), channel_id=1, source_target_pairs={{0,1},{1,0},{2,3},{3,2},{4,5},{5,4},{6,7},{7,6},{8,9},{9,8},{10,11... | collective-permute-start | bytes 2949128 | tf_op jit(solution)/shard_map/ppermute | solution.py:254
  1.2 56.0 %collective-permute-start.9 = (bf16[128,3840]{1,0:T(8,128)(2,1)}, bf16[128,3840]{1,0:T(8,128)(2,1)S(1)}, u32[]{:S(2)}, u32[]{:S(2)}) collective-permute-start(bf16[128,3840]{1,0:T(8,128)(2,1)} %bitcast.18), channel_id=1, source_target_pairs={{0,1},{1,0},{2,3},{3,2},{4,5},{5,4},{6,7},{7,6},{8,9},{9,8},{10,11... | collective-permute-start | bytes 2949128 | tf_op jit(solution)/shard_map/ppermute | solution.py:254
  1.7 78.1 %collective-permute-start = (bf16[128,3840]{1,0:T(8,128)(2,1)}, bf16[128,3840]{1,0:T(8,128)(2,1)S(1)}, u32[]{:S(2)}, u32[]{:S(2)}) collective-permute-start(bf16[128,3840]{1,0:T(8,128)(2,1)} %bitcast.27), channel_id=1, source_target_pairs={{0,24},{8,0},{16,8},{24,16},{1,25},{9,1},{17,9},{25,17},{2,26},{10... | collective-permute-start | bytes 2949128 | tf_op jit(solution)/shard_map/ppermute | solution.py:265
  5.2 0.7 copy-start.6
  5.2 0.7 copy-start.5
  5.2 0.7 copy-start.8
  5.9 1.2 %copy-start.4 = (bf16[1,128,3840]{2,1,0:T(8,128)(2,1)S(1)}, bf16[1,128,3840]{2,1,0:T(8,128)(2,1)}, u32[]{:S(2)}) copy-start(bf16[1,128,3840]{2,1,0:T(8,128)(2,1)} %param.8) | copy-start | bytes 2949124
  7.1 50.2 %copy-start = (bf16[1,128,3840]{2,1,0:T(8,128)(2,1)S(1)}, bf16[1,128,3840]{2,1,0:T(8,128)(2,1)}, u32[]{:S(2)}) copy-start(bf16[1,128,3840]{2,1,0:T(8,128)(2,1)} %param.15) | copy-start | bytes 2949124
  7.1 50.2 %copy-start.1 = (bf16[1,3840,128]{2,1,0:T(8,128)(2,1)S(1)}, bf16[1,3840,128]{2,1,0:T(8,128)(2,1)}, u32[]{:S(2)}) copy-start(bf16[1,3840,128]{2,1,0:T(8,128)(2,1)} %param.13) | copy-start | bytes 2949124
  7.3 20.7 %collective-permute-start.4 = (f32[4,128]{1,0:T(4,128)S(1)}, f32[4,128]{1,0:T(4,128)S(1)}, u32[]{:S(2)}, u32[]{:S(2)}) collective-permute-start(f32[4,128]{1,0:T(4,128)S(1)} %get-tuple-element.25), channel_id=1, source_target_pairs={{0,8},{8,16},{16,24},{24,0},{1,9},{9,17},{17,25},{25,1},{2,10},{10... | collective-permute-start | bytes 6152 | tf_op jit(solution)/shard_map/ppermute | solution.py:265
  28.1 5.5 %collective-permute-start.1 = (bf16[2,3968]{1,0:T(2,128)(2,1)S(1)}, bf16[2,3968]{1,0:T(2,128)(2,1)S(1)}, u32[]{:S(2)}, u32[]{:S(2)}) collective-permute-start(bf16[2,3968]{1,0:T(2,128)(2,1)S(1)} %get-tuple-element.22), channel_id=1, source_target_pairs={{0,2},{1,3},{2,4},{3,5},{4,6},{5,7},{6,0},{7,1},{8,10},{9,11},{10,... | collective-permute-start | bytes 47624 | tf_op jit(solution)/shard_map/ppermute | solution.py:259
  33.6 4.6 %collective-permute-start.2 = (bf16[2,3968]{1,0:T(2,128)(2,1)S(1)}, bf16[2,3968]{1,0:T(2,128)(2,1)S(1)}, u32[]{:S(2)}, u32[]{:S(2)}) collective-permute-start(bf16[2,3968]{1,0:T(2,128)(2,1)S(1)} %get-tuple-element.23), channel_id=1, source_target_pairs={{0,4},{1,5},{2,6},{3,7},{4,0},{5,1},{6,2},{7,3},{8,12},{9,13},{10,... | collective-permute-start | bytes 47624 | tf_op jit(solution)/shard_map/ppermute | solution.py:259
  38.2 1.4 %collective-permute-start.5 = (bf16[2,16,2,128]{3,2,1,0:T(2,128)(2,1)}, bf16[2,16,2,128]{3,2,1,0:T(2,128)(2,1)S(1)}, u32[]{:S(2)}, u32[]{:S(2)}) collective-permute-start(bf16[2,16,2,128]{3,2,1,0:T(2,128)(2,1)} %bitcast.38), channel_id=1, source_target_pairs={{0,1},{1,0},{2,3},{3,2},{4,5},{5,4},{6,7},{7,6},{8,9},{9,8},{10,11... | collective-permute-start | bytes 49160 | tf_op jit(solution)/shard_map/ppermute | solution.py:254
  39.6 3.7 %collective-permute-start.3 = (bf16[2,3968]{1,0:T(2,128)(2,1)S(1)}, bf16[2,3968]{1,0:T(2,128)(2,1)S(1)}, u32[]{:S(2)}, u32[]{:S(2)}) collective-permute-start(bf16[2,3968]{1,0:T(2,128)(2,1)S(1)} %get-tuple-element.24), channel_id=1, source_target_pairs={{0,6},{1,7},{2,0},{3,1},{4,2},{5,3},{6,4},{7,5},{8,14},{9,15},{10,... | collective-permute-start | bytes 47624 | tf_op jit(solution)/shard_map/ppermute | solution.py:259
  41.5 0.7 copy-start.7
  43.3 5.5 %collective-permute-start.6 = (bf16[2,3968]{1,0:T(2,128)(2,1)S(1)}, bf16[2,3968]{1,0:T(2,128)(2,1)S(1)}, u32[]{:S(2)}, u32[]{:S(2)}) collective-permute-start(bf16[2,3968]{1,0:T(2,128)(2,1)S(1)} %get-tuple-element.27), channel_id=1, source_target_pairs={{0,2},{1,3},{2,4},{3,5},{4,6},{5,7},{6,0},{7,1},{8,10},{9,11},{10,... | collective-permute-start | bytes 47624 | tf_op jit(solution)/shard_map/ppermute | solution.py:259
  48.9 4.6 %collective-permute-start.7 = (bf16[2,3968]{1,0:T(2,128)(2,1)S(1)}, bf16[2,3968]{1,0:T(2,128)(2,1)S(1)}, u32[]{:S(2)}, u32[]{:S(2)}) collective-permute-start(bf16[2,3968]{1,0:T(2,128)(2,1)S(1)} %get-tuple-element.28), channel_id=1, source_target_pairs={{0,4},{1,5},{2,6},{3,7},{4,0},{5,1},{6,2},{7,3},{8,12},{9,13},{10,... | collective-permute-start | bytes 47624 | tf_op jit(solution)/shard_map/ppermute | solution.py:259
  53.5 3.7 %collective-permute-start.8 = (bf16[2,3968]{1,0:T(2,128)(2,1)S(1)}, bf16[2,3968]{1,0:T(2,128)(2,1)S(1)}, u32[]{:S(2)}, u32[]{:S(2)}) collective-permute-start(bf16[2,3968]{1,0:T(2,128)(2,1)S(1)} %get-tuple-element.29), channel_id=1, source_target_pairs={{0,6},{1,7},{2,0},{3,1},{4,2},{5,3},{6,4},{7,5},{8,14},{9,15},{10,... | collective-permute-start | bytes 47624 | tf_op jit(solution)/shard_map/ppermute | solution.py:259
  57.3 1.2 %copy-start.2 = (bf16[1,3840,128]{2,1,0:T(8,128)(2,1)S(1)}, bf16[1,3840,128]{2,1,0:T(8,128)(2,1)}, u32[]{:S(2)}) copy-start(bf16[1,3840,128]{2,1,0:T(8,128)(2,1)} %param.14) | copy-start | bytes 2949124
  58.5 15.4 %copy-start.3 = (bf16[1,3840,128]{2,1,0:T(8,128)(2,1)S(1)}, bf16[1,3840,128]{2,1,0:T(8,128)(2,1)}, u32[]{:S(2)}) copy-start(bf16[1,3840,128]{2,1,0:T(8,128)(2,1)} %param.14) | copy-start | bytes 2949124
  61.2 4.3 %collective-permute-start.12 = (bf16[8,3968]{1,0:T(8,128)(2,1)S(1)}, bf16[8,3968]{1,0:T(8,128)(2,1)S(1)}, u32[]{:S(2)}, u32[]{:S(2)}) collective-permute-start(bf16[8,3968]{1,0:T(8,128)(2,1)S(1)} %get-tuple-element.31), channel_id=1, source_target_pairs={{0,24},{8,0},{16,8},{24,16},{1,25},{9,1},{17,9},{25,17},{2,26},{10... | collective-permute-start | bytes 190472 | tf_op jit(solution)/shard_map/ppermute | solution.py:265
  62.6 7.0 %collective-permute-start.16 = (bf16[8,3968]{1,0:T(8,128)(2,1)S(1)}, bf16[8,3968]{1,0:T(8,128)(2,1)S(1)}, u32[]{:S(2)}, u32[]{:S(2)}) collective-permute-start(bf16[8,3968]{1,0:T(8,128)(2,1)S(1)} %get-tuple-element.32), channel_id=1, source_target_pairs={{0,24},{8,0},{16,8},{24,16},{1,25},{9,1},{17,9},{25,17},{2,26},{10... | collective-permute-start | bytes 190472 | tf_op jit(solution)/shard_map/ppermute | solution.py:265
  65.4 6.1 %collective-permute-start.13 = (bf16[8,3968]{1,0:T(8,128)(2,1)S(1)}, bf16[8,3968]{1,0:T(8,128)(2,1)S(1)}, u32[]{:S(2)}, u32[]{:S(2)}) collective-permute-start(bf16[8,3968]{1,0:T(8,128)(2,1)S(1)} %collective-permute-done.12.refs_0_.refs_3_), channel_id=1, source_target_pairs={{0,2},{1,3},{2,4},{3,5},{4,6},{5,7},{6,0},{7,1},{8,10},{9,11},{10,... | collective-permute-start | bytes 190472 | tf_op jit(solution)/shard_map/ppermute | solution.py:259
  65.4 7.6 %collective-permute-start.14 = (bf16[8,3968]{1,0:T(8,128)(2,1)S(1)}, bf16[8,3968]{1,0:T(8,128)(2,1)S(1)}, u32[]{:S(2)}, u32[]{:S(2)}) collective-permute-start(bf16[8,3968]{1,0:T(8,128)(2,1)S(1)} %collective-permute-done.12.refs_0_.refs_3_), channel_id=1, source_target_pairs={{0,4},{1,5},{2,6},{3,7},{4,0},{5,1},{6,2},{7,3},{8,12},{9,13},{10,... | collective-permute-start | bytes 190472 | tf_op jit(solution)/shard_map/ppermute | solution.py:259
  69.7 4.2 %collective-permute-start.15 = (bf16[8,3968]{1,0:T(8,128)(2,1)S(1)}, bf16[8,3968]{1,0:T(8,128)(2,1)S(1)}, u32[]{:S(2)}, u32[]{:S(2)}) collective-permute-start(bf16[8,3968]{1,0:T(8,128)(2,1)S(1)} %collective-permute-done.12.refs_0_.refs_3_), channel_id=1, source_target_pairs={{0,6},{1,7},{2,0},{3,1},{4,2},{5,3},{6,4},{7,5},{8,14},{9,15},{10,... | collective-permute-start | bytes 190472 | tf_op jit(solution)/shard_map/ppermute | solution.py:259
  76.6 4.0 %collective-permute-start.17 = (bf16[2,3968]{1,0:T(2,128)(2,1)S(1)}, bf16[2,3968]{1,0:T(2,128)(2,1)S(1)}, u32[]{:S(2)}, u32[]{:S(2)}) collective-permute-start(bf16[2,3968]{1,0:T(2,128)(2,1)S(1)} %get-tuple-element.35), channel_id=1, source_target_pairs={{0,6},{1,7},{2,0},{3,1},{4,2},{5,3},{6,4},{7,5},{8,14},{9,15},{10,... | collective-permute-start | bytes 47624 | tf_op jit(solution)/shard_map/ppermute | solution.py:259
  79.2 4.6 %collective-permute-start.18 = (bf16[2,3968]{1,0:T(2,128)(2,1)S(1)}, bf16[2,3968]{1,0:T(2,128)(2,1)S(1)}, u32[]{:S(2)}, u32[]{:S(2)}) collective-permute-start(bf16[2,3968]{1,0:T(2,128)(2,1)S(1)} %get-tuple-element.36), channel_id=1, source_target_pairs={{0,4},{1,5},{2,6},{3,7},{4,0},{5,1},{6,2},{7,3},{8,12},{9,13},{10,... | collective-permute-start | bytes 47624 | tf_op jit(solution)/shard_map/ppermute | solution.py:259
  79.2 5.5 %collective-permute-start.19 = (bf16[2,3968]{1,0:T(2,128)(2,1)S(1)}, bf16[2,3968]{1,0:T(2,128)(2,1)S(1)}, u32[]{:S(2)}, u32[]{:S(2)}) collective-permute-start(bf16[2,3968]{1,0:T(2,128)(2,1)S(1)} %get-tuple-element.37), channel_id=1, source_target_pairs={{0,2},{1,3},{2,4},{3,5},{4,6},{5,7},{6,0},{7,1},{8,10},{9,11},{10,... | collective-permute-start | bytes 47624 | tf_op jit(solution)/shard_map/ppermute | solution.py:259

commit v2 on v1

--- a/solution.py
+++ b/solution.py
@@ -13,19 +13,28 @@
 PAIRS = E_FLY * MOST
 META = 128
 CHUNK = 256
+COST0 = 20_000_000_000
+COST1 = 0
+COST2 = 20_000_000_000
+COST3 = 20_000_000_000
+LIMIT = 50
 F32 = jnp.float32
 BF16 = jnp.bfloat16
 NT = (((1,), (1,)), ((), ()))
 TN = (((0,), (0,)), ((), ()))
 
 
-def call(kernel, name, out_shape, scratch=()):
+def call(kernel, name, out_shape, scratch=(), hbm=0, operands=0, limit=24, cost=0):
+    specs = [pl.BlockSpec(memory_space=pl.ANY)] * hbm
+    specs += [pl.BlockSpec(memory_space=pltpu.VMEM)] * (operands - hbm)
     return pl.pallas_call(
         kernel,
         name=name,
         out_shape=out_shape,
+        in_specs=specs,
         scratch_shapes=list(scratch),
-        compiler_params=pltpu.CompilerParams(vmem_limit_bytes=24 * 2**20),
+        cost_estimate=pl.CostEstimate(flops=cost, bytes_accessed=0, transcendentals=0),
+        compiler_params=pltpu.CompilerParams(vmem_limit_bytes=limit * 2**20),
     )
 
 
@@ -76,6 +85,11 @@
 def take_rows(scratch, refs):
     for k, ref in enumerate(refs):
         scratch[MOST * k:MOST * (k + 1), :] = ref[...].astype(F32)
+
+
+def table_kernel(routes, positions, probs, table):
+    table[0:2] = keys_of(routes, positions, 1).astype(F32)
+    table[2:4] = probs[1].astype(F32)
 
 
 def pick_kernel(grad, routes, positions, probs, *outs):
@@ -85,14 +99,10 @@
     select = one_hot(keys, label)
     rows = jnp.dot(select.astype(BF16), grad[...], preferred_element_type=F32)
     rate = rates_of(keys, probs[0].astype(F32), label)
-    put_rows(outs[:E_FLY], rows, first_lanes([rate]))
-    table = outs[E_FLY]
-    table[0:2] = keys_of(routes, positions, 1).astype(F32)
-    table[2:4] = probs[1].astype(F32)
-
-
-def ahead_kernel(grad, routes, positions, table, acts, acts_other, *refs):
-    outs, factors, gate_at, up_at = refs[:E_FLY], *refs[E_FLY:]
+    put_rows(outs, rows, first_lanes([rate]))
+
+
+def rows_ahead(grad, routes, positions, table, rows_out):
     p, z, c = place()
     keys0 = keys_of(routes, positions, 0)
     keys1 = table[0:2].astype(jnp.int32)
@@ -114,23 +124,54 @@
             select.astype(BF16), step0.astype(BF16), NT, preferred_element_type=F32
         )
         meta = meta + jnp.where(row // MOST == k, match, 0.0)
-    put_rows(outs, rows, meta)
-    for step in range(STEPS):
-        for k in range(E_FLY):
-            first = (2 * ((z + E_FLY - k) % E_FLY) + c) * MOST
-            for spot_at in range(MOST):
-                at = MOST * k + spot_at
-                for half, ref in enumerate((acts, acts_other)):
-                    pair = ref[step, first + spot_at].astype(F32)
-                    width = pair.shape[1]
-                    gate_at[at:at + 1, half * width:(half + 1) * width] = pair[0:1]
-                    up_at[at:at + 1, half * width:(half + 1) * width] = pair[1:2]
-        gate, up = gate_at[...], up_at[...]
+    features = rows.shape[1]
+    rows_out[PAIRS:, :features] = rows.astype(BF16)
+    rows_out[PAIRS:, features:] = meta.astype(BF16)
+    taken = one_hot(jnp.where(p == 0, -1, keys0), label)
+    rows_out[:PAIRS, features:] = taken.astype(BF16)
+
+
+def act_factors(acts, acts_other, factors, rows_at):
+    _, z, c = place()
+    steps, slots, _, width = acts.shape
+    for half, ref in enumerate((acts, acts_other)):
+        for at in range(steps * slots):
+            rows_at[2 * at:2 * at + 2, half * width:(half + 1) * width] = ref[
+                at // slots, at % slots
+            ].astype(F32)
+    stored = rows_at[...].astype(BF16)
+    row = lax.broadcasted_iota(jnp.int32, (2 * steps * PAIRS, 2 * steps * slots), 0)
+    column = lax.broadcasted_iota(jnp.int32, row.shape, 1)
+    group, k, spot = row // PAIRS, row // MOST % E_FLY, row % MOST
+    slot = (2 * ((z + E_FLY - k) % E_FLY) + c) * MOST + spot
+    wanted = 2 * (group // 2 * slots + slot) + group % 2
+    pick = jnp.where(column == wanted, 1.0, 0.0).astype(BF16)
+    picked = jnp.dot(pick, stored, preferred_element_type=F32)
+    for step in range(steps):
+        gate = picked[2 * step * PAIRS:(2 * step + 1) * PAIRS]
+        up = picked[(2 * step + 1) * PAIRS:(2 * step + 2) * PAIRS]
         sigmoid = 1.0 / (1.0 + jnp.exp(-gate))
         active = gate * sigmoid
         factors[step, 0] = up * sigmoid * (1.0 + gate * (1.0 - sigmoid))
         factors[step, 1] = active
         factors[step, 2] = active * up
+
+
+def prepare_kernel(*refs):
+    grad, *weights = refs[:4]
+    (routes, positions, table, acts, acts_other), (rows_out, factors) = refs[4:9], refs[9:11]
+    held, (grad_at, rows_at, sems) = refs[11:14], refs[14:]
+    copies = [
+        pltpu.make_async_copy(source, target, sems.at[index])
+        for index, (source, target) in enumerate(zip((grad, *weights), (grad_at, *held)))
+    ]
+    for copy in copies:
+        copy.start()
+    act_factors(acts, acts_other, factors, rows_at)
+    copies[0].wait()
+    rows_ahead(grad_at, routes, positions, table, rows_out)
+    for copy in copies[1:]:
+        copy.wait()
 
 
 def expert_rows(rows, rate, factors, step, weights):
@@ -142,37 +183,42 @@
         both = jnp.concatenate([down[:, part], down_other[:, part]], axis=0)
         v = v + lax.dot_general(rows[:, part], both, NT, preferred_element_type=F32)
     scaled = rate * v
-    grad_gate = (scaled * factors[step, 0]).astype(BF16)
-    grad_up = (scaled * factors[step, 1]).astype(BF16)
+    grads = jnp.concatenate(
+        [(scaled * factors[step, 0]).astype(BF16), (scaled * factors[step, 1]).astype(BF16)],
+        axis=1,
+    )
     terms = jnp.sum(factors[step, 2] * v, axis=1, keepdims=True)
-    grads = jnp.concatenate([grad_gate, grad_up], axis=1)
-
-    def back(part):
+
+    def back(at):
+        part = slice(at, at + CHUNK)
         wide = jnp.concatenate(
             [gate[part], gate_other[part], up[part], up_other[part]], axis=1
         )
-        return lax.dot_general(grads, wide, NT, preferred_element_type=F32)
-
-    return back, terms
+        return part, lax.dot_general(grads, wide, NT, preferred_element_type=F32)
+
+    return [functools.partial(back, at) for at in range(0, features, CHUNK)], terms
 
 
 def step_zero_kernel(*refs):
-    got, ahead, (routes, positions, factors) = refs[:4], refs[4:8], refs[8:11]
-    weights, (rows_out, ahead_out, terms_out, rows_at) = refs[11:17], refs[17:]
-    p, z, _ = place()
+    got, (factors, ahead), weights = refs[:4], refs[4:6], refs[6:12]
+    rows_out, terms_out, rows_at = refs[12:]
     take_rows(rows_at, got)
     features = rows_at.shape[1] - META
     rate = rows_at[:, features:features + 1]
-    back, terms = expert_rows(rows_at[:, :features].astype(BF16), rate, factors, 0, weights)
+    backs, terms = expert_rows(rows_at[:, :features].astype(BF16), rate, factors, 0, weights)
     terms_out[...] = jnp.broadcast_to(terms, terms_out.shape)
-    for at in range(0, features, CHUNK):
-        rows_out[:, at:at + CHUNK] = back(slice(at, at + CHUNK)).astype(BF16)
-    keys = keys_of(routes, positions, 0)
-    keys = jnp.where(p == 0, -1, keys)
-    select = one_hot(keys, labels(PAIRS, lambda k: (z + k) % E_FLY))
-    rows_out[:, features:] = select.astype(BF16)
-    take_rows(rows_at, ahead)
-    ahead_out[...] = rows_at[...].astype(BF16)
+    for back in backs:
+        part, value = back()
+        rows_out[:PAIRS, part] = value.astype(BF16)
+    rows_out[:PAIRS, features:] = ahead[:PAIRS, features:]
+    rows_out[PAIRS:] = ahead[PAIRS:]
+
+
+def merge_kernel(came, *outs):
+    for k, out in enumerate(outs):
+        first = PAIRS + MOST * (k + 1)
+        out[:PAIRS] = came[:PAIRS]
+        out[PAIRS:] = came[first:first + MOST]
 
 
 def split(value):
@@ -182,21 +228,21 @@
 
 
 def step_one_kernel(*refs):
-    came, (ahead, factors, terms0) = refs[:4], refs[4:7]
-    weights, outs = refs[7:13], refs[13:17]
-    features = ahead.shape[1] - META
-    meta = ahead[:, features:]
-    rate = meta[:, E_FLY * PAIRS:E_FLY * PAIRS + 1].astype(F32)
-    match = meta[:, :E_FLY * PAIRS]
-    everything = jnp.concatenate([ref[:, :features] for ref in came], axis=0)
-    rows = ahead[:, :features].astype(F32) + jnp.dot(
-        match, everything, preferred_element_type=F32
-    )
-    back, terms = expert_rows(rows.astype(BF16), rate, factors, 1, weights)
-    for at in range(0, features, CHUNK):
-        part = back(slice(at, at + CHUNK))
+    came, (factors, terms0), weights = refs[:4], refs[4:6], refs[6:12]
+    outs, ahead_at = refs[12:16], refs[16]
+    features = ahead_at.shape[1] - META
+    for k in range(E_FLY):
+        ahead_at[MOST * k:MOST * (k + 1), :] = came[k][PAIRS:PAIRS + MOST, :].astype(F32)
+    meta = ahead_at[:, features:]
+    rate = meta[:, E_FLY * PAIRS:E_FLY * PAIRS + 1]
+    match = meta[:, :E_FLY * PAIRS].astype(BF16)
+    everything = jnp.concatenate([ref[:PAIRS, :features] for ref in came], axis=0)
+    rows = ahead_at[:, :features] + jnp.dot(match, everything, preferred_element_type=F32)
+    backs, terms = expert_rows(rows.astype(BF16), rate, factors, 1, weights)
+    for back in backs:
+        part, value = back()
         for k, out in enumerate(outs):
-            out[:, at:at + CHUNK] = part[MOST * k:MOST * (k + 1)].astype(BF16)
+            out[:, part] = value[MOST * k:MOST * (k + 1)].astype(BF16)
     meta = first_lanes(split(terms) + split(terms0[:, 0:1]))
     for k, out in enumerate(outs):
         out[:, features:] = meta[MOST * k:MOST * (k + 1)].astype(BF16)
@@ -212,7 +258,7 @@
         rows = came[(E_FLY - k) % E_FLY][MOST * k:MOST * (k + 1), :features]
         rows_at[MOST * k:MOST * (k + 1), :] = rows.astype(F32)
     take_rows(back_at, got)
-    select0 = came[0][:, features:]
+    select0 = came[0][:PAIRS, features:]
     keys = [keys_of(routes, positions, step) for step in range(STEPS)]
     select1 = one_hot(keys[1], label).astype(BF16)
     last = p == lax.axis_size("pipe") - 1
@@ -266,37 +312,62 @@
 
     pair = jax.ShapeDtypeStruct((MOST, width), BF16)
     block = jax.ShapeDtypeStruct((PAIRS, width), BF16)
+    wide = jax.ShapeDtypeStruct((PAIRS + MOST, width), BF16)
     row_scratch = pltpu.VMEM((PAIRS, width), F32)
 
-    picked = call(
-        pick_kernel, "pick_rows", [pair] * E_FLY + [jax.ShapeDtypeStruct((4, tokens), F32)]
-    )(grad, routes, positions, probs)
-    got = [along(picked[k], k) for k in range(E_FLY)]
-    table = relay(picked[E_FLY], 1)
+    acts_other = across(acts)
     weights = []
     for array in (w_down[0], w_gate[0], w_up[0]):
         weights += [array, across(array)]
-    acts_other = across(acts)
-    shifted = relay(grad, -1)
-    *ahead, factors = call(
-        ahead_kernel,
-        "rows_ahead",
-        [pair] * E_FLY + [jax.ShapeDtypeStruct((STEPS, 3, PAIRS, hidden), F32)],
-        [pltpu.VMEM((PAIRS, hidden), F32)] * 2,
-    )(grad, routes, positions, table, acts, acts_other)
-    ahead = [along(ahead[k], k) for k in range(E_FLY)]
-    rows, ahead_rows, terms0 = call(
+    table = call(
+        table_kernel, "next_table", jax.ShapeDtypeStruct((4, tokens), F32), operands=3
+    )(routes, positions, probs)
+    table = relay(table, 1)
+    picked = list(
+        call(pick_kernel, "pick_rows", [pair] * E_FLY, operands=4)(
+            grad, routes, positions, probs
+        )
+    )
+    acts_other, picked[1] = lax.optimization_barrier((acts_other, picked[1]))
+    weights[1], picked[2] = lax.optimization_barrier((weights[1], picked[2]))
+    weights[3], picked[3] = lax.optimization_barrier((weights[3], picked[3]))
+    got = [along(picked[k], k) for k in range(E_FLY)]
+    own = weights[::2]
+    ahead, factors, *own = call(
+        prepare_kernel,
+        "prepare",
+        [pltpu.VMEM((2 * PAIRS, width), BF16), pltpu.VMEM((STEPS, 3, PAIRS, hidden), F32)]
+        + [pltpu.VMEM(array.shape, BF16) for array in own],
+        [
+            pltpu.VMEM(grad.shape, BF16),
+            pltpu.VMEM((2 * acts.shape[0] * acts.shape[1], hidden), F32),
+            pltpu.SemaphoreType.DMA((4,)),
+        ],
+        hbm=4,
+        operands=9,
+        limit=LIMIT,
+        cost=COST3,
+    )(grad, *own, routes, positions, table, acts, acts_other)
+    weights[::2] = own
+    rows, terms0 = call(
         step_zero_kernel,
         "step_zero",
-        [block, block, jax.ShapeDtypeStruct((PAIRS, META), F32)],
+        [
+            jax.ShapeDtypeStruct((2 * PAIRS, width), BF16),
+            jax.ShapeDtypeStruct((PAIRS, META), F32),
+        ],
         [row_scratch],
-    )(*got, *ahead, routes, positions, factors, *weights)
+        operands=12,
+        cost=COST0,
+    )(*got, factors, ahead, *weights)
     came = relay(rows, -1)
-    ahead_rows = relay(ahead_rows, -1)
-    came = [along(came, j) for j in range(E_FLY)]
-    back = call(step_one_kernel, "step_one", [pair] * E_FLY)(
-        *came, ahead_rows, factors, terms0, *weights
-    )
+    shifted, rows = lax.optimization_barrier((grad, rows))
+    shifted = relay(shifted, -1)
+    sends = call(merge_kernel, "merge", [wide] * (E_FLY - 1), operands=1, cost=COST2)(came)
+    came = [came] + [along(send, k + 1) for k, send in enumerate(sends)]
+    back = call(
+        step_one_kernel, "step_one", [pair] * E_FLY, [row_scratch], operands=12, cost=COST1
+    )(*came, factors, terms0, *weights)
     back = [along(back[k], E_FLY - k) for k in range(E_FLY)]
     result, prob = call(
         final_kernel,
@@ -306,6 +377,7 @@
             jax.ShapeDtypeStruct((STEPS, 2, tokens), F32),
         ],
         [pltpu.VMEM((PAIRS, features), F32), row_scratch],
+        operands=11,
     )(shifted, routes, positions, *came, *back)
     return result[None], prob.transpose(0, 2, 1)[None]
 

time: 86.7 us -> 47.4 us (0.55)
  waiting for transfers between devices: 54.2 us -> 16.4 us
  local copies, waits for them, and re-layouts: 3.83 us -> 1.92 us
  Pallas kernels: 7.65 us -> 9.5 us
  starting transfers between devices: 20 us -> 18.7 us
    ppermute x4 -> x3, waiting for transfers between devices: 23.1 us -> 3.25 us  [relay(): return lax.ppermute(block, 'pipe', route)]
    ppermute x12 -> x9, waiting for transfers between devices: 29.7 us -> 13.1 us  [along(): lax.ppermute(block, 'expert', [(i, (i + 2 * k) % devices) for i in range(...]
    unnamed x18 -> x12, local copies, waits for them, and re-layouts: 3.83 us -> 1.92 us
    pallas_call x4 -> x6, Pallas kernels: 5.97 us -> 7.82 us  [the longest x1 2.73 us: local_chip(): call(step_one_kernel, 'step_one', [pair] * E_FLY, [row_scratch], operands...]
    ppermute x12 -> x9, starting transfers between devices: 13.6 us -> 11.9 us  [along(): lax.ppermute(block, 'expert', [(i, (i + 2 * k) % devices) for i in range(...]
    ppermute x4, waiting for transfers between devices: 1.4 us -> 0.01 us  [across(): return lax.ppermute(block, 'expert', [(i, i ^ 1) for i in range(devices)])]
    ppermute x4 -> x3, starting transfers between devices: 5.41 us -> 5.61 us  [relay(): return lax.ppermute(block, 'pipe', route)]
  transfers between devices with their start and end apart: 20 -> 16, of which waited for: 15 -> 7; matrix products, arithmetic and copies ran while one was open for 0% -> 0% of each run, Pallas kernels for 7% -> 11%
where the time goes in v2:
time: 47.4 us; the launch traced here: 47.2 us
  starting transfers between devices  18.7 us (39%)
  waiting for transfers between devices  16.4 us (35%)
  Pallas kernels  9.5 us (20%)
  local copies, waits for them, and re-layouts  1.92 us (4%)
  between operations  0.7 us (1%)
    ppermute x9, waiting for transfers between devices, along(): lax.ppermute(block, 'expert', [(i, (i + 2 * k) % devices) for i in range(...  13.1 us
    ppermute x9, starting transfers between devices, along(): lax.ppermute(block, 'expert', [(i, (i + 2 * k) % devices) for i in range(...  11.9 us
    ppermute x3, starting transfers between devices, relay(): return lax.ppermute(block, 'pipe', route)  5.61 us
    ppermute x3, waiting for transfers between devices, relay(): return lax.ppermute(block, 'pipe', route)  3.25 us
    pallas_call x1, Pallas kernels, local_chip(): call(step_one_kernel, 'step_one', [pair] * E_FLY, [row_scratch], operands...  2.73 us
    pallas_call x1, Pallas kernels, local_chip(): call(step_zero_kernel, 'step_zero', [jax.ShapeDtypeStruct((2 * PAIRS, wid...  2.65 us
    pallas_call x1, Pallas kernels, local_chip(): call(prepare_kernel, 'prepare', [pltpu.VMEM((2 * PAIRS, width), BF16), pl...  2.16 us
    unnamed x12, local copies, waits for them, and re-layouts  1.92 us
  transfers between devices with their start and end apart: 16, of which 7 were waited for; matrix products, arithmetic and copies ran while one was open for 0% of the time, Pallas kernels for 11%

profile of v2, /device:TPU:0, one launch (start us, length us, event | category | flops | bytes accessed | tf_op | source)
XLA Modules:
  0.0 47.2 jit_solution(7044297993867247669)
XLA Ops:
  0.6 0.5 %collective-permute-start.4 = (bf16[3840,128]{1,0:T(8,128)(2,1)}, bf16[3840,128]{1,0:T(8,128)(2,1)S(1)}, u32[]{:S(2)}, u32[]{:S(2)}) collective-permute-start(bf16[3840,128]{1,0:T(8,128)(2,1)} %bitcast.35), channel_id=1, source_target_pairs={{0,1},{1,0},{2,3},{3,2},{4,5},{5,4},{6,7},{7,6},{8,9},{9,8},{10,11... | collective-permute-start | bytes 2949128 | tf_op jit(solution)/shard_map/ppermute | solution.py:300
  1.1 0.1 collective-permute-start.2
  1.2 0.4 collective-permute-start
  1.7 0.0 copy-start.3
  1.7 0.0 copy-start.2
  1.7 0.0 copy-start.4
  1.7 0.7 %copy-done.3 = s32[1,2,128,2]{2,3,1,0:T(2,128)S(1)} copy-done((s32[1,2,128,2]{2,3,1,0:T(2,128)S(1)}, s32[1,2,128,2]{2,3,1,0:T(2,128)}, u32[]{:S(2)}) %copy-start.3) | copy-done | bytes 2072
  2.3 0.0 copy-done.2
  2.4 0.0 copy-done.4
  2.4 2.6 %collective-permute-start.6 = (f32[4,128]{1,0:T(4,128)S(1)}, f32[4,128]{1,0:T(4,128)S(1)}, u32[]{:S(2)}, u32[]{:S(2)}) collective-permute-start(f32[4,128]{1,0:T(4,128)S(1)} %next_table.1), channel_id=1, source_target_pairs={{0,8},{8,16},{16,24},{24,0},{1,9},{9,17},{17,25},{25,1},{2,10},{10... | collective-permute-start | bytes 6152 | tf_op jit(solution)/shard_map/ppermute | solution.py:311
  5.0 0.2 collective-permute-start.7
  5.1 0.0 copy-start
  5.1 1.2 %copy-done = bf16[1,128,3840]{2,1,0:T(8,128)(2,1)S(1)} copy-done((bf16[1,128,3840]{2,1,0:T(8,128)(2,1)S(1)}, bf16[1,128,3840]{2,1,0:T(8,128)(2,1)}, u32[]{:S(2)}) %copy-start) | copy-done | bytes 983064
  6.3 0.0 copy-start.5
  6.3 0.2 pick_rows.1
  6.6 0.0 collective-permute-done.refs_8_
  6.6 1.6 %collective-permute-start.1 = (bf16[2,3968]{1,0:T(2,128)(2,1)S(1)}, bf16[2,3968]{1,0:T(2,128)(2,1)S(1)}, u32[]{:S(2)}, u32[]{:S(2)}) collective-permute-start(bf16[2,3968]{1,0:T(2,128)(2,1)S(1)} %get-tuple-element.31), channel_id=1, source_target_pairs={{0,2},{1,3},{2,4},{3,5},{4,6},{5,7},{6,0},{7,1},{8,10},{9,11},{10,... | collective-permute-start | bytes 47624 | tf_op jit(solution)/shard_map/ppermute | solution.py:305
  8.2 0.0 collective-permute-done.4.refs_9_
  8.2 2.2 %collective-permute-start.5 = (bf16[2,3968]{1,0:T(2,128)(2,1)S(1)}, bf16[2,3968]{1,0:T(2,128)(2,1)S(1)}, u32[]{:S(2)}, u32[]{:S(2)}) collective-permute-start(bf16[2,3968]{1,0:T(2,128)(2,1)S(1)} %get-tuple-element.35), channel_id=1, source_target_pairs={{0,6},{1,7},{2,0},{3,1},{4,2},{5,3},{6,4},{7,5},{8,14},{9,15},{10,... | collective-permute-start | bytes 47624 | tf_op jit(solution)/shard_map/ppermute | solution.py:305
  10.5 0.0 collective-permute-done.2.refs_7_
  10.5 0.8 %collective-permute-start.3 = (bf16[2,3968]{1,0:T(2,128)(2,1)S(1)}, bf16[2,3968]{1,0:T(2,128)(2,1)S(1)}, u32[]{:S(2)}, u32[]{:S(2)}) collective-permute-start(bf16[2,3968]{1,0:T(2,128)(2,1)S(1)} %get-tuple-element.33), channel_id=1, source_target_pairs={{0,4},{1,5},{2,6},{3,7},{4,0},{5,1},{6,2},{7,3},{8,12},{9,13},{10,... | collective-permute-start | bytes 47624 | tf_op jit(solution)/shard_map/ppermute | solution.py:305
  11.3 0.0 collective-permute-done.6.refs_6_
  11.3 0.0 copy-done.5
  11.3 2.2 %prepare.1 = (bf16[16,3968]{1,0:T(8,128)(2,1)S(1)}, f32[2,3,8,256]{3,2,1,0:T(8,128)S(1)}, bf16[128,3840]{1,0:T(8,128)(2,1)S(1)}, bf16[3840,128]{1,0:T(8,128)(2,1)S(1)}, bf16[3840,128]{1,0:T(8,128)(2,1)S(1)}) custom-call(bf16[128,3840]{1,0:T(8,128)(2,1)} %bitcast.18, bf16[128,3840]{1,0:T(8,128)(2,1)} %bitcast.34, bf16[3840,128]{1,0:T(8,128)(2,1)} %bitcast.36, ...), custom_call_target="tpu_custom_call" | custom-call | flops 20000000000 | tf_op jit(solution)/shard_map/prepare/pallas_call | solution.py:336
  13.5 0.0 collective-permute-done.1.refs_1_
  13.5 0.0 collective-permute-done.7.refs_11_
  13.5 0.0 collective-permute-done.5.refs_3_
  13.5 1.6 %collective-permute-done.3.refs_2_ = bf16[2,3968]{1,0:T(2,128)(2,1)S(1)} collective-permute-done((bf16[2,3968]{1,0:T(2,128)(2,1)S(1)}, bf16[2,3968]{1,0:T(2,128)(2,1)S(1)}, u32[]{:S(2)}, u32[]{:S(2)}) %collective-permute-start.3) | collective-permute-done | bytes 15904 | tf_op jit(solution)/shard_map/ppermute | solution.py:305
  15.1 2.7 %step_zero.1 = (bf16[16,3968]{1,0:T(8,128)(2,1)S(1)}, f32[8,128]{1,0:T(8,128)S(1)}) custom-call(bf16[2,3968]{1,0:T(2,128)(2,1)S(1)} %get-tuple-element.29.refs_0_, bf16[2,3968]{1,0:T(2,128)(2,1)S(1)} %collective-permute-done.1.refs_1_, bf16[2,3968]{1,0:T(2,128)(2,1)S(1)} %collective-permute-done.3.refs_2_, ...), custom_call_target="tpu_custom_call" | custom-call | flops 20000000000 | tf_op jit(solution)/shard_map/step_zero/pallas_call | solution.py:352
  17.8 2.2 %collective-permute-start.9 = (bf16[16,3968]{1,0:T(8,128)(2,1)S(1)}, bf16[16,3968]{1,0:T(8,128)(2,1)S(1)}, u32[]{:S(2)}, u32[]{:S(2)}) collective-permute-start(bf16[16,3968]{1,0:T(8,128)(2,1)S(1)} %get-tuple-element.44), channel_id=1, source_target_pairs={{0,24},{8,0},{16,8},{24,16},{1,25},{9,1},{17,9},{25,17},{2,26},{10... | collective-permute-start | bytes 380936 | tf_op jit(solution)/shard_map/ppermute | solution.py:311
  19.9 0.0 copy-done.1
  19.9 0.8 %collective-permute-start.8 = (bf16[128,3840]{1,0:T(8,128)(2,1)S(1)}, bf16[128,3840]{1,0:T(8,128)(2,1)S(1)}, u32[]{:S(2)}, u32[]{:S(2)}) collective-permute-start(bf16[128,3840]{1,0:T(8,128)(2,1)S(1)} %bitcast.20), channel_id=1, source_target_pairs={{0,24},{8,0},{16,8},{24,16},{1,25},{9,1},{17,9},{25,17},{2,26},{10... | collective-permute-start | bytes 2949128 | tf_op jit(solution)/shard_map/ppermute | solution.py:311
  20.8 3.2 %collective-permute-done.9.came.refs_0_.refs_3_ = bf16[16,3968]{1,0:T(8,128)(2,1)S(1)} collective-permute-done((bf16[16,3968]{1,0:T(8,128)(2,1)S(1)}, bf16[16,3968]{1,0:T(8,128)(2,1)S(1)}, u32[]{:S(2)}, u32[]{:S(2)}) %collective-permute-start.9) | collective-permute-done | bytes 127008 | tf_op jit(solution)/shard_map/ppermute | solution.py:311
  24.1 0.1 collective-permute-start.10
  24.1 2.4 %collective-permute-start.11 = (bf16[10,3968]{1,0:T(8,128)(2,1)S(1)}, bf16[10,3968]{1,0:T(8,128)(2,1)S(1)}, u32[]{:S(2)}, u32[]{:S(2)}) collective-permute-start(bf16[10,3968]{1,0:T(8,128)(2,1)S(1)} %get-tuple-element.47), channel_id=1, source_target_pairs={{0,4},{1,5},{2,6},{3,7},{4,0},{5,1},{6,2},{7,3},{8,12},{9,13},{10,... | collective-permute-start | bytes 238088 | tf_op jit(solution)/shard_map/ppermute | solution.py:305
  26.5 1.4 %collective-permute-start.12 = (bf16[10,3968]{1,0:T(8,128)(2,1)S(1)}, bf16[10,3968]{1,0:T(8,128)(2,1)S(1)}, u32[]{:S(2)}, u32[]{:S(2)}) collective-permute-start(bf16[10,3968]{1,0:T(8,128)(2,1)S(1)} %get-tuple-element.48), channel_id=1, source_target_pairs={{0,6},{1,7},{2,0},{3,1},{4,2},{5,3},{6,4},{7,5},{8,14},{9,15},{10,... | collective-permute-start | bytes 238088 | tf_op jit(solution)/shard_map/ppermute | solution.py:305
  27.9 3.1 %collective-permute-done.10.refs_1_.refs_4_ = bf16[10,3968]{1,0:T(8,128)(2,1)S(1)} collective-permute-done((bf16[10,3968]{1,0:T(8,128)(2,1)S(1)}, bf16[10,3968]{1,0:T(8,128)(2,1)S(1)}, u32[]{:S(2)}, u32[]{:S(2)}) %collective-permute-start.10) | collective-permute-done | bytes 79392 | tf_op jit(solution)/shard_map/ppermute | solution.py:305
  31.0 2.8 %collective-permute-done.11.refs_2_.refs_5_ = bf16[10,3968]{1,0:T(8,128)(2,1)S(1)} collective-permute-done((bf16[10,3968]{1,0:T(8,128)(2,1)S(1)}, bf16[10,3968]{1,0:T(8,128)(2,1)S(1)}, u32[]{:S(2)}, u32[]{:S(2)}) %collective-permute-start.11) | collective-permute-done | bytes 79392 | tf_op jit(solution)/shard_map/ppermute | solution.py:305
  33.9 0.0 collective-permute-done.12.refs_3_.refs_6_
  33.9 2.7 %step_one.1 = (bf16[2,3968]{1,0:T(2,128)(2,1)S(1)}, bf16[2,3968]{1,0:T(2,128)(2,1)S(1)}, bf16[2,3968]{1,0:T(2,128)(2,1)S(1)}, bf16[2,3968]{1,0:T(2,128)(2,1)S(1)}) custom-call(bf16[16,3968]{1,0:T(8,128)(2,1)S(1)} %collective-permute-done.9.came.refs_0_.refs_3_, bf16[10,3968]{1,0:T(8,128)(2,1)S(1)} %collective-permute-done.10.refs_1_.refs_4_, ...), custom_call_target="tpu_custom_call" | custom-call | tf_op jit(solution)/shard_map/step_one/pallas_call | solution.py:368
  36.6 2.8 %collective-permute-start.13 = (bf16[2,3968]{1,0:T(2,128)(2,1)S(1)}, bf16[2,3968]{1,0:T(2,128)(2,1)S(1)}, u32[]{:S(2)}, u32[]{:S(2)}) collective-permute-start(bf16[2,3968]{1,0:T(2,128)(2,1)S(1)} %get-tuple-element.51), channel_id=1, source_target_pairs={{0,6},{1,7},{2,0},{3,1},{4,2},{5,3},{6,4},{7,5},{8,14},{9,15},{10,... | collective-permute-start | bytes 47624 | tf_op jit(solution)/shard_map/ppermute | solution.py:305
  39.4 0.6 %collective-permute-start.14 = (bf16[2,3968]{1,0:T(2,128)(2,1)S(1)}, bf16[2,3968]{1,0:T(2,128)(2,1)S(1)}, u32[]{:S(2)}, u32[]{:S(2)}) collective-permute-start(bf16[2,3968]{1,0:T(2,128)(2,1)S(1)} %get-tuple-element.52), channel_id=1, source_target_pairs={{0,4},{1,5},{2,6},{3,7},{4,0},{5,1},{6,2},{7,3},{8,12},{9,13},{10,... | collective-permute-start | bytes 47624 | tf_op jit(solution)/shard_map/ppermute | solution.py:305
  40.0 0.0 collective-permute-start.15
  40.0 0.8 %collective-permute-done.13.refs_8_ = bf16[2,3968]{1,0:T(2,128)(2,1)S(1)} collective-permute-done((bf16[2,3968]{1,0:T(2,128)(2,1)S(1)}, bf16[2,3968]{1,0:T(2,128)(2,1)S(1)}, u32[]{:S(2)}, u32[]{:S(2)}) %collective-permute-start.13) | collective-permute-done | bytes 15904 | tf_op jit(solution)/shard_map/ppermute | solution.py:305
  40.9 3.2 %collective-permute-done.14.refs_9_ = bf16[2,3968]{1,0:T(2,128)(2,1)S(1)} collective-permute-done((bf16[2,3968]{1,0:T(2,128)(2,1)S(1)}, bf16[2,3968]{1,0:T(2,128)(2,1)S(1)}, u32[]{:S(2)}, u32[]{:S(2)}) %collective-permute-start.14) | collective-permute-done | bytes 15904 | tf_op jit(solution)/shard_map/ppermute | solution.py:305
  44.0 1.5 %collective-permute-done.15.refs_10_ = bf16[2,3968]{1,0:T(2,128)(2,1)S(1)} collective-permute-done((bf16[2,3968]{1,0:T(2,128)(2,1)S(1)}, bf16[2,3968]{1,0:T(2,128)(2,1)S(1)}, u32[]{:S(2)}, u32[]{:S(2)}) %collective-permute-start.15) | collective-permute-done | bytes 15904 | tf_op jit(solution)/shard_map/ppermute | solution.py:305
  45.5 0.0 collective-permute-done.8.refs_0_
  45.5 1.7 %final_sums.1 = (bf16[128,3840]{1,0:T(8,128)(2,1)}, f32[2,2,128]{2,1,0:T(2,128)}) custom-call(bf16[128,3840]{1,0:T(8,128)(2,1)S(1)} %collective-permute-done.8.refs_0_, s32[2,2,128]{2,1,0:T(2,128)S(1)} %bitcast.24, s32[2,2,128]{2,1,0:T(2,128)S(1)} %bitcast.28, bf16[16,3968]{1,0:T(8,128)(2,1)S(1)} %collective-permute-done.9.came.refs_0_.refs_3_, ...), custom_call_target="tpu_custom_call" | custom-call | tf_op jit(solution)/shard_map/final_sums/pallas_call | solution.py:372
  (3 shorter events, 0.0 us)
Async XLA Ops:
  0.6 7.6 %collective-permute-start.4 = (bf16[3840,128]{1,0:T(8,128)(2,1)}, bf16[3840,128]{1,0:T(8,128)(2,1)S(1)}, u32[]{:S(2)}, u32[]{:S(2)}) collective-permute-start(bf16[3840,128]{1,0:T(8,128)(2,1)} %bitcast.35), channel_id=1, source_target_pairs={{0,1},{1,0},{2,3},{3,2},{4,5},{5,4},{6,7},{7,6},{8,9},{9,8},{10,11... | collective-permute-start | bytes 2949128 | tf_op jit(solution)/shard_map/ppermute | solution.py:300
  1.1 9.3 %collective-permute-start.2 = (bf16[128,3840]{1,0:T(8,128)(2,1)}, bf16[128,3840]{1,0:T(8,128)(2,1)S(1)}, u32[]{:S(2)}, u32[]{:S(2)}) collective-permute-start(bf16[128,3840]{1,0:T(8,128)(2,1)} %bitcast.33), channel_id=1, source_target_pairs={{0,1},{1,0},{2,3},{3,2},{4,5},{5,4},{6,7},{7,6},{8,9},{9,8},{10,11... | collective-permute-start | bytes 2949128 | tf_op jit(solution)/shard_map/ppermute | solution.py:300
  1.2 5.4 %collective-permute-start = (bf16[2,16,2,128]{3,2,1,0:T(2,128)(2,1)}, bf16[2,16,2,128]{3,2,1,0:T(2,128)(2,1)S(1)}, u32[]{:S(2)}, u32[]{:S(2)}) collective-permute-start(bf16[2,16,2,128]{3,2,1,0:T(2,128)(2,1)} %bitcast.31), channel_id=1, source_target_pairs={{0,1},{1,0},{2,3},{3,2},{4,5},{5,4},{6,7},{7,6},{8,9},{9,8},{10,11... | collective-permute-start | bytes 49160 | tf_op jit(solution)/shard_map/ppermute | solution.py:300
  1.7 0.7 %copy-start.3 = (s32[1,2,128,2]{2,3,1,0:T(2,128)S(1)}, s32[1,2,128,2]{2,3,1,0:T(2,128)}, u32[]{:S(2)}) copy-start(s32[1,2,128,2]{2,3,1,0:T(2,128)} %param.10) | copy-start | bytes 6148
  1.7 0.7 %copy-start.2 = (s32[1,2,128,2]{2,3,1,0:T(2,128)S(1)}, s32[1,2,128,2]{2,3,1,0:T(2,128)}, u32[]{:S(2)}) copy-start(s32[1,2,128,2]{2,3,1,0:T(2,128)} %param.9) | copy-start | bytes 6148
  1.7 0.7 %copy-start.4 = (bf16[1,2,128,2]{2,3,1,0:T(2,128)(2,1)S(1)}, bf16[1,2,128,2]{2,3,1,0:T(2,128)(2,1)}, u32[]{:S(2)}) copy-start(bf16[1,2,128,2]{2,3,1,0:T(2,128)(2,1)} %param.11) | copy-start | bytes 3076
  2.4 8.9 %collective-permute-start.6 = (f32[4,128]{1,0:T(4,128)S(1)}, f32[4,128]{1,0:T(4,128)S(1)}, u32[]{:S(2)}, u32[]{:S(2)}) collective-permute-start(f32[4,128]{1,0:T(4,128)S(1)} %next_table.1), channel_id=1, source_target_pairs={{0,8},{8,16},{16,24},{24,0},{1,9},{9,17},{17,25},{25,1},{2,10},{10... | collective-permute-start | bytes 6152 | tf_op jit(solution)/shard_map/ppermute | solution.py:311
  5.0 8.5 %collective-permute-start.7 = (bf16[3840,128]{1,0:T(8,128)(2,1)}, bf16[3840,128]{1,0:T(8,128)(2,1)S(1)}, u32[]{:S(2)}, u32[]{:S(2)}) collective-permute-start(bf16[3840,128]{1,0:T(8,128)(2,1)} %bitcast.37), channel_id=1, source_target_pairs={{0,1},{1,0},{2,3},{3,2},{4,5},{5,4},{6,7},{7,6},{8,9},{9,8},{10,11... | collective-permute-start | bytes 2949128 | tf_op jit(solution)/shard_map/ppermute | solution.py:300
  5.1 1.2 %copy-start = (bf16[1,128,3840]{2,1,0:T(8,128)(2,1)S(1)}, bf16[1,128,3840]{2,1,0:T(8,128)(2,1)}, u32[]{:S(2)}) copy-start(bf16[1,128,3840]{2,1,0:T(8,128)(2,1)} %param.8) | copy-start | bytes 2949124
  6.3 4.9 %copy-start.5 = (bf16[1,2,16,2,128]{4,3,2,1,0:T(2,128)(2,1)S(1)}, bf16[1,2,16,2,128]{4,3,2,1,0:T(2,128)(2,1)}, u32[]{:S(2)}) copy-start(bf16[1,2,16,2,128]{4,3,2,1,0:T(2,128)(2,1)} %param.12) | copy-start | bytes 49156
  6.6 6.9 %collective-permute-start.1 = (bf16[2,3968]{1,0:T(2,128)(2,1)S(1)}, bf16[2,3968]{1,0:T(2,128)(2,1)S(1)}, u32[]{:S(2)}, u32[]{:S(2)}) collective-permute-start(bf16[2,3968]{1,0:T(2,128)(2,1)S(1)} %get-tuple-element.31), channel_id=1, source_target_pairs={{0,2},{1,3},{2,4},{3,5},{4,6},{5,7},{6,0},{7,1},{8,10},{9,11},{10,... | collective-permute-start | bytes 47624 | tf_op jit(solution)/shard_map/ppermute | solution.py:305
  8.2 5.2 %collective-permute-start.5 = (bf16[2,3968]{1,0:T(2,128)(2,1)S(1)}, bf16[2,3968]{1,0:T(2,128)(2,1)S(1)}, u32[]{:S(2)}, u32[]{:S(2)}) collective-permute-start(bf16[2,3968]{1,0:T(2,128)(2,1)S(1)} %get-tuple-element.35), channel_id=1, source_target_pairs={{0,6},{1,7},{2,0},{3,1},{4,2},{5,3},{6,4},{7,5},{8,14},{9,15},{10,... | collective-permute-start | bytes 47624 | tf_op jit(solution)/shard_map/ppermute | solution.py:305
  10.5 4.6 %collective-permute-start.3 = (bf16[2,3968]{1,0:T(2,128)(2,1)S(1)}, bf16[2,3968]{1,0:T(2,128)(2,1)S(1)}, u32[]{:S(2)}, u32[]{:S(2)}) collective-permute-start(bf16[2,3968]{1,0:T(2,128)(2,1)S(1)} %get-tuple-element.33), channel_id=1, source_target_pairs={{0,4},{1,5},{2,6},{3,7},{4,0},{5,1},{6,2},{7,3},{8,12},{9,13},{10,... | collective-permute-start | bytes 47624 | tf_op jit(solution)/shard_map/ppermute | solution.py:305
  15.1 4.8 %copy-start.1 = (bf16[1,128,3840]{2,1,0:T(8,128)(2,1)S(1)}, bf16[1,128,3840]{2,1,0:T(8,128)(2,1)}, u32[]{:S(2)}) copy-start(bf16[1,128,3840]{2,1,0:T(8,128)(2,1)} %param.8) | copy-start | bytes 2949124
  17.8 6.3 %collective-permute-start.9 = (bf16[16,3968]{1,0:T(8,128)(2,1)S(1)}, bf16[16,3968]{1,0:T(8,128)(2,1)S(1)}, u32[]{:S(2)}, u32[]{:S(2)}) collective-permute-start(bf16[16,3968]{1,0:T(8,128)(2,1)S(1)} %get-tuple-element.44), channel_id=1, source_target_pairs={{0,24},{8,0},{16,8},{24,16},{1,25},{9,1},{17,9},{25,17},{2,26},{10... | collective-permute-start | bytes 380936 | tf_op jit(solution)/shard_map/ppermute | solution.py:311
  19.9 25.6 %collective-permute-start.8 = (bf16[128,3840]{1,0:T(8,128)(2,1)S(1)}, bf16[128,3840]{1,0:T(8,128)(2,1)S(1)}, u32[]{:S(2)}, u32[]{:S(2)}) collective-permute-start(bf16[128,3840]{1,0:T(8,128)(2,1)S(1)} %bitcast.20), channel_id=1, source_target_pairs={{0,24},{8,0},{16,8},{24,16},{1,25},{9,1},{17,9},{25,17},{2,26},{10... | collective-permute-start | bytes 2949128 | tf_op jit(solution)/shard_map/ppermute | solution.py:311
  24.1 7.0 %collective-permute-start.10 = (bf16[10,3968]{1,0:T(8,128)(2,1)S(1)}, bf16[10,3968]{1,0:T(8,128)(2,1)S(1)}, u32[]{:S(2)}, u32[]{:S(2)}) collective-permute-start(bf16[10,3968]{1,0:T(8,128)(2,1)S(1)} %get-tuple-element.46), channel_id=1, source_target_pairs={{0,2},{1,3},{2,4},{3,5},{4,6},{5,7},{6,0},{7,1},{8,10},{9,11},{10,... | collective-permute-start | bytes 238088 | tf_op jit(solution)/shard_map/ppermute | solution.py:305
  24.1 9.7 %collective-permute-start.11 = (bf16[10,3968]{1,0:T(8,128)(2,1)S(1)}, bf16[10,3968]{1,0:T(8,128)(2,1)S(1)}, u32[]{:S(2)}, u32[]{:S(2)}) collective-permute-start(bf16[10,3968]{1,0:T(8,128)(2,1)S(1)} %get-tuple-element.47), channel_id=1, source_target_pairs={{0,4},{1,5},{2,6},{3,7},{4,0},{5,1},{6,2},{7,3},{8,12},{9,13},{10,... | collective-permute-start | bytes 238088 | tf_op jit(solution)/shard_map/ppermute | solution.py:305
  26.5 7.4 %collective-permute-start.12 = (bf16[10,3968]{1,0:T(8,128)(2,1)S(1)}, bf16[10,3968]{1,0:T(8,128)(2,1)S(1)}, u32[]{:S(2)}, u32[]{:S(2)}) collective-permute-start(bf16[10,3968]{1,0:T(8,128)(2,1)S(1)} %get-tuple-element.48), channel_id=1, source_target_pairs={{0,6},{1,7},{2,0},{3,1},{4,2},{5,3},{6,4},{7,5},{8,14},{9,15},{10,... | collective-permute-start | bytes 238088 | tf_op jit(solution)/shard_map/ppermute | solution.py:305
  36.6 4.2 %collective-permute-start.13 = (bf16[2,3968]{1,0:T(2,128)(2,1)S(1)}, bf16[2,3968]{1,0:T(2,128)(2,1)S(1)}, u32[]{:S(2)}, u32[]{:S(2)}) collective-permute-start(bf16[2,3968]{1,0:T(2,128)(2,1)S(1)} %get-tuple-element.51), channel_id=1, source_target_pairs={{0,6},{1,7},{2,0},{3,1},{4,2},{5,3},{6,4},{7,5},{8,14},{9,15},{10,... | collective-permute-start | bytes 47624 | tf_op jit(solution)/shard_map/ppermute | solution.py:305
  39.4 4.6 %collective-permute-start.14 = (bf16[2,3968]{1,0:T(2,128)(2,1)S(1)}, bf16[2,3968]{1,0:T(2,128)(2,1)S(1)}, u32[]{:S(2)}, u32[]{:S(2)}) collective-permute-start(bf16[2,3968]{1,0:T(2,128)(2,1)S(1)} %get-tuple-element.52), channel_id=1, source_target_pairs={{0,4},{1,5},{2,6},{3,7},{4,0},{5,1},{6,2},{7,3},{8,12},{9,13},{10,... | collective-permute-start | bytes 47624 | tf_op jit(solution)/shard_map/ppermute | solution.py:305
  40.0 5.5 %collective-permute-start.15 = (bf16[2,3968]{1,0:T(2,128)(2,1)S(1)}, bf16[2,3968]{1,0:T(2,128)(2,1)S(1)}, u32[]{:S(2)}, u32[]{:S(2)}) collective-permute-start(bf16[2,3968]{1,0:T(2,128)(2,1)S(1)} %get-tuple-element.53), channel_id=1, source_target_pairs={{0,2},{1,3},{2,4},{3,5},{4,6},{5,7},{6,0},{7,1},{8,10},{9,11},{10,... | collective-permute-start | bytes 47624 | tf_op jit(solution)/shard_map/ppermute | solution.py:305

commit v3 on v2

--- a/solution.py
+++ b/solution.py
@@ -13,11 +13,12 @@
 PAIRS = E_FLY * MOST
 META = 128
 CHUNK = 256
+SPAN = 1024
 COST0 = 20_000_000_000
 COST1 = 0
 COST2 = 20_000_000_000
 COST3 = 20_000_000_000
-LIMIT = 50
+LIMIT = 54
 F32 = jnp.float32
 BF16 = jnp.bfloat16
 NT = (((1,), (1,)), ((), ()))
@@ -75,6 +76,16 @@
     return out
 
 
+def bring(sources, targets, sems):
+    copies = [
+        pltpu.make_async_copy(source, target, sems.at[index])
+        for index, (source, target) in enumerate(zip(sources, targets))
+    ]
+    for copy in copies:
+        copy.start()
+    return copies
+
+
 def put_rows(outs, rows, meta):
     width = rows.shape[1]
     for k, out in enumerate(outs):
@@ -87,27 +98,32 @@
         scratch[MOST * k:MOST * (k + 1), :] = ref[...].astype(F32)
 
 
-def table_kernel(routes, positions, probs, table):
+def pick_kernel(*refs):
+    outs, (table, *weights), held, sems = refs[7:11], refs[11:15], refs[15:19], refs[19]
+    copies = bring(refs[:7], (*held, *weights), sems)
+    routes, positions, probs, grad = held
+    for copy in copies[:3]:
+        copy.wait()
+    _, z, _ = place()
+    keys = keys_of(routes, positions, 0)
+    label = labels(PAIRS, lambda k: z ^ k)
+    select = one_hot(keys, label)
+    rate = rates_of(keys, probs[0].astype(F32), label)
     table[0:2] = keys_of(routes, positions, 1).astype(F32)
     table[2:4] = probs[1].astype(F32)
-
-
-def pick_kernel(grad, routes, positions, probs, *outs):
-    _, z, _ = place()
-    keys = keys_of(routes, positions, 0)
-    label = labels(PAIRS, lambda k: (z + k) % E_FLY)
-    select = one_hot(keys, label)
+    copies[3].wait()
     rows = jnp.dot(select.astype(BF16), grad[...], preferred_element_type=F32)
-    rate = rates_of(keys, probs[0].astype(F32), label)
     put_rows(outs, rows, first_lanes([rate]))
-
-
-def rows_ahead(grad, routes, positions, table, rows_out):
+    for copy in copies[4:]:
+        copy.wait()
+
+
+def ahead_kernel(grad, routes, positions, table, done, rows_out, held, packed):
     p, z, c = place()
     keys0 = keys_of(routes, positions, 0)
     keys1 = table[0:2].astype(jnp.int32)
     keys1 = jnp.where(p == 0, -1, keys1)
-    label = labels(PAIRS, lambda k: (z + k) % E_FLY)
+    label = labels(PAIRS, lambda k: z ^ k)
     select = one_hot(keys1, label)
     rows = jnp.dot(select.astype(BF16), grad[...], preferred_element_type=F32)
     rate = rates_of(keys1, table[2:4], label)
@@ -117,21 +133,30 @@
     source, block, spot = column // PAIRS, column // MOST % E_FLY, column % MOST
     row = lax.broadcasted_iota(jnp.int32, (PAIRS, 1), 0)
     for k in range(E_FLY):
-        expert = (z + k + E_FLY - source) % E_FLY
-        own = (source < E_FLY) & ((source + block) % E_FLY == k)
+        expert = z ^ k ^ source
+        own = (source < E_FLY) & (source ^ block == k)
         step0 = one_hot(keys0, jnp.where(own, expert * MOST + spot, -2))
         match = lax.dot_general(
             select.astype(BF16), step0.astype(BF16), NT, preferred_element_type=F32
         )
         meta = meta + jnp.where(row // MOST == k, match, 0.0)
     features = rows.shape[1]
-    rows_out[PAIRS:, :features] = rows.astype(BF16)
-    rows_out[PAIRS:, features:] = meta.astype(BF16)
+    width = features + META
+    rows_out[:, :features] = done[...]
     taken = one_hot(jnp.where(p == 0, -1, keys0), label)
-    rows_out[:PAIRS, features:] = taken.astype(BF16)
-
-
-def act_factors(acts, acts_other, factors, rows_at):
+    rows_out[:, features:width] = taken.astype(BF16)
+    held[:, :features] = rows
+    held[:, features:width] = meta
+    parts = PAIRS // MOST
+    for at in range(PAIRS):
+        k, spot = at // MOST, at % MOST
+        for part in range(parts):
+            piece = held[at:at + 1, part * SPAN:(part + 1) * SPAN]
+            packed[parts * spot + part:parts * spot + part + 1, k * SPAN:(k + 1) * SPAN] = piece
+    rows_out[:, width:] = packed[...].astype(BF16)
+
+
+def factor_kernel(acts, acts_other, factors, rows_at):
     _, z, c = place()
     steps, slots, _, width = acts.shape
     for half, ref in enumerate((acts, acts_other)):
@@ -143,7 +168,7 @@
     row = lax.broadcasted_iota(jnp.int32, (2 * steps * PAIRS, 2 * steps * slots), 0)
     column = lax.broadcasted_iota(jnp.int32, row.shape, 1)
     group, k, spot = row // PAIRS, row // MOST % E_FLY, row % MOST
-    slot = (2 * ((z + E_FLY - k) % E_FLY) + c) * MOST + spot
+    slot = (2 * (z ^ k) + c) * MOST + spot
     wanted = 2 * (group // 2 * slots + slot) + group % 2
     pick = jnp.where(column == wanted, 1.0, 0.0).astype(BF16)
     picked = jnp.dot(pick, stored, preferred_element_type=F32)
@@ -157,31 +182,12 @@
         factors[step, 2] = active * up
 
 
-def prepare_kernel(*refs):
-    grad, *weights = refs[:4]
-    (routes, positions, table, acts, acts_other), (rows_out, factors) = refs[4:9], refs[9:11]
-    held, (grad_at, rows_at, sems) = refs[11:14], refs[14:]
-    copies = [
-        pltpu.make_async_copy(source, target, sems.at[index])
-        for index, (source, target) in enumerate(zip((grad, *weights), (grad_at, *held)))
-    ]
-    for copy in copies:
-        copy.start()
-    act_factors(acts, acts_other, factors, rows_at)
-    copies[0].wait()
-    rows_ahead(grad_at, routes, positions, table, rows_out)
-    for copy in copies[1:]:
-        copy.wait()
-
-
 def expert_rows(rows, rate, factors, step, weights):
-    down, down_other, gate, gate_other, up, up_other = weights
-    features = rows.shape[1]
-    v = jnp.zeros((rows.shape[0], 2 * down.shape[0]), F32)
-    for at in range(0, features, CHUNK):
-        part = slice(at, at + CHUNK)
-        both = jnp.concatenate([down[:, part], down_other[:, part]], axis=0)
-        v = v + lax.dot_general(rows[:, part], both, NT, preferred_element_type=F32)
+    down, gate, up = weights[:2], weights[2:4], weights[4:]
+    v = jnp.concatenate(
+        [lax.dot_general(ref[...], rows, NT, preferred_element_type=F32).T for ref in down],
+        axis=1,
+    )
     scaled = rate * v
     grads = jnp.concatenate(
         [(scaled * factors[step, 0]).astype(BF16), (scaled * factors[step, 1]).astype(BF16)],
@@ -191,17 +197,15 @@
 
     def back(at):
         part = slice(at, at + CHUNK)
-        wide = jnp.concatenate(
-            [gate[part], gate_other[part], up[part], up_other[part]], axis=1
-        )
-        return part, lax.dot_general(grads, wide, NT, preferred_element_type=F32)
-
-    return [functools.partial(back, at) for at in range(0, features, CHUNK)], terms
+        wide = jnp.concatenate([ref[part] for ref in (*gate, *up)], axis=1)
+        return part, lax.dot_general(wide, grads, NT, preferred_element_type=F32).T
+
+    return [functools.partial(back, at) for at in range(0, rows.shape[1], CHUNK)], terms
 
 
 def step_zero_kernel(*refs):
-    got, (factors, ahead), weights = refs[:4], refs[4:6], refs[6:12]
-    rows_out, terms_out, rows_at = refs[12:]
+    got, factors, weights = refs[:4], refs[4], refs[5:11]
+    done, terms_out, rows_at = refs[11:]
     take_rows(rows_at, got)
     features = rows_at.shape[1] - META
     rate = rows_at[:, features:features + 1]
@@ -209,16 +213,15 @@
     terms_out[...] = jnp.broadcast_to(terms, terms_out.shape)
     for back in backs:
         part, value = back()
-        rows_out[:PAIRS, part] = value.astype(BF16)
-    rows_out[:PAIRS, features:] = ahead[:PAIRS, features:]
-    rows_out[PAIRS:] = ahead[PAIRS:]
+        done[:, part] = value.astype(BF16)
 
 
 def merge_kernel(came, *outs):
+    features = outs[0].shape[1] - SPAN
     for k, out in enumerate(outs):
-        first = PAIRS + MOST * (k + 1)
-        out[:PAIRS] = came[:PAIRS]
-        out[PAIRS:] = came[first:first + MOST]
+        first = features + META + SPAN * (k + 1)
+        out[:, :features] = came[:, :features]
+        out[:, features:] = came[:, first:first + SPAN]
 
 
 def split(value):
@@ -230,13 +233,20 @@
 def step_one_kernel(*refs):
     came, (factors, terms0), weights = refs[:4], refs[4:6], refs[6:12]
     outs, ahead_at = refs[12:16], refs[16]
-    features = ahead_at.shape[1] - META
+    features = came[1].shape[1] - SPAN
+    parts = PAIRS // MOST
     for k in range(E_FLY):
-        ahead_at[MOST * k:MOST * (k + 1), :] = came[k][PAIRS:PAIRS + MOST, :].astype(F32)
-    meta = ahead_at[:, features:]
+        first = features + META if k == 0 else features
+        pieces = came[k][:, first:first + SPAN].astype(F32)
+        for spot in range(MOST):
+            at = MOST * k + spot
+            for part in range(parts):
+                row = parts * spot + part
+                ahead_at[at:at + 1, part * SPAN:(part + 1) * SPAN] = pieces[row:row + 1]
+    meta = ahead_at[:, features:features + META]
     rate = meta[:, E_FLY * PAIRS:E_FLY * PAIRS + 1]
     match = meta[:, :E_FLY * PAIRS].astype(BF16)
-    everything = jnp.concatenate([ref[:PAIRS, :features] for ref in came], axis=0)
+    everything = jnp.concatenate([ref[:, :features] for ref in came], axis=0)
     rows = ahead_at[:, :features] + jnp.dot(match, everything, preferred_element_type=F32)
     backs, terms = expert_rows(rows.astype(BF16), rate, factors, 1, weights)
     for back in backs:
@@ -248,32 +258,37 @@
         out[:, features:] = meta[MOST * k:MOST * (k + 1)].astype(BF16)
 
 
-def final_kernel(*refs):
-    shifted, routes, positions = refs[:3]
-    came, got, (out, prob_out, rows_at, back_at) = refs[3:7], refs[7:11], refs[11:]
-    p, z, _ = place()
+def base_kernel(*refs):
+    shifted, came, (out, rows_at) = refs[0], refs[1:5], refs[5:]
     features = out.shape[1]
-    label = labels(PAIRS, lambda k: (z + k) % E_FLY)
     for k in range(E_FLY):
-        rows = came[(E_FLY - k) % E_FLY][MOST * k:MOST * (k + 1), :features]
+        rows = came[k][MOST * k:MOST * (k + 1), :features]
         rows_at[MOST * k:MOST * (k + 1), :] = rows.astype(F32)
-    take_rows(back_at, got)
-    select0 = came[0][:PAIRS, features:]
-    keys = [keys_of(routes, positions, step) for step in range(STEPS)]
-    select1 = one_hot(keys[1], label).astype(BF16)
-    last = p == lax.axis_size("pipe") - 1
+    select = came[0][:, features:features + META]
+    last = lax.axis_index("pipe") == lax.axis_size("pipe") - 1
     for at in range(0, features, CHUNK):
         part = slice(at, at + CHUNK)
-        base = shifted[:, part].astype(F32)
-        base = jnp.where(last, 0.0, base)
+        base = jnp.where(last, 0.0, shifted[:, part].astype(F32))
         base = base + lax.dot_general(
-            select0, rows_at[:, part].astype(BF16), TN, preferred_element_type=F32
-        )
-        base = base.astype(BF16).astype(F32)
-        base = base + lax.dot_general(
-            select1, back_at[:, part].astype(BF16), TN, preferred_element_type=F32
+            select, rows_at[:, part].astype(BF16), TN, preferred_element_type=F32
         )
         out[:, part] = base.astype(BF16)
+
+
+def final_kernel(*refs):
+    base, routes, positions = refs[:3]
+    got, (out, prob_out, back_at) = refs[3:7], refs[7:]
+    _, z, _ = place()
+    features = out.shape[1]
+    label = labels(PAIRS, lambda k: z ^ k)
+    take_rows(back_at, got)
+    keys = [keys_of(routes, positions, step) for step in range(STEPS)]
+    select = one_hot(keys[1], label).astype(BF16)
+    for at in range(0, features, CHUNK):
+        part = slice(at, at + CHUNK)
+        rows = back_at[:, part].astype(BF16)
+        delta = lax.dot_general(select, rows, TN, preferred_element_type=F32)
+        out[:, part] = (base[:, part].astype(F32) + delta).astype(BF16)
     meta = back_at[:, features:]
     for step in range(STEPS):
         first = 3 * (STEPS - 1 - step)
@@ -300,11 +315,12 @@
         return lax.ppermute(block, "expert", [(i, i ^ 1) for i in range(devices)])
 
     def along(block, k):
-        if k % E_FLY == 0:
+        if k == 0:
             return block
-        return lax.ppermute(
-            block, "expert", [(i, (i + 2 * k) % devices) for i in range(devices)]
-        )
+        return lax.ppermute(block, "expert", [(i, i ^ (2 * k)) for i in range(devices)])
+
+    def along_all(blocks):
+        return [along(blocks[k], k) for k in reversed(range(E_FLY))][::-1]
 
     def relay(block, distance):
         route = [(i, (i + distance) % sections) for i in range(sections)]
@@ -312,63 +328,81 @@
 
     pair = jax.ShapeDtypeStruct((MOST, width), BF16)
     block = jax.ShapeDtypeStruct((PAIRS, width), BF16)
-    wide = jax.ShapeDtypeStruct((PAIRS + MOST, width), BF16)
+    wide = jax.ShapeDtypeStruct((PAIRS, features + SPAN), BF16)
+    pieces = PAIRS // MOST * SPAN
     row_scratch = pltpu.VMEM((PAIRS, width), F32)
 
+    own = [w_down[0], w_gate[0], w_up[0]]
     acts_other = across(acts)
-    weights = []
-    for array in (w_down[0], w_gate[0], w_up[0]):
-        weights += [array, across(array)]
-    table = call(
-        table_kernel, "next_table", jax.ShapeDtypeStruct((4, tokens), F32), operands=3
-    )(routes, positions, probs)
+    others = [across(own[0])]
+    small = (routes, positions, probs, grad)
+    *picked, table, down, gate, up = call(
+        pick_kernel,
+        "pick_rows",
+        [pltpu.VMEM(pair.shape, BF16)] * E_FLY
+        + [pltpu.VMEM((4, tokens), F32)]
+        + [pltpu.VMEM(array.shape, BF16) for array in own],
+        [pltpu.VMEM(array.shape, array.dtype) for array in small]
+        + [pltpu.SemaphoreType.DMA((7,))],
+        hbm=7,
+        operands=7,
+        limit=LIMIT,
+    )(*small, *own)
+    *own, picked[0] = lax.optimization_barrier((*own, picked[0]))
+    others += [across(array) for array in own[1:]]
+    others[0], picked[2] = lax.optimization_barrier((others[0], picked[2]))
+    acts_other, picked[1] = lax.optimization_barrier((acts_other, picked[1]))
+    got = along_all(picked)
+    table, others[1] = lax.optimization_barrier((table, others[1]))
     table = relay(table, 1)
-    picked = list(
-        call(pick_kernel, "pick_rows", [pair] * E_FLY, operands=4)(
-            grad, routes, positions, probs
-        )
-    )
-    acts_other, picked[1] = lax.optimization_barrier((acts_other, picked[1]))
-    weights[1], picked[2] = lax.optimization_barrier((weights[1], picked[2]))
-    weights[3], picked[3] = lax.optimization_barrier((weights[3], picked[3]))
-    got = [along(picked[k], k) for k in range(E_FLY)]
-    own = weights[::2]
-    ahead, factors, *own = call(
-        prepare_kernel,
-        "prepare",
-        [pltpu.VMEM((2 * PAIRS, width), BF16), pltpu.VMEM((STEPS, 3, PAIRS, hidden), F32)]
-        + [pltpu.VMEM(array.shape, BF16) for array in own],
-        [
-            pltpu.VMEM(grad.shape, BF16),
-            pltpu.VMEM((2 * acts.shape[0] * acts.shape[1], hidden), F32),
-            pltpu.SemaphoreType.DMA((4,)),
-        ],
-        hbm=4,
-        operands=9,
-        limit=LIMIT,
+    factors = call(
+        factor_kernel,
+        "factors",
+        jax.ShapeDtypeStruct((STEPS, 3, PAIRS, hidden), F32),
+        [pltpu.VMEM((2 * acts.shape[0] * acts.shape[1], hidden), F32)],
+        operands=2,
         cost=COST3,
-    )(grad, *own, routes, positions, table, acts, acts_other)
-    weights[::2] = own
-    rows, terms0 = call(
+    )(acts, acts_other)
+    weights = [array for pair_of in zip((down, gate, up), others) for array in pair_of]
+    done, terms0 = call(
         step_zero_kernel,
         "step_zero",
         [
-            jax.ShapeDtypeStruct((2 * PAIRS, width), BF16),
+            jax.ShapeDtypeStruct((PAIRS, features), BF16),
             jax.ShapeDtypeStruct((PAIRS, META), F32),
         ],
         [row_scratch],
-        operands=12,
+        operands=11,
         cost=COST0,
-    )(*got, factors, ahead, *weights)
+    )(*got, factors, *weights)
+    rows = call(
+        ahead_kernel,
+        "rows_ahead",
+        jax.ShapeDtypeStruct((PAIRS, width + E_FLY * SPAN), BF16),
+        [pltpu.VMEM((PAIRS, pieces), F32), pltpu.VMEM((PAIRS, E_FLY * SPAN), F32)],
+        operands=5,
+    )(grad, routes, positions, table, done)
     came = relay(rows, -1)
     shifted, rows = lax.optimization_barrier((grad, rows))
     shifted = relay(shifted, -1)
     sends = call(merge_kernel, "merge", [wide] * (E_FLY - 1), operands=1, cost=COST2)(came)
     came = [came] + [along(send, k + 1) for k, send in enumerate(sends)]
     back = call(
-        step_one_kernel, "step_one", [pair] * E_FLY, [row_scratch], operands=12, cost=COST1
+        step_one_kernel,
+        "step_one",
+        [pair] * E_FLY,
+        [pltpu.VMEM((PAIRS, pieces), F32)],
+        operands=12,
+        cost=COST1,
     )(*came, factors, terms0, *weights)
-    back = [along(back[k], E_FLY - k) for k in range(E_FLY)]
+    back = along_all(back)
+    base = call(
+        base_kernel,
+        "base_sums",
+        pltpu.VMEM((tokens, features), BF16),
+        [pltpu.VMEM((PAIRS, features), F32)],
+        operands=5,
+    )(shifted, *came)
     result, prob = call(
         final_kernel,
         "final_sums",
@@ -376,9 +410,9 @@
             jax.ShapeDtypeStruct((tokens, features), BF16),
             jax.ShapeDtypeStruct((STEPS, 2, tokens), F32),
         ],
-        [pltpu.VMEM((PAIRS, features), F32), row_scratch],
-        operands=11,
-    )(shifted, routes, positions, *came, *back)
+        [row_scratch],
+        operands=7,
+    )(base, routes, positions, *back)
     return result[None], prob.transpose(0, 2, 1)[None]
 
 

time: 47.4 us -> 44.3 us (0.935)
  waiting for transfers between devices: 16.4 us -> 14.4 us
  local copies, waits for them, and re-layouts: 1.92 us -> 0.03 us
  starting transfers between devices: 18.7 us -> 20.3 us
  Pallas kernels: 9.5 us -> 8.74 us
    ppermute x9, waiting for transfers between devices: 13.1 us -> 6.12 us  [along(): lax.ppermute(block, 'expert', [(i, i ^ 2 * k) for i in range(devices)])]
    ppermute x3, waiting for transfers between devices: 3.25 us -> 7.07 us  [relay(): return lax.ppermute(block, 'pipe', route)]
    ppermute x9, starting transfers between devices: 11.9 us -> 14.6 us  [along(): lax.ppermute(block, 'expert', [(i, i ^ 2 * k) for i in range(devices)])]
    unnamed x12, local copies, waits for them, and re-layouts: 1.92 us -> 0.03 us
    ppermute x4, waiting for transfers between devices: 0.01 us -> 1.21 us  [across(): return lax.ppermute(block, 'expert', [(i, i ^ 1) for i in range(devices)])]
    ppermute x3, starting transfers between devices: 5.61 us -> 4.53 us  [relay(): return lax.ppermute(block, 'pipe', route)]
    pallas_call x5 -> x6, Pallas kernels: 7.79 us -> 7.3 us  [the longest x1 2.34 us: local_chip(): call(pick_kernel, 'pick_rows', [pltpu.VMEM(pair.shape, BF16)] * E_FLY + [...]
  transfers between devices with their start and end apart: 16 -> 16, of which waited for: 7 -> 8; matrix products, arithmetic and copies ran while one was open for 0% -> 0% of each run, Pallas kernels for 11% -> 16%
where the time goes in v3:
time: 44.3 us; the launch traced here: 44.2 us
  starting transfers between devices  20.3 us (46%)
  waiting for transfers between devices  14.4 us (33%)
  Pallas kernels  8.74 us (20%)
  between operations  0.74 us (2%)
    ppermute x9, starting transfers between devices, along(): lax.ppermute(block, 'expert', [(i, i ^ 2 * k) for i in range(devices)])  14.6 us
    ppermute x3, waiting for transfers between devices, relay(): return lax.ppermute(block, 'pipe', route)  7.07 us
    ppermute x9, waiting for transfers between devices, along(): lax.ppermute(block, 'expert', [(i, i ^ 2 * k) for i in range(devices)])  6.12 us
    ppermute x3, starting transfers between devices, relay(): return lax.ppermute(block, 'pipe', route)  4.53 us
    pallas_call x1, Pallas kernels, local_chip(): call(pick_kernel, 'pick_rows', [pltpu.VMEM(pair.shape, BF16)] * E_FLY + [...  2.34 us
    pallas_call x1, Pallas kernels, local_chip(): call(step_one_kernel, 'step_one', [pair] * E_FLY, [pltpu.VMEM((PAIRS, pie...  2.1 us
    pallas_call x1, Pallas kernels, local_chip(): call(step_zero_kernel, 'step_zero', [jax.ShapeDtypeStruct((PAIRS, feature...  1.89 us
    pallas_call x1, Pallas kernels, local_chip(): call(final_kernel, 'final_sums', [jax.ShapeDtypeStruct((tokens, features)...  1.43 us
  transfers between devices with their start and end apart: 16, of which 8 were waited for; matrix products, arithmetic and copies ran while one was open for 0% of the time, Pallas kernels for 16%

profile of v3, /device:TPU:0, one launch (start us, length us, event | category | flops | bytes accessed | tf_op | source)
XLA Modules:
  0.0 44.2 jit_solution(1689905058298929073)
XLA Ops:
  0.6 0.5 %collective-permute-start.4 = (bf16[128,3840]{1,0:T(8,128)(2,1)}, bf16[128,3840]{1,0:T(8,128)(2,1)S(1)}, u32[]{:S(2)}, u32[]{:S(2)}) collective-permute-start(bf16[128,3840]{1,0:T(8,128)(2,1)} %bitcast.29), channel_id=1, source_target_pairs={{0,1},{1,0},{2,3},{3,2},{4,5},{5,4},{6,7},{7,6},{8,9},{9,8},{10,11... | collective-permute-start | bytes 2949128 | tf_op jit(solution)/shard_map/ppermute | solution.py:315
  1.1 0.1 collective-permute-start.2
  1.2 0.0 copy-start.4
  1.2 0.0 copy-start.5
  1.2 0.0 copy-start.3
  1.2 2.3 %pick_rows.1 = (bf16[2,3968]{1,0:T(2,128)(2,1)S(1)}, bf16[2,3968]{1,0:T(2,128)(2,1)S(1)}, bf16[2,3968]{1,0:T(2,128)(2,1)S(1)}, bf16[2,3968]{1,0:T(2,128)(2,1)S(1...) custom-call(s32[2,2,128]{2,1,0:T(2,128)} %bitcast.21, ...), custom_call_target="tpu_custom_call" | custom-call | tf_op jit(solution)/shard_map/pick_rows/pallas_call | solution.py:339
  3.6 5.1 %collective-permute-start.6 = (bf16[2,3968]{1,0:T(2,128)(2,1)S(1)}, bf16[2,3968]{1,0:T(2,128)(2,1)S(1)}, u32[]{:S(2)}, u32[]{:S(2)}) collective-permute-start(bf16[2,3968]{1,0:T(2,128)(2,1)S(1)} %get-tuple-element.40), channel_id=1, source_target_pairs={{0,6},{1,7},{2,4},{3,5},{4,2},{5,3},{6,0},{7,1},{8,14},{9,15},{10,... | collective-permute-start | bytes 47624 | tf_op jit(solution)/shard_map/ppermute | solution.py:320
  8.7 0.0 copy-done.4
  8.7 0.0 collective-permute-start
  8.7 0.0 copy-done.5
  8.7 0.5 %collective-permute-start.7 = (bf16[3840,128]{1,0:T(8,128)(2,1)S(1)}, bf16[3840,128]{1,0:T(8,128)(2,1)S(1)}, u32[]{:S(2)}, u32[]{:S(2)}) collective-permute-start(bf16[3840,128]{1,0:T(8,128)(2,1)S(1)} %bitcast.34), channel_id=1, source_target_pairs={{0,1},{1,0},{2,3},{3,2},{4,5},{5,4},{6,7},{7,6},{8,9},{9,8},{10,11... | collective-permute-start | bytes 2949128 | tf_op jit(solution)/shard_map/ppermute | solution.py:315
  9.2 0.0 collective-permute-done.2.acts_other
  9.2 0.0 collective-permute-start.3
  9.2 0.0 collective-permute-done.4.refs_6_.refs_7_
  9.2 0.6 %collective-permute-start.5 = (bf16[2,3968]{1,0:T(2,128)(2,1)S(1)}, bf16[2,3968]{1,0:T(2,128)(2,1)S(1)}, u32[]{:S(2)}, u32[]{:S(2)}) collective-permute-start(bf16[2,3968]{1,0:T(2,128)(2,1)S(1)} %get-tuple-element.39), channel_id=1, source_target_pairs={{0,4},{1,5},{2,6},{3,7},{4,0},{5,1},{6,2},{7,3},{8,12},{9,13},{10,... | collective-permute-start | bytes 47624 | tf_op jit(solution)/shard_map/ppermute | solution.py:320
  9.8 0.0 copy-done.3
  9.8 0.2 factors.1.refs_4_
  10.0 1.2 %collective-permute-done.refs_8_.refs_9_ = bf16[3840,128]{1,0:T(8,128)(2,1)S(1)} collective-permute-done((bf16[3840,128]{1,0:T(8,128)(2,1)S(1)}, bf16[3840,128]{1,0:T(8,128)(2,1)S(1)}, u32[]{:S(2)}, u32[]{:S(2)}) %collective-permute-start) | collective-permute-done | bytes 983072 | tf_op jit(solution)/shard_map/ppermute | solution.py:315
  11.2 1.5 %collective-permute-start.1 = (f32[4,128]{1,0:T(4,128)S(1)}, f32[4,128]{1,0:T(4,128)S(1)}, u32[]{:S(2)}, u32[]{:S(2)}) collective-permute-start(f32[4,128]{1,0:T(4,128)S(1)} %get-tuple-element.34), channel_id=1, source_target_pairs={{0,8},{8,16},{16,24},{24,0},{1,9},{9,17},{17,25},{25,1},{2,10},{10... | collective-permute-start | bytes 6152 | tf_op jit(solution)/shard_map/ppermute | solution.py:327
  12.7 0.0 collective-permute-done.6.refs_3_
  12.7 0.2 collective-permute-done.3.refs_1_
  12.9 0.0 collective-permute-done.7.refs_10_.refs_11_
  12.9 1.0 %collective-permute-done.5.refs_2_ = bf16[2,3968]{1,0:T(2,128)(2,1)S(1)} collective-permute-done((bf16[2,3968]{1,0:T(2,128)(2,1)S(1)}, bf16[2,3968]{1,0:T(2,128)(2,1)S(1)}, u32[]{:S(2)}, u32[]{:S(2)}) %collective-permute-start.5) | collective-permute-done | bytes 15904 | tf_op jit(solution)/shard_map/ppermute | solution.py:320
  13.9 1.9 %step_zero.1 = (bf16[8,3840]{1,0:T(8,128)(2,1)S(1)}, f32[8,128]{1,0:T(8,128)S(1)}) custom-call(bf16[2,3968]{1,0:T(2,128)(2,1)S(1)} %get-tuple-element.35.refs_0_, bf16[2,3968]{1,0:T(2,128)(2,1)S(1)} %collective-permute-done.3.refs_1_, bf16[2,3968]{1,0:T(2,128)(2,1)S(1)} %collective-permute-done.5.refs_2_, ...), custom_call_target="tpu_custom_call" | custom-call | flops 20000000000 | tf_op jit(solution)/shard_map/step_zero/pallas_call | solution.py:367
  15.8 0.0 collective-permute-done.1.table
  15.8 0.0 copy-done
  15.8 0.0 copy-done.1
  15.8 0.0 copy-done.2
  15.8 0.3 rows_ahead.1
  16.2 2.5 %collective-permute-start.9 = (bf16[8,8064]{1,0:T(8,128)(2,1)S(1)}, bf16[8,8064]{1,0:T(8,128)(2,1)S(1)}, u32[]{:S(2)}, u32[]{:S(2)}) collective-permute-start(bf16[8,8064]{1,0:T(8,128)(2,1)S(1)} %rows_ahead.1), channel_id=1, source_target_pairs={{0,24},{8,0},{16,8},{24,16},{1,25},{9,1},{17,9},{25,17},{2,26},{10... | collective-permute-start | bytes 387080 | tf_op jit(solution)/shard_map/ppermute | solution.py:327
  18.7 0.5 %collective-permute-start.8 = (bf16[128,3840]{1,0:T(8,128)(2,1)S(1)}, bf16[128,3840]{1,0:T(8,128)(2,1)S(1)}, u32[]{:S(2)}, u32[]{:S(2)}) collective-permute-start(bf16[128,3840]{1,0:T(8,128)(2,1)S(1)} %bitcast.20), channel_id=1, source_target_pairs={{0,24},{8,0},{16,8},{24,16},{1,25},{9,1},{17,9},{25,17},{2,26},{10... | collective-permute-start | bytes 2949128 | tf_op jit(solution)/shard_map/ppermute | solution.py:327
  19.2 3.4 %collective-permute-done.9.came.refs_1_.refs_0_ = bf16[8,8064]{1,0:T(8,128)(2,1)S(1)} collective-permute-done((bf16[8,8064]{1,0:T(8,128)(2,1)S(1)}, bf16[8,8064]{1,0:T(8,128)(2,1)S(1)}, u32[]{:S(2)}, u32[]{:S(2)}) %collective-permute-start.9) | collective-permute-done | bytes 129056 | tf_op jit(solution)/shard_map/ppermute | solution.py:327
  22.6 2.0 %collective-permute-start.10 = (bf16[8,4864]{1,0:T(8,128)(2,1)S(1)}, bf16[8,4864]{1,0:T(8,128)(2,1)S(1)}, u32[]{:S(2)}, u32[]{:S(2)}) collective-permute-start(bf16[8,4864]{1,0:T(8,128)(2,1)S(1)} %get-tuple-element.50), channel_id=1, source_target_pairs={{0,2},{1,3},{2,0},{3,1},{4,6},{5,7},{6,4},{7,5},{8,10},{9,11},{10,... | collective-permute-start | bytes 233480 | tf_op jit(solution)/shard_map/ppermute | solution.py:320
  24.6 1.0 %collective-permute-start.11 = (bf16[8,4864]{1,0:T(8,128)(2,1)S(1)}, bf16[8,4864]{1,0:T(8,128)(2,1)S(1)}, u32[]{:S(2)}, u32[]{:S(2)}) collective-permute-start(bf16[8,4864]{1,0:T(8,128)(2,1)S(1)} %get-tuple-element.51), channel_id=1, source_target_pairs={{0,4},{1,5},{2,6},{3,7},{4,0},{5,1},{6,2},{7,3},{8,12},{9,13},{10,... | collective-permute-start | bytes 233480 | tf_op jit(solution)/shard_map/ppermute | solution.py:320
  25.7 1.4 %collective-permute-start.12 = (bf16[8,4864]{1,0:T(8,128)(2,1)S(1)}, bf16[8,4864]{1,0:T(8,128)(2,1)S(1)}, u32[]{:S(2)}, u32[]{:S(2)}) collective-permute-start(bf16[8,4864]{1,0:T(8,128)(2,1)S(1)} %get-tuple-element.52), channel_id=1, source_target_pairs={{0,6},{1,7},{2,4},{3,5},{4,2},{5,3},{6,0},{7,1},{8,14},{9,15},{10,... | collective-permute-start | bytes 233480 | tf_op jit(solution)/shard_map/ppermute | solution.py:320
  27.1 0.4 collective-permute-done.10.refs_2_.refs_1_
  27.4 2.8 %collective-permute-done.11.refs_3_.refs_2_ = bf16[8,4864]{1,0:T(8,128)(2,1)S(1)} collective-permute-done((bf16[8,4864]{1,0:T(8,128)(2,1)S(1)}, bf16[8,4864]{1,0:T(8,128)(2,1)S(1)}, u32[]{:S(2)}, u32[]{:S(2)}) %collective-permute-start.11) | collective-permute-done | bytes 77856 | tf_op jit(solution)/shard_map/ppermute | solution.py:320
  30.3 1.7 %collective-permute-done.12.refs_4_.refs_3_ = bf16[8,4864]{1,0:T(8,128)(2,1)S(1)} collective-permute-done((bf16[8,4864]{1,0:T(8,128)(2,1)S(1)}, bf16[8,4864]{1,0:T(8,128)(2,1)S(1)}, u32[]{:S(2)}, u32[]{:S(2)}) %collective-permute-start.12) | collective-permute-done | bytes 77856 | tf_op jit(solution)/shard_map/ppermute | solution.py:320
  32.0 2.1 %step_one.1 = (bf16[2,3968]{1,0:T(2,128)(2,1)S(1)}, bf16[2,3968]{1,0:T(2,128)(2,1)S(1)}, bf16[2,3968]{1,0:T(2,128)(2,1)S(1)}, bf16[2,3968]{1,0:T(2,128)(2,1)S(1)}) custom-call(bf16[8,8064]{1,0:T(8,128)(2,1)S(1)} %collective-permute-done.9.came.refs_1_.refs_0_, bf16[8,4864]{1,0:T(8,128)(2,1)S(1)} %collective-permute-done.10.refs_2_.refs_1_, ...), custom_call_target="tpu_custom_call" | custom-call | tf_op jit(solution)/shard_map/step_one/pallas_call | solution.py:390
  34.1 0.0 collective-permute-start.13
  34.2 1.9 %collective-permute-start.14 = (bf16[2,3968]{1,0:T(2,128)(2,1)S(1)}, bf16[2,3968]{1,0:T(2,128)(2,1)S(1)}, u32[]{:S(2)}, u32[]{:S(2)}) collective-permute-start(bf16[2,3968]{1,0:T(2,128)(2,1)S(1)} %get-tuple-element.56), channel_id=1, source_target_pairs={{0,4},{1,5},{2,6},{3,7},{4,0},{5,1},{6,2},{7,3},{8,12},{9,13},{10,... | collective-permute-start | bytes 47624 | tf_op jit(solution)/shard_map/ppermute | solution.py:320
  36.1 2.5 %collective-permute-start.15 = (bf16[2,3968]{1,0:T(2,128)(2,1)S(1)}, bf16[2,3968]{1,0:T(2,128)(2,1)S(1)}, u32[]{:S(2)}, u32[]{:S(2)}) collective-permute-start(bf16[2,3968]{1,0:T(2,128)(2,1)S(1)} %get-tuple-element.57), channel_id=1, source_target_pairs={{0,6},{1,7},{2,4},{3,5},{4,2},{5,3},{6,0},{7,1},{8,14},{9,15},{10,... | collective-permute-start | bytes 47624 | tf_op jit(solution)/shard_map/ppermute | solution.py:320
  38.6 3.7 %collective-permute-done.8.refs_0_ = bf16[128,3840]{1,0:T(8,128)(2,1)S(1)} collective-permute-done((bf16[128,3840]{1,0:T(8,128)(2,1)S(1)}, bf16[128,3840]{1,0:T(8,128)(2,1)S(1)}, u32[]{:S(2)}, u32[]{:S(2)}) %collective-permute-start.8) | collective-permute-done | bytes 983072 | tf_op jit(solution)/shard_map/ppermute | solution.py:327
  42.2 0.4 %base_sums.1.refs_0_ = bf16[128,3840]{1,0:T(8,128)(2,1)S(1)} custom-call(bf16[128,3840]{1,0:T(8,128)(2,1)S(1)} %collective-permute-done.8.refs_0_, bf16[8,8064]{1,0:T(8,128)(2,1)S(1)} %collective-permute-done.9.came.refs_1_.refs_0_, bf16[8,4864]{1,0:T(8,128)(2,1)S(1)} %collective-permute-done.10.refs_2_.refs_1_, ...), custom_call_target="tpu_custom_call" | custom-call | tf_op jit(solution)/shard_map/base_sums/pallas_call | solution.py:399
  42.7 0.0 collective-permute-done.13.refs_4_
  42.7 0.0 collective-permute-done.14.refs_5_
  42.7 0.0 collective-permute-done.15.refs_6_
  42.7 1.4 %final_sums.1 = (bf16[128,3840]{1,0:T(8,128)(2,1)}, f32[2,2,128]{2,1,0:T(2,128)}) custom-call(bf16[128,3840]{1,0:T(8,128)(2,1)S(1)} %base_sums.1.refs_0_, s32[2,2,128]{2,1,0:T(2,128)S(1)} %bitcast.23, s32[2,2,128]{2,1,0:T(2,128)S(1)} %bitcast.26, bf16[2,3968]{1,0:T(2,128)(2,1)S(1)} %get-tuple-element.54.refs_3_, ...), custom_call_target="tpu_custom_call" | custom-call | tf_op jit(solution)/shard_map/final_sums/pallas_call | solution.py:406
  (4 shorter events, 0.0 us)
Async XLA Ops:
  0.6 8.6 %collective-permute-start.4 = (bf16[128,3840]{1,0:T(8,128)(2,1)}, bf16[128,3840]{1,0:T(8,128)(2,1)S(1)}, u32[]{:S(2)}, u32[]{:S(2)}) collective-permute-start(bf16[128,3840]{1,0:T(8,128)(2,1)} %bitcast.29), channel_id=1, source_target_pairs={{0,1},{1,0},{2,3},{3,2},{4,5},{5,4},{6,7},{7,6},{8,9},{9,8},{10,11... | collective-permute-start | bytes 2949128 | tf_op jit(solution)/shard_map/ppermute | solution.py:315
  1.1 8.0 %collective-permute-start.2 = (bf16[2,16,2,128]{3,2,1,0:T(2,128)(2,1)}, bf16[2,16,2,128]{3,2,1,0:T(2,128)(2,1)S(1)}, u32[]{:S(2)}, u32[]{:S(2)}) collective-permute-start(bf16[2,16,2,128]{3,2,1,0:T(2,128)(2,1)} %bitcast.27), channel_id=1, source_target_pairs={{0,1},{1,0},{2,3},{3,2},{4,5},{5,4},{6,7},{7,6},{8,9},{9,8},{10,11... | collective-permute-start | bytes 49160 | tf_op jit(solution)/shard_map/ppermute | solution.py:315
  1.2 7.4 %copy-start.4 = (bf16[1,3840,128]{2,1,0:T(8,128)(2,1)S(1)}, bf16[1,3840,128]{2,1,0:T(8,128)(2,1)}, u32[]{:S(2)}) copy-start(bf16[1,3840,128]{2,1,0:T(8,128)(2,1)} %param.13) | copy-start | bytes 2949124
  1.2 7.5 %copy-start.5 = (bf16[1,3840,128]{2,1,0:T(8,128)(2,1)S(1)}, bf16[1,3840,128]{2,1,0:T(8,128)(2,1)}, u32[]{:S(2)}) copy-start(bf16[1,3840,128]{2,1,0:T(8,128)(2,1)} %param.14) | copy-start | bytes 2949124
  1.2 8.6 %copy-start.3 = (bf16[1,2,16,2,128]{4,3,2,1,0:T(2,128)(2,1)S(1)}, bf16[1,2,16,2,128]{4,3,2,1,0:T(2,128)(2,1)}, u32[]{:S(2)}) copy-start(bf16[1,2,16,2,128]{4,3,2,1,0:T(2,128)(2,1)} %param.12) | copy-start | bytes 49156
  3.6 9.2 %collective-permute-start.6 = (bf16[2,3968]{1,0:T(2,128)(2,1)S(1)}, bf16[2,3968]{1,0:T(2,128)(2,1)S(1)}, u32[]{:S(2)}, u32[]{:S(2)}) collective-permute-start(bf16[2,3968]{1,0:T(2,128)(2,1)S(1)} %get-tuple-element.40), channel_id=1, source_target_pairs={{0,6},{1,7},{2,4},{3,5},{4,2},{5,3},{6,0},{7,1},{8,14},{9,15},{10,... | collective-permute-start | bytes 47624 | tf_op jit(solution)/shard_map/ppermute | solution.py:320
  8.7 2.6 %collective-permute-start = (bf16[3840,128]{1,0:T(8,128)(2,1)S(1)}, bf16[3840,128]{1,0:T(8,128)(2,1)S(1)}, u32[]{:S(2)}, u32[]{:S(2)}) collective-permute-start(bf16[3840,128]{1,0:T(8,128)(2,1)S(1)} %bitcast.32), channel_id=1, source_target_pairs={{0,1},{1,0},{2,3},{3,2},{4,5},{5,4},{6,7},{7,6},{8,9},{9,8},{10,11... | collective-permute-start | bytes 2949128 | tf_op jit(solution)/shard_map/ppermute | solution.py:315
  8.7 4.3 %collective-permute-start.7 = (bf16[3840,128]{1,0:T(8,128)(2,1)S(1)}, bf16[3840,128]{1,0:T(8,128)(2,1)S(1)}, u32[]{:S(2)}, u32[]{:S(2)}) collective-permute-start(bf16[3840,128]{1,0:T(8,128)(2,1)S(1)} %bitcast.34), channel_id=1, source_target_pairs={{0,1},{1,0},{2,3},{3,2},{4,5},{5,4},{6,7},{7,6},{8,9},{9,8},{10,11... | collective-permute-start | bytes 2949128 | tf_op jit(solution)/shard_map/ppermute | solution.py:315
  9.2 3.7 %collective-permute-start.3 = (bf16[2,3968]{1,0:T(2,128)(2,1)S(1)}, bf16[2,3968]{1,0:T(2,128)(2,1)S(1)}, u32[]{:S(2)}, u32[]{:S(2)}) collective-permute-start(bf16[2,3968]{1,0:T(2,128)(2,1)S(1)} %get-tuple-element.37), channel_id=1, source_target_pairs={{0,2},{1,3},{2,0},{3,1},{4,6},{5,7},{6,4},{7,5},{8,10},{9,11},{10,... | collective-permute-start | bytes 47624 | tf_op jit(solution)/shard_map/ppermute | solution.py:320
  9.2 4.7 %collective-permute-start.5 = (bf16[2,3968]{1,0:T(2,128)(2,1)S(1)}, bf16[2,3968]{1,0:T(2,128)(2,1)S(1)}, u32[]{:S(2)}, u32[]{:S(2)}) collective-permute-start(bf16[2,3968]{1,0:T(2,128)(2,1)S(1)} %get-tuple-element.39), channel_id=1, source_target_pairs={{0,4},{1,5},{2,6},{3,7},{4,0},{5,1},{6,2},{7,3},{8,12},{9,13},{10,... | collective-permute-start | bytes 47624 | tf_op jit(solution)/shard_map/ppermute | solution.py:320
  11.2 4.6 %collective-permute-start.1 = (f32[4,128]{1,0:T(4,128)S(1)}, f32[4,128]{1,0:T(4,128)S(1)}, u32[]{:S(2)}, u32[]{:S(2)}) collective-permute-start(f32[4,128]{1,0:T(4,128)S(1)} %get-tuple-element.34), channel_id=1, source_target_pairs={{0,8},{8,16},{16,24},{24,0},{1,9},{9,17},{17,25},{25,1},{2,10},{10... | collective-permute-start | bytes 6152 | tf_op jit(solution)/shard_map/ppermute | solution.py:327
  13.9 1.9 %copy-start = (bf16[1,128,3840]{2,1,0:T(8,128)(2,1)S(1)}, bf16[1,128,3840]{2,1,0:T(8,128)(2,1)}, u32[]{:S(2)}) copy-start(bf16[1,128,3840]{2,1,0:T(8,128)(2,1)} %param.8) | copy-start | bytes 2949124
  13.9 1.9 %copy-start.1 = (s32[1,2,128,2]{2,3,1,0:T(2,128)S(1)}, s32[1,2,128,2]{2,3,1,0:T(2,128)}, u32[]{:S(2)}) copy-start(s32[1,2,128,2]{2,3,1,0:T(2,128)} %param.9) | copy-start | bytes 6148
  13.9 1.9 %copy-start.2 = (s32[1,2,128,2]{2,3,1,0:T(2,128)S(1)}, s32[1,2,128,2]{2,3,1,0:T(2,128)}, u32[]{:S(2)}) copy-start(s32[1,2,128,2]{2,3,1,0:T(2,128)} %param.10) | copy-start | bytes 6148
  16.2 6.4 %collective-permute-start.9 = (bf16[8,8064]{1,0:T(8,128)(2,1)S(1)}, bf16[8,8064]{1,0:T(8,128)(2,1)S(1)}, u32[]{:S(2)}, u32[]{:S(2)}) collective-permute-start(bf16[8,8064]{1,0:T(8,128)(2,1)S(1)} %rows_ahead.1), channel_id=1, source_target_pairs={{0,24},{8,0},{16,8},{24,16},{1,25},{9,1},{17,9},{25,17},{2,26},{10... | collective-permute-start | bytes 387080 | tf_op jit(solution)/shard_map/ppermute | solution.py:327
  18.7 23.6 %collective-permute-start.8 = (bf16[128,3840]{1,0:T(8,128)(2,1)S(1)}, bf16[128,3840]{1,0:T(8,128)(2,1)S(1)}, u32[]{:S(2)}, u32[]{:S(2)}) collective-permute-start(bf16[128,3840]{1,0:T(8,128)(2,1)S(1)} %bitcast.20), channel_id=1, source_target_pairs={{0,24},{8,0},{16,8},{24,16},{1,25},{9,1},{17,9},{25,17},{2,26},{10... | collective-permute-start | bytes 2949128 | tf_op jit(solution)/shard_map/ppermute | solution.py:327
  22.6 4.8 %collective-permute-start.10 = (bf16[8,4864]{1,0:T(8,128)(2,1)S(1)}, bf16[8,4864]{1,0:T(8,128)(2,1)S(1)}, u32[]{:S(2)}, u32[]{:S(2)}) collective-permute-start(bf16[8,4864]{1,0:T(8,128)(2,1)S(1)} %get-tuple-element.50), channel_id=1, source_target_pairs={{0,2},{1,3},{2,0},{3,1},{4,6},{5,7},{6,4},{7,5},{8,10},{9,11},{10,... | collective-permute-start | bytes 233480 | tf_op jit(solution)/shard_map/ppermute | solution.py:320
  24.6 5.6 %collective-permute-start.11 = (bf16[8,4864]{1,0:T(8,128)(2,1)S(1)}, bf16[8,4864]{1,0:T(8,128)(2,1)S(1)}, u32[]{:S(2)}, u32[]{:S(2)}) collective-permute-start(bf16[8,4864]{1,0:T(8,128)(2,1)S(1)} %get-tuple-element.51), channel_id=1, source_target_pairs={{0,4},{1,5},{2,6},{3,7},{4,0},{5,1},{6,2},{7,3},{8,12},{9,13},{10,... | collective-permute-start | bytes 233480 | tf_op jit(solution)/shard_map/ppermute | solution.py:320
  25.7 6.4 %collective-permute-start.12 = (bf16[8,4864]{1,0:T(8,128)(2,1)S(1)}, bf16[8,4864]{1,0:T(8,128)(2,1)S(1)}, u32[]{:S(2)}, u32[]{:S(2)}) collective-permute-start(bf16[8,4864]{1,0:T(8,128)(2,1)S(1)} %get-tuple-element.52), channel_id=1, source_target_pairs={{0,6},{1,7},{2,4},{3,5},{4,2},{5,3},{6,0},{7,1},{8,14},{9,15},{10,... | collective-permute-start | bytes 233480 | tf_op jit(solution)/shard_map/ppermute | solution.py:320
  34.1 8.6 %collective-permute-start.13 = (bf16[2,3968]{1,0:T(2,128)(2,1)S(1)}, bf16[2,3968]{1,0:T(2,128)(2,1)S(1)}, u32[]{:S(2)}, u32[]{:S(2)}) collective-permute-start(bf16[2,3968]{1,0:T(2,128)(2,1)S(1)} %get-tuple-element.55), channel_id=1, source_target_pairs={{0,2},{1,3},{2,0},{3,1},{4,6},{5,7},{6,4},{7,5},{8,10},{9,11},{10,... | collective-permute-start | bytes 47624 | tf_op jit(solution)/shard_map/ppermute | solution.py:320
  34.2 8.5 %collective-permute-start.14 = (bf16[2,3968]{1,0:T(2,128)(2,1)S(1)}, bf16[2,3968]{1,0:T(2,128)(2,1)S(1)}, u32[]{:S(2)}, u32[]{:S(2)}) collective-permute-start(bf16[2,3968]{1,0:T(2,128)(2,1)S(1)} %get-tuple-element.56), channel_id=1, source_target_pairs={{0,4},{1,5},{2,6},{3,7},{4,0},{5,1},{6,2},{7,3},{8,12},{9,13},{10,... | collective-permute-start | bytes 47624 | tf_op jit(solution)/shard_map/ppermute | solution.py:320
  36.1 6.6 %collective-permute-start.15 = (bf16[2,3968]{1,0:T(2,128)(2,1)S(1)}, bf16[2,3968]{1,0:T(2,128)(2,1)S(1)}, u32[]{:S(2)}, u32[]{:S(2)}) collective-permute-start(bf16[2,3968]{1,0:T(2,128)(2,1)S(1)} %get-tuple-element.57), channel_id=1, source_target_pairs={{0,6},{1,7},{2,4},{3,5},{4,2},{5,3},{6,0},{7,1},{8,14},{9,15},{10,... | collective-permute-start | bytes 47624 | tf_op jit(solution)/shard_map/ppermute | solution.py:320

commit v4 on v3

--- a/solution.py
+++ b/solution.py
@@ -14,11 +14,13 @@
 META = 128
 CHUNK = 256
 SPAN = 1024
-COST0 = 20_000_000_000
+COST0 = 20000000000
 COST1 = 0
-COST2 = 20_000_000_000
-COST3 = 20_000_000_000
+COST2 = 20000000000
+COST4 = 0
+COST3 = 20000000000
 LIMIT = 54
+EARLY = 24
 F32 = jnp.float32
 BF16 = jnp.bfloat16
 NT = (((1,), (1,)), ((), ()))
@@ -76,6 +78,11 @@
     return out
 
 
+def picked_rows(select, early, late):
+    grad = jnp.concatenate([early[...], late[...]], axis=0)
+    return jnp.dot(select.astype(BF16), grad, preferred_element_type=F32)
+
+
 def bring(sources, targets, sems):
     copies = [
         pltpu.make_async_copy(source, target, sems.at[index])
@@ -99,9 +106,12 @@
 
 
 def pick_kernel(*refs):
-    outs, (table, *weights), held, sems = refs[7:11], refs[11:15], refs[15:19], refs[19]
-    copies = bring(refs[:7], (*held, *weights), sems)
-    routes, positions, probs, grad = held
+    grad, *small = refs[:4]
+    outs, (table, early, late), held, sems = refs[4:8], refs[8:11], refs[11:14], refs[14]
+    first = early.shape[0]
+    parts = (grad.at[pl.ds(0, first)], grad.at[pl.ds(first, late.shape[0])])
+    copies = bring((*small, *parts), (*held, early, late), sems)
+    routes, positions, probs = held
     for copy in copies[:3]:
         copy.wait()
     _, z, _ = place()
@@ -111,22 +121,23 @@
     rate = rates_of(keys, probs[0].astype(F32), label)
     table[0:2] = keys_of(routes, positions, 1).astype(F32)
     table[2:4] = probs[1].astype(F32)
-    copies[3].wait()
-    rows = jnp.dot(select.astype(BF16), grad[...], preferred_element_type=F32)
+    table[4:6] = keys.astype(F32)
+    table[6:8] = jnp.zeros_like(table[6:8])
+    for copy in copies[3:5]:
+        copy.wait()
+    rows = picked_rows(select, early, late)
     put_rows(outs, rows, first_lanes([rate]))
-    for copy in copies[4:]:
-        copy.wait()
-
-
-def ahead_kernel(grad, routes, positions, table, done, rows_out, held, packed):
+
+
+def rows_ahead(early, late, table, came_table, rows_out, held, packed):
     p, z, c = place()
-    keys0 = keys_of(routes, positions, 0)
-    keys1 = table[0:2].astype(jnp.int32)
+    keys0 = table[4:6].astype(jnp.int32)
+    keys1 = came_table[0:2].astype(jnp.int32)
     keys1 = jnp.where(p == 0, -1, keys1)
     label = labels(PAIRS, lambda k: z ^ k)
     select = one_hot(keys1, label)
-    rows = jnp.dot(select.astype(BF16), grad[...], preferred_element_type=F32)
-    rate = rates_of(keys1, table[2:4], label)
+    rows = picked_rows(select, early, late)
+    rate = rates_of(keys1, came_table[2:4], label)
     lane = lax.broadcasted_iota(jnp.int32, (PAIRS, META), 1)
     meta = jnp.where(lane == E_FLY * PAIRS, rate, 0.0)
     column = lax.broadcasted_iota(jnp.int32, (META, 1), 0)
@@ -142,9 +153,8 @@
         meta = meta + jnp.where(row // MOST == k, match, 0.0)
     features = rows.shape[1]
     width = features + META
-    rows_out[:, :features] = done[...]
     taken = one_hot(jnp.where(p == 0, -1, keys0), label)
-    rows_out[:, features:width] = taken.astype(BF16)
+    rows_out[:, :META] = taken.astype(BF16)
     held[:, :features] = rows
     held[:, features:width] = meta
     parts = PAIRS // MOST
@@ -153,10 +163,10 @@
         for part in range(parts):
             piece = held[at:at + 1, part * SPAN:(part + 1) * SPAN]
             packed[parts * spot + part:parts * spot + part + 1, k * SPAN:(k + 1) * SPAN] = piece
-    rows_out[:, width:] = packed[...].astype(BF16)
-
-
-def factor_kernel(acts, acts_other, factors, rows_at):
+    rows_out[:, META:] = packed[...].astype(BF16)
+
+
+def act_factors(acts, acts_other, factors, rows_at):
     _, z, c = place()
     steps, slots, _, width = acts.shape
     for half, ref in enumerate((acts, acts_other)):
@@ -168,7 +178,7 @@
     row = lax.broadcasted_iota(jnp.int32, (2 * steps * PAIRS, 2 * steps * slots), 0)
     column = lax.broadcasted_iota(jnp.int32, row.shape, 1)
     group, k, spot = row // PAIRS, row // MOST % E_FLY, row % MOST
-    slot = (2 * (z ^ k) + c) * MOST + spot
+    slot = (2 * (z ^ k) + (c ^ (group // 2))) * MOST + spot
     wanted = 2 * (group // 2 * slots + slot) + group % 2
     pick = jnp.where(column == wanted, 1.0, 0.0).astype(BF16)
     picked = jnp.dot(pick, stored, preferred_element_type=F32)
@@ -182,6 +192,12 @@
         factors[step, 2] = active * up
 
 
+def prepare_kernel(*refs):
+    ahead, acts, (rows_out, factors, held, packed, acts_at) = refs[:4], refs[4:6], refs[6:]
+    act_factors(*acts, factors, acts_at)
+    rows_ahead(*ahead, rows_out, held, packed)
+
+
 def expert_rows(rows, rate, factors, step, weights):
     down, gate, up = weights[:2], weights[2:4], weights[4:]
     v = jnp.concatenate(
@@ -204,16 +220,17 @@
 
 
 def step_zero_kernel(*refs):
-    got, factors, weights = refs[:4], refs[4], refs[5:11]
-    done, terms_out, rows_at = refs[11:]
+    got, (ahead, factors), weights = refs[:4], refs[4:6], refs[6:12]
+    rows_out, terms_out, rows_at = refs[12:]
     take_rows(rows_at, got)
     features = rows_at.shape[1] - META
     rate = rows_at[:, features:features + 1]
     backs, terms = expert_rows(rows_at[:, :features].astype(BF16), rate, factors, 0, weights)
     terms_out[...] = jnp.broadcast_to(terms, terms_out.shape)
+    rows_out[:, features:] = ahead[...]
     for back in backs:
         part, value = back()
-        done[:, part] = value.astype(BF16)
+        rows_out[:, part] = value.astype(BF16)
 
 
 def merge_kernel(came, *outs):
@@ -232,7 +249,7 @@
 
 def step_one_kernel(*refs):
     came, (factors, terms0), weights = refs[:4], refs[4:6], refs[6:12]
-    outs, ahead_at = refs[12:16], refs[16]
+    outs, home, ahead_at, back_at = refs[12:15], *refs[15:]
     features = came[1].shape[1] - SPAN
     parts = PAIRS // MOST
     for k in range(E_FLY):
@@ -249,40 +266,44 @@
     everything = jnp.concatenate([ref[:, :features] for ref in came], axis=0)
     rows = ahead_at[:, :features] + jnp.dot(match, everything, preferred_element_type=F32)
     backs, terms = expert_rows(rows.astype(BF16), rate, factors, 1, weights)
+    for k in range(E_FLY):
+        own = came[k][MOST * k:MOST * (k + 1), :features]
+        back_at[MOST * k:MOST * (k + 1), :features] = own.astype(F32)
+    back_at[:PAIRS, features:] = came[0][:, features:features + META].astype(F32)
     for back in backs:
         part, value = back()
+        back_at[PAIRS:, part] = value
         for k, out in enumerate(outs):
-            out[:, part] = value[MOST * k:MOST * (k + 1)].astype(BF16)
+            out[:, part] = value[MOST * (k + 1):MOST * (k + 2)].astype(BF16)
     meta = first_lanes(split(terms) + split(terms0[:, 0:1]))
+    back_at[PAIRS:, features:] = meta
     for k, out in enumerate(outs):
-        out[:, features:] = meta[MOST * k:MOST * (k + 1)].astype(BF16)
+        out[:, features:] = meta[MOST * (k + 1):MOST * (k + 2)].astype(BF16)
+    home[...] = back_at[...].astype(BF16)
 
 
 def base_kernel(*refs):
-    shifted, came, (out, rows_at) = refs[0], refs[1:5], refs[5:]
+    early, late, home, out = refs
     features = out.shape[1]
-    for k in range(E_FLY):
-        rows = came[k][MOST * k:MOST * (k + 1), :features]
-        rows_at[MOST * k:MOST * (k + 1), :] = rows.astype(F32)
-    select = came[0][:, features:features + META]
+    select = home[:PAIRS, features:]
     last = lax.axis_index("pipe") == lax.axis_size("pipe") - 1
     for at in range(0, features, CHUNK):
         part = slice(at, at + CHUNK)
-        base = jnp.where(last, 0.0, shifted[:, part].astype(F32))
+        base = jnp.concatenate([early[:, part], late[:, part]], axis=0).astype(F32)
+        base = jnp.where(last, 0.0, base)
         base = base + lax.dot_general(
-            select, rows_at[:, part].astype(BF16), TN, preferred_element_type=F32
+            select, home[:PAIRS, part], TN, preferred_element_type=F32
         )
         out[:, part] = base.astype(BF16)
 
 
 def final_kernel(*refs):
-    base, routes, positions = refs[:3]
-    got, (out, prob_out, back_at) = refs[3:7], refs[7:]
+    base, table, got, (out, prob_out, back_at) = *refs[:2], refs[2:6], refs[6:]
     _, z, _ = place()
     features = out.shape[1]
     label = labels(PAIRS, lambda k: z ^ k)
-    take_rows(back_at, got)
-    keys = [keys_of(routes, positions, step) for step in range(STEPS)]
+    take_rows(back_at, [got[0].at[pl.ds(PAIRS, MOST)], *got[1:]])
+    keys = [table[first:first + 2].astype(jnp.int32) for first in (4, 0)]
     select = one_hot(keys[1], label).astype(BF16)
     for at in range(0, features, CHUNK):
         part = slice(at, at + CHUNK)
@@ -322,6 +343,17 @@
     def along_all(blocks):
         return [along(blocks[k], k) for k in reversed(range(E_FLY))][::-1]
 
+    def crossing(block, k):
+        return lax.ppermute(block, "expert", [(i, i ^ (2 * k + 1)) for i in range(devices)])
+
+    def relay_crossing(block, distance):
+        route = [
+            (p * devices + i, (p + distance) % sections * devices + (i ^ 1))
+            for p in range(sections)
+            for i in range(devices)
+        ]
+        return lax.ppermute(block, ("pipe", "expert"), route)
+
     def relay(block, distance):
         route = [(i, (i + distance) % sections) for i in range(sections)]
         return lax.ppermute(block, "pipe", route)
@@ -335,74 +367,77 @@
     own = [w_down[0], w_gate[0], w_up[0]]
     acts_other = across(acts)
     others = [across(own[0])]
-    small = (routes, positions, probs, grad)
-    *picked, table, down, gate, up = call(
+    first = EARLY * tokens // 128
+    small = (routes, positions, probs)
+    *picked, table, early, late = call(
         pick_kernel,
         "pick_rows",
         [pltpu.VMEM(pair.shape, BF16)] * E_FLY
-        + [pltpu.VMEM((4, tokens), F32)]
-        + [pltpu.VMEM(array.shape, BF16) for array in own],
+        + [pltpu.VMEM((8, tokens), F32)]
+        + [pltpu.VMEM((rows, features), BF16) for rows in (first, tokens - first)],
         [pltpu.VMEM(array.shape, array.dtype) for array in small]
-        + [pltpu.SemaphoreType.DMA((7,))],
-        hbm=7,
-        operands=7,
+        + [pltpu.SemaphoreType.DMA((5,))],
+        hbm=4,
+        operands=4,
         limit=LIMIT,
-    )(*small, *own)
+        cost=COST4,
+    )(grad, *small)
     *own, picked[0] = lax.optimization_barrier((*own, picked[0]))
     others += [across(array) for array in own[1:]]
     others[0], picked[2] = lax.optimization_barrier((others[0], picked[2]))
     acts_other, picked[1] = lax.optimization_barrier((acts_other, picked[1]))
+    came_table = relay(table, 1)
+    came_early = relay(early, -1)
     got = along_all(picked)
-    table, others[1] = lax.optimization_barrier((table, others[1]))
-    table = relay(table, 1)
-    factors = call(
-        factor_kernel,
-        "factors",
-        jax.ShapeDtypeStruct((STEPS, 3, PAIRS, hidden), F32),
-        [pltpu.VMEM((2 * acts.shape[0] * acts.shape[1], hidden), F32)],
-        operands=2,
+    ahead, factors = call(
+        prepare_kernel,
+        "prepare",
+        [
+            jax.ShapeDtypeStruct((PAIRS, META + E_FLY * SPAN), BF16),
+            jax.ShapeDtypeStruct((STEPS, 3, PAIRS, hidden), F32),
+        ],
+        [
+            pltpu.VMEM((PAIRS, pieces), F32),
+            pltpu.VMEM((PAIRS, E_FLY * SPAN), F32),
+            pltpu.VMEM((2 * acts.shape[0] * acts.shape[1], hidden), F32),
+        ],
+        operands=6,
         cost=COST3,
-    )(acts, acts_other)
-    weights = [array for pair_of in zip((down, gate, up), others) for array in pair_of]
-    done, terms0 = call(
+    )(early, late, table, came_table, acts, acts_other)
+    weights = [array for pair_of in zip(own, others) for array in pair_of]
+    rows, terms0 = call(
         step_zero_kernel,
         "step_zero",
         [
-            jax.ShapeDtypeStruct((PAIRS, features), BF16),
+            jax.ShapeDtypeStruct((PAIRS, width + E_FLY * SPAN), BF16),
             jax.ShapeDtypeStruct((PAIRS, META), F32),
         ],
         [row_scratch],
-        operands=11,
+        operands=12,
         cost=COST0,
-    )(*got, factors, *weights)
-    rows = call(
-        ahead_kernel,
-        "rows_ahead",
-        jax.ShapeDtypeStruct((PAIRS, width + E_FLY * SPAN), BF16),
-        [pltpu.VMEM((PAIRS, pieces), F32), pltpu.VMEM((PAIRS, E_FLY * SPAN), F32)],
-        operands=5,
-    )(grad, routes, positions, table, done)
-    came = relay(rows, -1)
-    shifted, rows = lax.optimization_barrier((grad, rows))
-    shifted = relay(shifted, -1)
+    )(*got, ahead, factors, *weights)
+    came = relay_crossing(rows, -1)
+    terms0 = across(terms0)
+    came_early, late = lax.optimization_barrier((came_early, late))
+    came_late = relay(late, -1)
     sends = call(merge_kernel, "merge", [wide] * (E_FLY - 1), operands=1, cost=COST2)(came)
-    came = [came] + [along(send, k + 1) for k, send in enumerate(sends)]
-    back = call(
+    came = along_all([came, *sends])
+    *back, home = call(
         step_one_kernel,
         "step_one",
-        [pair] * E_FLY,
-        [pltpu.VMEM((PAIRS, pieces), F32)],
+        [pair] * (E_FLY - 1) + [jax.ShapeDtypeStruct((STEPS * PAIRS, width), BF16)],
+        [pltpu.VMEM((PAIRS, pieces), F32), pltpu.VMEM((STEPS * PAIRS, width), F32)],
         operands=12,
         cost=COST1,
     )(*came, factors, terms0, *weights)
-    back = along_all(back)
+    back = [crossing(back[k - 1], k) for k in reversed(range(1, E_FLY))][::-1]
+    home = crossing(home, 0)
     base = call(
         base_kernel,
         "base_sums",
         pltpu.VMEM((tokens, features), BF16),
-        [pltpu.VMEM((PAIRS, features), F32)],
-        operands=5,
-    )(shifted, *came)
+        operands=3,
+    )(came_early, came_late, home)
     result, prob = call(
         final_kernel,
         "final_sums",
@@ -411,8 +446,8 @@
             jax.ShapeDtypeStruct((STEPS, 2, tokens), F32),
         ],
         [row_scratch],
-        operands=7,
-    )(base, routes, positions, *back)
+        operands=6,
+    )(base, table, home, *back)
     return result[None], prob.transpose(0, 2, 1)[None]
 
 

time: 44.3 us -> 43.5 us (0.982)
  waiting for transfers between devices: 14.4 us -> 12.5 us
  starting transfers between devices: 20.3 us -> 22.2 us
  Pallas kernels: 8.74 us -> 7.87 us
    ppermute x3, waiting for transfers between devices: 7.07 us -> 1.08 us  [relay(): return lax.ppermute(block, 'pipe', route)]
    ppermute x9 -> x6, starting transfers between devices: 14.6 us -> 9.54 us  [along(): lax.ppermute(block, 'expert', [(i, i ^ 2 * k) for i in range(devices)])]
    ppermute x0 -> x5, starting transfers between devices: none -> 4.55 us  [the longest x4 4.4 us: crossing(): lax.ppermute(block, 'expert', [(i, i ^ 2 * k + 1) for i in range(devices)])]
    ppermute x0 -> x5, waiting for transfers between devices: none -> 4.44 us  [the longest x1 2.43 us: relay_crossing(): return lax.ppermute(block, ('pipe', 'expert'), route)]
    ppermute x3, starting transfers between devices: 4.53 us -> 7.01 us  [relay(): return lax.ppermute(block, 'pipe', route)]
    pallas_call x1, Pallas kernels: 2.34 us -> 1.58 us  [local_chip(): call(pick_kernel, 'pick_rows', [pltpu.VMEM(pair.shape, BF16)] * E_FLY + [...]
    ppermute x9 -> x6, waiting for transfers between devices: 6.12 us -> 5.82 us  [along(): lax.ppermute(block, 'expert', [(i, i ^ 2 * k) for i in range(devices)])]
    pallas_call x5 -> x4, Pallas kernels: 4.96 us -> 4.86 us  [the longest x1 2.1 us: local_chip(): call(step_one_kernel, 'step_one', [pair] * (E_FLY - 1) + [jax.ShapeDtypeS...]
  transfers between devices with their start and end apart: 16 -> 19, of which waited for: 8 -> 9; matrix products, arithmetic and copies ran while one was open for 0% -> 0% of each run, Pallas kernels for 16% -> 15%
where the time goes in v4:
time: 43.5 us; the launch traced here: 43.3 us
  starting transfers between devices  22.2 us (51%)
  waiting for transfers between devices  12.5 us (29%)
  Pallas kernels  7.87 us (18%)
  between operations  0.72 us (2%)
    ppermute x6, starting transfers between devices, along(): lax.ppermute(block, 'expert', [(i, i ^ 2 * k) for i in range(devices)])  9.54 us
    ppermute x3, starting transfers between devices, relay(): return lax.ppermute(block, 'pipe', route)  7.01 us
    ppermute x6, waiting for transfers between devices, along(): lax.ppermute(block, 'expert', [(i, i ^ 2 * k) for i in range(devices)])  5.82 us
    ppermute x4, starting transfers between devices, crossing(): lax.ppermute(block, 'expert', [(i, i ^ 2 * k + 1) for i in range(devices)])  4.4 us
    ppermute x1, waiting for transfers between devices, relay_crossing(): return lax.ppermute(block, ('pipe', 'expert'), route)  2.43 us
    pallas_call x1, Pallas kernels, local_chip(): call(step_one_kernel, 'step_one', [pair] * (E_FLY - 1) + [jax.ShapeDtypeS...  2.1 us
    ppermute x4, waiting for transfers between devices, crossing(): lax.ppermute(block, 'expert', [(i, i ^ 2 * k + 1) for i in range(devices)])  2.01 us
    pallas_call x1, Pallas kernels, local_chip(): call(step_zero_kernel, 'step_zero', [jax.ShapeDtypeStruct((PAIRS, width +...  1.91 us
  transfers between devices with their start and end apart: 19, of which 9 were waited for; matrix products, arithmetic and copies ran while one was open for 0% of the time, Pallas kernels for 15%

profile of v4, /device:TPU:0, one launch (start us, length us, event | category | flops | bytes accessed | tf_op | source)
XLA Modules:
  0.0 43.3 jit_solution(10665489147715648357)
XLA Ops:
  0.6 0.0 copy-start.1
  0.6 0.5 %collective-permute-start.4 = (bf16[128,3840]{1,0:T(8,128)(2,1)}, bf16[128,3840]{1,0:T(8,128)(2,1)S(1)}, u32[]{:S(2)}, u32[]{:S(2)}) collective-permute-start(bf16[128,3840]{1,0:T(8,128)(2,1)} %bitcast.18), channel_id=1, source_target_pairs={{0,1},{1,0},{2,3},{3,2},{4,5},{5,4},{6,7},{7,6},{8,9},{9,8},{10,11... | collective-permute-start | bytes 2949128 | tf_op jit(solution)/shard_map/ppermute | solution.py:336
  1.2 0.1 collective-permute-start.2
  1.2 1.6 %pick_rows.1 = (bf16[2,3968]{1,0:T(2,128)(2,1)S(1)}, bf16[2,3968]{1,0:T(2,128)(2,1)S(1)}, bf16[2,3968]{1,0:T(2,128)(2,1)S(1)}, bf16[2,3968]{1,0:T(2,128)(2,1)S(1...) custom-call(bf16[128,3840]{1,0:T(8,128)(2,1)} %bitcast.29, ...), custom_call_target="tpu_custom_call" | custom-call | tf_op jit(solution)/shard_map/pick_rows/pallas_call | solution.py:372
  2.8 0.0 copy-start.3
  2.8 3.0 %collective-permute-start.7 = (f32[8,128]{1,0:T(8,128)S(1)}, f32[8,128]{1,0:T(8,128)S(1)}, u32[]{:S(2)}, u32[]{:S(2)}) collective-permute-start(f32[8,128]{1,0:T(8,128)S(1)} %get-tuple-element.43.refs_2_.refs_1_), channel_id=1, source_target_pairs={{0,8},{8,16},{16,24},{24,0},{1,9},{9,17},{17,25},{25,1},{2,10},{10... | collective-permute-start | bytes 12296 | tf_op jit(solution)/shard_map/ppermute | solution.py:359
  5.8 3.6 %collective-permute-start.6 = (bf16[2,3968]{1,0:T(2,128)(2,1)S(1)}, bf16[2,3968]{1,0:T(2,128)(2,1)S(1)}, u32[]{:S(2)}, u32[]{:S(2)}) collective-permute-start(bf16[2,3968]{1,0:T(2,128)(2,1)S(1)} %get-tuple-element.42), channel_id=1, source_target_pairs={{0,6},{1,7},{2,4},{3,5},{4,2},{5,3},{6,0},{7,1},{8,14},{9,15},{10,... | collective-permute-start | bytes 47624 | tf_op jit(solution)/shard_map/ppermute | solution.py:341
  9.4 0.0 copy-done.1
  9.4 0.0 collective-permute-start.8
  9.4 0.0 collective-permute-done.2.refs_5_
  9.4 0.5 %collective-permute-start.9 = (bf16[3840,128]{1,0:T(8,128)(2,1)}, bf16[3840,128]{1,0:T(8,128)(2,1)S(1)}, u32[]{:S(2)}, u32[]{:S(2)}) collective-permute-start(bf16[3840,128]{1,0:T(8,128)(2,1)} %bitcast.24), channel_id=1, source_target_pairs={{0,1},{1,0},{2,3},{3,2},{4,5},{5,4},{6,7},{7,6},{8,9},{9,8},{10,11... | collective-permute-start | bytes 2949128 | tf_op jit(solution)/shard_map/ppermute | solution.py:336
  9.9 0.0 collective-permute-done.4.refs_7_
  9.9 0.0 collective-permute-start.3
  9.9 0.0 collective-permute-done.7.refs_3_
  9.9 1.5 %collective-permute-start.5 = (bf16[2,3968]{1,0:T(2,128)(2,1)S(1)}, bf16[2,3968]{1,0:T(2,128)(2,1)S(1)}, u32[]{:S(2)}, u32[]{:S(2)}) collective-permute-start(bf16[2,3968]{1,0:T(2,128)(2,1)S(1)} %get-tuple-element.41), channel_id=1, source_target_pairs={{0,4},{1,5},{2,6},{3,7},{4,0},{5,1},{6,2},{7,3},{8,12},{9,13},{10,... | collective-permute-start | bytes 47624 | tf_op jit(solution)/shard_map/ppermute | solution.py:341
  11.4 0.0 copy-done.3
  11.4 0.4 prepare.1
  11.8 0.0 collective-permute-done.6.refs_3_
  11.8 1.6 %collective-permute-start = (bf16[24,3840]{1,0:T(8,128)(2,1)S(1)}, bf16[24,3840]{1,0:T(8,128)(2,1)S(1)}, u32[]{:S(2)}, u32[]{:S(2)}) collective-permute-start(bf16[24,3840]{1,0:T(8,128)(2,1)S(1)} %get-tuple-element.32.refs_0_), channel_id=1, source_target_pairs={{0,24},{8,0},{16,8},{24,16},{1,25},{9,1},{17,9},{25,17},{2,26},{10... | collective-permute-start | bytes 552968 | tf_op jit(solution)/shard_map/ppermute | solution.py:359
  13.4 0.2 collective-permute-done.3.refs_1_
  13.7 0.0 collective-permute-done.8.refs_9_
  13.7 0.0 collective-permute-done.9.refs_11_
  13.7 1.0 %collective-permute-done.5.refs_2_ = bf16[2,3968]{1,0:T(2,128)(2,1)S(1)} collective-permute-done((bf16[2,3968]{1,0:T(2,128)(2,1)S(1)}, bf16[2,3968]{1,0:T(2,128)(2,1)S(1)}, u32[]{:S(2)}, u32[]{:S(2)}) %collective-permute-start.5) | collective-permute-done | bytes 15904 | tf_op jit(solution)/shard_map/ppermute | solution.py:341
  14.6 1.9 %step_zero.1 = (bf16[8,8064]{1,0:T(8,128)(2,1)S(1)}, f32[8,128]{1,0:T(8,128)S(1)}) custom-call(bf16[2,3968]{1,0:T(2,128)(2,1)S(1)} %get-tuple-element.37.refs_0_, bf16[2,3968]{1,0:T(2,128)(2,1)S(1)} %collective-permute-done.3.refs_1_, bf16[2,3968]{1,0:T(2,128)(2,1)S(1)} %collective-permute-done.5.refs_2_, ...), custom_call_target="tpu_custom_call" | custom-call | flops 20000000000 | tf_op jit(solution)/shard_map/step_zero/pallas_call | solution.py:408
  16.6 0.2 collective-permute-start.10
  16.7 0.7 %collective-permute-done.refs_0_ = bf16[24,3840]{1,0:T(8,128)(2,1)S(1)} collective-permute-done((bf16[24,3840]{1,0:T(8,128)(2,1)S(1)}, bf16[24,3840]{1,0:T(8,128)(2,1)S(1)}, u32[]{:S(2)}, u32[]{:S(2)}) %collective-permute-start) | collective-permute-done | bytes 184352 | tf_op jit(solution)/shard_map/ppermute | solution.py:359
  17.4 2.4 %collective-permute-start.1 = (bf16[104,3840]{1,0:T(8,128)(2,1)S(1)}, bf16[104,3840]{1,0:T(8,128)(2,1)S(1)}, u32[]{:S(2)}, u32[]{:S(2)}) collective-permute-start(bf16[104,3840]{1,0:T(8,128)(2,1)S(1)} %get-tuple-element.35.refs_1_), channel_id=1, source_target_pairs={{0,24},{8,0},{16,8},{24,16},{1,25},{9,1},{17,9},{25,17},{2,26},{10... | collective-permute-start | bytes 2396168 | tf_op jit(solution)/shard_map/ppermute | solution.py:359
  19.9 2.4 %collective-permute-done.10.came.refs_0_ = bf16[8,8064]{1,0:T(8,128)(2,1)S(1)} collective-permute-done((bf16[8,8064]{1,0:T(8,128)(2,1)S(1)}, bf16[8,8064]{1,0:T(8,128)(2,1)S(1)}, u32[]{:S(2)}, u32[]{:S(2)}) %collective-permute-start.10) | collective-permute-done | bytes 129056 | tf_op jit(solution)/shard_map/ppermute | solution.py:355
  22.3 2.0 %collective-permute-start.11 = (bf16[8,4864]{1,0:T(8,128)(2,1)S(1)}, bf16[8,4864]{1,0:T(8,128)(2,1)S(1)}, u32[]{:S(2)}, u32[]{:S(2)}) collective-permute-start(bf16[8,4864]{1,0:T(8,128)(2,1)S(1)} %get-tuple-element.52), channel_id=1, source_target_pairs={{0,2},{1,3},{2,0},{3,1},{4,6},{5,7},{6,4},{7,5},{8,10},{9,11},{10,... | collective-permute-start | bytes 233480 | tf_op jit(solution)/shard_map/ppermute | solution.py:341
  24.3 0.2 collective-permute-start.12
  24.6 2.2 %collective-permute-start.13 = (bf16[8,4864]{1,0:T(8,128)(2,1)S(1)}, bf16[8,4864]{1,0:T(8,128)(2,1)S(1)}, u32[]{:S(2)}, u32[]{:S(2)}) collective-permute-start(bf16[8,4864]{1,0:T(8,128)(2,1)S(1)} %get-tuple-element.54), channel_id=1, source_target_pairs={{0,6},{1,7},{2,4},{3,5},{4,2},{5,3},{6,0},{7,1},{8,14},{9,15},{10,... | collective-permute-start | bytes 233480 | tf_op jit(solution)/shard_map/ppermute | solution.py:341
  26.8 0.0 collective-permute-start.14
  26.8 1.2 %collective-permute-done.14.refs_5_ = f32[8,128]{1,0:T(8,128)S(1)} collective-permute-done((f32[8,128]{1,0:T(8,128)S(1)}, f32[8,128]{1,0:T(8,128)S(1)}, u32[]{:S(2)}, u32[]{:S(2)}) %collective-permute-start.14) | collective-permute-done | bytes 4128 | tf_op jit(solution)/shard_map/ppermute | solution.py:336
  27.9 0.0 collective-permute-done.11.refs_1_
  27.9 4.6 %collective-permute-done.12.refs_2_ = bf16[8,4864]{1,0:T(8,128)(2,1)S(1)} collective-permute-done((bf16[8,4864]{1,0:T(8,128)(2,1)S(1)}, bf16[8,4864]{1,0:T(8,128)(2,1)S(1)}, u32[]{:S(2)}, u32[]{:S(2)}) %collective-permute-start.12) | collective-permute-done | bytes 77856 | tf_op jit(solution)/shard_map/ppermute | solution.py:341
  32.6 0.0 collective-permute-done.13.refs_3_
  32.6 2.1 %step_one.1 = (bf16[2,3968]{1,0:T(2,128)(2,1)S(1)}, bf16[2,3968]{1,0:T(2,128)(2,1)S(1)}, bf16[2,3968]{1,0:T(2,128)(2,1)S(1)}, bf16[16,3968]{1,0:T(8,128)(2,1)S(1)}) custom-call(bf16[8,8064]{1,0:T(8,128)(2,1)S(1)} %collective-permute-done.10.came.refs_0_, bf16[8,4864]{1,0:T(8,128)(2,1)S(1)} %collective-permute-done.11.refs_1_, ...), custom_call_target="tpu_custom_call" | custom-call | tf_op jit(solution)/shard_map/step_one/pallas_call | solution.py:425
  34.7 0.0 collective-permute-start.15
  34.7 2.3 %collective-permute-start.16 = (bf16[2,3968]{1,0:T(2,128)(2,1)S(1)}, bf16[2,3968]{1,0:T(2,128)(2,1)S(1)}, u32[]{:S(2)}, u32[]{:S(2)}) collective-permute-start(bf16[2,3968]{1,0:T(2,128)(2,1)S(1)} %get-tuple-element.57), channel_id=1, source_target_pairs={{0,3},{1,2},{2,1},{3,0},{4,7},{5,6},{6,5},{7,4},{8,11},{9,10},{10,... | collective-permute-start | bytes 47624 | tf_op jit(solution)/shard_map/ppermute | solution.py:347
  37.0 0.0 collective-permute-start.17
  37.0 2.1 %collective-permute-start.18 = (bf16[2,3968]{1,0:T(2,128)(2,1)S(1)}, bf16[2,3968]{1,0:T(2,128)(2,1)S(1)}, u32[]{:S(2)}, u32[]{:S(2)}) collective-permute-start(bf16[2,3968]{1,0:T(2,128)(2,1)S(1)} %get-tuple-element.59), channel_id=1, source_target_pairs={{0,7},{1,6},{2,5},{3,4},{4,3},{5,2},{6,1},{7,0},{8,15},{9,14},{10,... | collective-permute-start | bytes 47624 | tf_op jit(solution)/shard_map/ppermute | solution.py:347
  39.1 0.4 collective-permute-done.1.refs_1_
  39.5 0.0 collective-permute-done.15.refs_2_
  39.5 0.5 %base_sums.1.refs_0_ = bf16[128,3840]{1,0:T(8,128)(2,1)S(1)} custom-call(bf16[24,3840]{1,0:T(8,128)(2,1)S(1)} %collective-permute-done.refs_0_, bf16[104,3840]{1,0:T(8,128)(2,1)S(1)} %collective-permute-done.1.refs_1_, bf16[16,3968]{1,0:T(8,128)(2,1)S(1)} %collective-permute-done.15.refs_2_), custom_call_target="tpu_custom_call" | custom-call | tf_op jit(solution)/shard_map/base_sums/pallas_call | solution.py:435
  39.9 0.0 collective-permute-done.16.refs_3_
  39.9 1.4 %collective-permute-done.17.refs_4_ = bf16[2,3968]{1,0:T(2,128)(2,1)S(1)} collective-permute-done((bf16[2,3968]{1,0:T(2,128)(2,1)S(1)}, bf16[2,3968]{1,0:T(2,128)(2,1)S(1)}, u32[]{:S(2)}, u32[]{:S(2)}) %collective-permute-start.17) | collective-permute-done | bytes 15904 | tf_op jit(solution)/shard_map/ppermute | solution.py:347
  41.3 0.6 %collective-permute-done.18.refs_5_ = bf16[2,3968]{1,0:T(2,128)(2,1)S(1)} collective-permute-done((bf16[2,3968]{1,0:T(2,128)(2,1)S(1)}, bf16[2,3968]{1,0:T(2,128)(2,1)S(1)}, u32[]{:S(2)}, u32[]{:S(2)}) %collective-permute-start.18) | collective-permute-done | bytes 15904 | tf_op jit(solution)/shard_map/ppermute | solution.py:347
  41.9 1.4 %final_sums.1 = (bf16[128,3840]{1,0:T(8,128)(2,1)}, f32[2,2,128]{2,1,0:T(2,128)}) custom-call(bf16[128,3840]{1,0:T(8,128)(2,1)S(1)} %base_sums.1.refs_0_, f32[8,128]{1,0:T(8,128)S(1)} %get-tuple-element.43.refs_2_.refs_1_, bf16[16,3968]{1,0:T(8,128)(2,1)S(1)} %collective-permute-done.15.refs_2_, bf16[2,3968]{1,0:T(2,128)(2,1)S(1)} %collective-permute-done.16.refs_3_, ...), custom_call_target="tpu_custom_call" | custom-call | tf_op jit(solution)/shard_map/final_sums/pallas_call | solution.py:441
  (5 shorter events, 0.0 us)
Async XLA Ops:
  0.6 8.8 %copy-start.1 = (bf16[1,3840,128]{2,1,0:T(8,128)(2,1)S(1)}, bf16[1,3840,128]{2,1,0:T(8,128)(2,1)}, u32[]{:S(2)}) copy-start(bf16[1,3840,128]{2,1,0:T(8,128)(2,1)} %param.13) | copy-start | bytes 2949124
  0.6 9.3 %collective-permute-start.4 = (bf16[128,3840]{1,0:T(8,128)(2,1)}, bf16[128,3840]{1,0:T(8,128)(2,1)S(1)}, u32[]{:S(2)}, u32[]{:S(2)}) collective-permute-start(bf16[128,3840]{1,0:T(8,128)(2,1)} %bitcast.18), channel_id=1, source_target_pairs={{0,1},{1,0},{2,3},{3,2},{4,5},{5,4},{6,7},{7,6},{8,9},{9,8},{10,11... | collective-permute-start | bytes 2949128 | tf_op jit(solution)/shard_map/ppermute | solution.py:336
  1.2 8.3 %collective-permute-start.2 = (bf16[2,16,2,128]{3,2,1,0:T(2,128)(2,1)}, bf16[2,16,2,128]{3,2,1,0:T(2,128)(2,1)S(1)}, u32[]{:S(2)}, u32[]{:S(2)}) collective-permute-start(bf16[2,16,2,128]{3,2,1,0:T(2,128)(2,1)} %bitcast.27), channel_id=1, source_target_pairs={{0,1},{1,0},{2,3},{3,2},{4,5},{5,4},{6,7},{7,6},{8,9},{9,8},{10,11... | collective-permute-start | bytes 49160 | tf_op jit(solution)/shard_map/ppermute | solution.py:336
  2.8 8.6 %copy-start.3 = (bf16[1,2,16,2,128]{4,3,2,1,0:T(2,128)(2,1)S(1)}, bf16[1,2,16,2,128]{4,3,2,1,0:T(2,128)(2,1)}, u32[]{:S(2)}) copy-start(bf16[1,2,16,2,128]{4,3,2,1,0:T(2,128)(2,1)} %param.12) | copy-start | bytes 49156
  2.8 7.1 %collective-permute-start.7 = (f32[8,128]{1,0:T(8,128)S(1)}, f32[8,128]{1,0:T(8,128)S(1)}, u32[]{:S(2)}, u32[]{:S(2)}) collective-permute-start(f32[8,128]{1,0:T(8,128)S(1)} %get-tuple-element.43.refs_2_.refs_1_), channel_id=1, source_target_pairs={{0,8},{8,16},{16,24},{24,0},{1,9},{9,17},{17,25},{25,1},{2,10},{10... | collective-permute-start | bytes 12296 | tf_op jit(solution)/shard_map/ppermute | solution.py:359
  5.8 6.0 %collective-permute-start.6 = (bf16[2,3968]{1,0:T(2,128)(2,1)S(1)}, bf16[2,3968]{1,0:T(2,128)(2,1)S(1)}, u32[]{:S(2)}, u32[]{:S(2)}) collective-permute-start(bf16[2,3968]{1,0:T(2,128)(2,1)S(1)} %get-tuple-element.42), channel_id=1, source_target_pairs={{0,6},{1,7},{2,4},{3,5},{4,2},{5,3},{6,0},{7,1},{8,14},{9,15},{10,... | collective-permute-start | bytes 47624 | tf_op jit(solution)/shard_map/ppermute | solution.py:341
  9.4 4.3 %collective-permute-start.8 = (bf16[3840,128]{1,0:T(8,128)(2,1)S(1)}, bf16[3840,128]{1,0:T(8,128)(2,1)S(1)}, u32[]{:S(2)}, u32[]{:S(2)}) collective-permute-start(bf16[3840,128]{1,0:T(8,128)(2,1)S(1)} %bitcast.21), channel_id=1, source_target_pairs={{0,1},{1,0},{2,3},{3,2},{4,5},{5,4},{6,7},{7,6},{8,9},{9,8},{10,11... | collective-permute-start | bytes 2949128 | tf_op jit(solution)/shard_map/ppermute | solution.py:336
  9.4 4.3 %collective-permute-start.9 = (bf16[3840,128]{1,0:T(8,128)(2,1)}, bf16[3840,128]{1,0:T(8,128)(2,1)S(1)}, u32[]{:S(2)}, u32[]{:S(2)}) collective-permute-start(bf16[3840,128]{1,0:T(8,128)(2,1)} %bitcast.24), channel_id=1, source_target_pairs={{0,1},{1,0},{2,3},{3,2},{4,5},{5,4},{6,7},{7,6},{8,9},{9,8},{10,11... | collective-permute-start | bytes 2949128 | tf_op jit(solution)/shard_map/ppermute | solution.py:336
  9.9 3.7 %collective-permute-start.3 = (bf16[2,3968]{1,0:T(2,128)(2,1)S(1)}, bf16[2,3968]{1,0:T(2,128)(2,1)S(1)}, u32[]{:S(2)}, u32[]{:S(2)}) collective-permute-start(bf16[2,3968]{1,0:T(2,128)(2,1)S(1)} %get-tuple-element.39), channel_id=1, source_target_pairs={{0,2},{1,3},{2,0},{3,1},{4,6},{5,7},{6,4},{7,5},{8,10},{9,11},{10,... | collective-permute-start | bytes 47624 | tf_op jit(solution)/shard_map/ppermute | solution.py:341
  9.9 4.7 %collective-permute-start.5 = (bf16[2,3968]{1,0:T(2,128)(2,1)S(1)}, bf16[2,3968]{1,0:T(2,128)(2,1)S(1)}, u32[]{:S(2)}, u32[]{:S(2)}) collective-permute-start(bf16[2,3968]{1,0:T(2,128)(2,1)S(1)} %get-tuple-element.41), channel_id=1, source_target_pairs={{0,4},{1,5},{2,6},{3,7},{4,0},{5,1},{6,2},{7,3},{8,12},{9,13},{10,... | collective-permute-start | bytes 47624 | tf_op jit(solution)/shard_map/ppermute | solution.py:341
  11.4 3.2 %copy-start = (bf16[1,128,3840]{2,1,0:T(8,128)(2,1)S(1)}, bf16[1,128,3840]{2,1,0:T(8,128)(2,1)}, u32[]{:S(2)}) copy-start(bf16[1,128,3840]{2,1,0:T(8,128)(2,1)} %param.15) | copy-start | bytes 2949124
  11.4 3.2 %copy-start.2 = (bf16[1,3840,128]{2,1,0:T(8,128)(2,1)S(1)}, bf16[1,3840,128]{2,1,0:T(8,128)(2,1)}, u32[]{:S(2)}) copy-start(bf16[1,3840,128]{2,1,0:T(8,128)(2,1)} %param.14) | copy-start | bytes 2949124
  11.8 5.6 %collective-permute-start = (bf16[24,3840]{1,0:T(8,128)(2,1)S(1)}, bf16[24,3840]{1,0:T(8,128)(2,1)S(1)}, u32[]{:S(2)}, u32[]{:S(2)}) collective-permute-start(bf16[24,3840]{1,0:T(8,128)(2,1)S(1)} %get-tuple-element.32.refs_0_), channel_id=1, source_target_pairs={{0,24},{8,0},{16,8},{24,16},{1,25},{9,1},{17,9},{25,17},{2,26},{10... | collective-permute-start | bytes 552968 | tf_op jit(solution)/shard_map/ppermute | solution.py:359
  16.6 5.7 %collective-permute-start.10 = (bf16[8,8064]{1,0:T(8,128)(2,1)S(1)}, bf16[8,8064]{1,0:T(8,128)(2,1)S(1)}, u32[]{:S(2)}, u32[]{:S(2)}) collective-permute-start(bf16[8,8064]{1,0:T(8,128)(2,1)S(1)} %get-tuple-element.51), channel_id=1, source_target_pairs={{0,25},{1,24},{2,27},{3,26},{4,29},{5,28},{6,31},{7,30},{8,1},{9,0... | collective-permute-start | bytes 387080 | tf_op jit(solution)/shard_map/ppermute | solution.py:355
  17.4 22.0 %collective-permute-start.1 = (bf16[104,3840]{1,0:T(8,128)(2,1)S(1)}, bf16[104,3840]{1,0:T(8,128)(2,1)S(1)}, u32[]{:S(2)}, u32[]{:S(2)}) collective-permute-start(bf16[104,3840]{1,0:T(8,128)(2,1)S(1)} %get-tuple-element.35.refs_1_), channel_id=1, source_target_pairs={{0,24},{8,0},{16,8},{24,16},{1,25},{9,1},{17,9},{25,17},{2,26},{10... | collective-permute-start | bytes 2396168 | tf_op jit(solution)/shard_map/ppermute | solution.py:359
  22.3 5.6 %collective-permute-start.11 = (bf16[8,4864]{1,0:T(8,128)(2,1)S(1)}, bf16[8,4864]{1,0:T(8,128)(2,1)S(1)}, u32[]{:S(2)}, u32[]{:S(2)}) collective-permute-start(bf16[8,4864]{1,0:T(8,128)(2,1)S(1)} %get-tuple-element.52), channel_id=1, source_target_pairs={{0,2},{1,3},{2,0},{3,1},{4,6},{5,7},{6,4},{7,5},{8,10},{9,11},{10,... | collective-permute-start | bytes 233480 | tf_op jit(solution)/shard_map/ppermute | solution.py:341
  24.3 8.2 %collective-permute-start.12 = (bf16[8,4864]{1,0:T(8,128)(2,1)S(1)}, bf16[8,4864]{1,0:T(8,128)(2,1)S(1)}, u32[]{:S(2)}, u32[]{:S(2)}) collective-permute-start(bf16[8,4864]{1,0:T(8,128)(2,1)S(1)} %get-tuple-element.53), channel_id=1, source_target_pairs={{0,4},{1,5},{2,6},{3,7},{4,0},{5,1},{6,2},{7,3},{8,12},{9,13},{10,... | collective-permute-start | bytes 233480 | tf_op jit(solution)/shard_map/ppermute | solution.py:341
  24.6 8.0 %collective-permute-start.13 = (bf16[8,4864]{1,0:T(8,128)(2,1)S(1)}, bf16[8,4864]{1,0:T(8,128)(2,1)S(1)}, u32[]{:S(2)}, u32[]{:S(2)}) collective-permute-start(bf16[8,4864]{1,0:T(8,128)(2,1)S(1)} %get-tuple-element.54), channel_id=1, source_target_pairs={{0,6},{1,7},{2,4},{3,5},{4,2},{5,3},{6,0},{7,1},{8,14},{9,15},{10,... | collective-permute-start | bytes 233480 | tf_op jit(solution)/shard_map/ppermute | solution.py:341
  26.8 1.2 %collective-permute-start.14 = (f32[8,128]{1,0:T(8,128)S(1)}, f32[8,128]{1,0:T(8,128)S(1)}, u32[]{:S(2)}, u32[]{:S(2)}) collective-permute-start(f32[8,128]{1,0:T(8,128)S(1)} %get-tuple-element.55), channel_id=1, source_target_pairs={{0,1},{1,0},{2,3},{3,2},{4,5},{5,4},{6,7},{7,6},{8,9},{9,8},{10,11... | collective-permute-start | bytes 12296 | tf_op jit(solution)/shard_map/ppermute | solution.py:336
  34.7 4.8 %collective-permute-start.15 = (bf16[16,3968]{1,0:T(8,128)(2,1)S(1)}, bf16[16,3968]{1,0:T(8,128)(2,1)S(1)}, u32[]{:S(2)}, u32[]{:S(2)}) collective-permute-start(bf16[16,3968]{1,0:T(8,128)(2,1)S(1)} %get-tuple-element.56), channel_id=1, source_target_pairs={{0,1},{1,0},{2,3},{3,2},{4,5},{5,4},{6,7},{7,6},{8,9},{9,8},{10,11... | collective-permute-start | bytes 380936 | tf_op jit(solution)/shard_map/ppermute | solution.py:347
  34.7 5.2 %collective-permute-start.16 = (bf16[2,3968]{1,0:T(2,128)(2,1)S(1)}, bf16[2,3968]{1,0:T(2,128)(2,1)S(1)}, u32[]{:S(2)}, u32[]{:S(2)}) collective-permute-start(bf16[2,3968]{1,0:T(2,128)(2,1)S(1)} %get-tuple-element.57), channel_id=1, source_target_pairs={{0,3},{1,2},{2,1},{3,0},{4,7},{5,6},{6,5},{7,4},{8,11},{9,10},{10,... | collective-permute-start | bytes 47624 | tf_op jit(solution)/shard_map/ppermute | solution.py:347
  37.0 4.3 %collective-permute-start.17 = (bf16[2,3968]{1,0:T(2,128)(2,1)S(1)}, bf16[2,3968]{1,0:T(2,128)(2,1)S(1)}, u32[]{:S(2)}, u32[]{:S(2)}) collective-permute-start(bf16[2,3968]{1,0:T(2,128)(2,1)S(1)} %get-tuple-element.58), channel_id=1, source_target_pairs={{0,5},{1,4},{2,7},{3,6},{4,1},{5,0},{6,3},{7,2},{8,13},{9,12},{10,... | collective-permute-start | bytes 47624 | tf_op jit(solution)/shard_map/ppermute | solution.py:347
  37.0 5.0 %collective-permute-start.18 = (bf16[2,3968]{1,0:T(2,128)(2,1)S(1)}, bf16[2,3968]{1,0:T(2,128)(2,1)S(1)}, u32[]{:S(2)}, u32[]{:S(2)}) collective-permute-start(bf16[2,3968]{1,0:T(2,128)(2,1)S(1)} %get-tuple-element.59), channel_id=1, source_target_pairs={{0,7},{1,6},{2,5},{3,4},{4,3},{5,2},{6,1},{7,0},{8,15},{9,14},{10,... | collective-permute-start | bytes 47624 | tf_op jit(solution)/shard_map/ppermute | solution.py:347

commit v5 on v3

--- a/solution.py
+++ b/solution.py
@@ -14,6 +14,7 @@
 META = 128
 CHUNK = 256
 SPAN = 1024
+OUT = 1280
 COST0 = 20_000_000_000
 COST1 = 0
 COST2 = 20_000_000_000
@@ -25,7 +26,7 @@
 TN = (((0,), (0,)), ((), ()))
 
 
-def call(kernel, name, out_shape, scratch=(), hbm=0, operands=0, limit=24, cost=0):
+def call(kernel, name, out_shape, scratch=(), hbm=0, operands=0, limit=24, cost=0, out_specs=None):
     specs = [pl.BlockSpec(memory_space=pl.ANY)] * hbm
     specs += [pl.BlockSpec(memory_space=pltpu.VMEM)] * (operands - hbm)
     return pl.pallas_call(
@@ -33,6 +34,7 @@
         name=name,
         out_shape=out_shape,
         in_specs=specs,
+        **({} if out_specs is None else {"out_specs": out_specs}),
         scratch_shapes=list(scratch),
         cost_estimate=pl.CostEstimate(flops=cost, bytes_accessed=0, transcendentals=0),
         compiler_params=pltpu.CompilerParams(vmem_limit_bytes=limit * 2**20),
@@ -99,8 +101,8 @@
 
 
 def pick_kernel(*refs):
-    outs, (table, *weights), held, sems = refs[7:11], refs[11:15], refs[15:19], refs[19]
-    copies = bring(refs[:7], (*held, *weights), sems)
+    outs, table, held, sems = refs[4:8], refs[8], refs[9:13], refs[13]
+    copies = bring(refs[:4], held, sems)
     routes, positions, probs, grad = held
     for copy in copies[:3]:
         copy.wait()
@@ -114,8 +116,6 @@
     copies[3].wait()
     rows = jnp.dot(select.astype(BF16), grad[...], preferred_element_type=F32)
     put_rows(outs, rows, first_lanes([rate]))
-    for copy in copies[4:]:
-        copy.wait()
 
 
 def ahead_kernel(grad, routes, positions, table, done, rows_out, held, packed):
@@ -258,45 +258,53 @@
         out[:, features:] = meta[MOST * k:MOST * (k + 1)].astype(BF16)
 
 
-def base_kernel(*refs):
-    shifted, came, (out, rows_at) = refs[0], refs[1:5], refs[5:]
-    features = out.shape[1]
+def own_kernel(*refs):
+    routes, positions, came, (rows, takes) = *refs[:2], refs[2:6], refs[6:]
+    _, z, _ = place()
+    features = rows.shape[1]
     for k in range(E_FLY):
-        rows = came[k][MOST * k:MOST * (k + 1), :features]
-        rows_at[MOST * k:MOST * (k + 1), :] = rows.astype(F32)
-    select = came[0][:, features:features + META]
-    last = lax.axis_index("pipe") == lax.axis_size("pipe") - 1
-    for at in range(0, features, CHUNK):
-        part = slice(at, at + CHUNK)
-        base = jnp.where(last, 0.0, shifted[:, part].astype(F32))
-        base = base + lax.dot_general(
-            select, rows_at[:, part].astype(BF16), TN, preferred_element_type=F32
-        )
-        out[:, part] = base.astype(BF16)
+        own = came[k][MOST * k:MOST * (k + 1), :features]
+        rows[MOST * k:MOST * (k + 1), :] = own.astype(F32)
+    select = one_hot(keys_of(routes, positions, 1), labels(PAIRS, lambda k: z ^ k))
+    before = came[0][:, features:features + META].astype(F32)
+    takes[...] = jnp.concatenate([before, select], axis=0).astype(BF16)
 
 
 def final_kernel(*refs):
-    base, routes, positions = refs[:3]
-    got, (out, prob_out, back_at) = refs[3:7], refs[7:]
-    _, z, _ = place()
+    shifted, own, takes, routes, positions = refs[:5]
+    got, (out, prob_out) = refs[5:9], refs[9:11]
+    back_at, out_at, prob_at, sems = refs[11:]
+    p, z, _ = place()
     features = out.shape[1]
     label = labels(PAIRS, lambda k: z ^ k)
     take_rows(back_at, got)
-    keys = [keys_of(routes, positions, step) for step in range(STEPS)]
-    select = one_hot(keys[1], label).astype(BF16)
-    for at in range(0, features, CHUNK):
-        part = slice(at, at + CHUNK)
-        rows = back_at[:, part].astype(BF16)
-        delta = lax.dot_general(select, rows, TN, preferred_element_type=F32)
-        out[:, part] = (base[:, part].astype(F32) + delta).astype(BF16)
     meta = back_at[:, features:]
     for step in range(STEPS):
         first = 3 * (STEPS - 1 - step)
         terms = meta[:, first:first + 1] + (meta[:, first + 1:first + 2] + meta[:, first + 2:first + 3])
-        for choice, hit in enumerate(hits(keys[step], label)):
-            prob_out[step, choice:choice + 1] = jnp.sum(
+        for choice, hit in enumerate(hits(keys_of(routes, positions, step), label)):
+            prob_at[step, choice:choice + 1] = jnp.sum(
                 jnp.where(hit, terms, 0.0), axis=0, keepdims=True
             )
+    copies = [pltpu.make_async_copy(prob_at, prob_out, sems.at[0])]
+    copies[0].start()
+    last = p == lax.axis_size("pipe") - 1
+    for at in range(0, features, CHUNK):
+        part = slice(at, at + CHUNK)
+        rows = jnp.concatenate([own[:, part], back_at[:, part]], axis=0).astype(BF16)
+        delta = lax.dot_general(takes[...], rows, TN, preferred_element_type=F32)
+        base = jnp.where(last, 0.0, shifted[:, part].astype(F32))
+        out_at[:, part] = (base + delta).astype(BF16)
+        if (at + CHUNK) % OUT == 0:
+            wide = pl.ds(at + CHUNK - OUT, OUT)
+            copies.append(
+                pltpu.make_async_copy(
+                    out_at.at[:, wide], out.at[:, wide], sems.at[len(copies)]
+                )
+            )
+            copies[-1].start()
+    for copy in copies:
+        copy.wait()
 
 
 def local_chip(out_grad, routes, positions, route_probs, saved_acts, w_gate, w_up, w_down):
@@ -336,18 +344,17 @@
     acts_other = across(acts)
     others = [across(own[0])]
     small = (routes, positions, probs, grad)
-    *picked, table, down, gate, up = call(
+    *picked, table = call(
         pick_kernel,
         "pick_rows",
         [pltpu.VMEM(pair.shape, BF16)] * E_FLY
-        + [pltpu.VMEM((4, tokens), F32)]
-        + [pltpu.VMEM(array.shape, BF16) for array in own],
+        + [pltpu.VMEM((4, tokens), F32)],
         [pltpu.VMEM(array.shape, array.dtype) for array in small]
-        + [pltpu.SemaphoreType.DMA((7,))],
-        hbm=7,
-        operands=7,
+        + [pltpu.SemaphoreType.DMA((4,))],
+        hbm=4,
+        operands=4,
         limit=LIMIT,
-    )(*small, *own)
+    )(*small)
     *own, picked[0] = lax.optimization_barrier((*own, picked[0]))
     others += [across(array) for array in own[1:]]
     others[0], picked[2] = lax.optimization_barrier((others[0], picked[2]))
@@ -363,7 +370,7 @@
         operands=2,
         cost=COST3,
     )(acts, acts_other)
-    weights = [array for pair_of in zip((down, gate, up), others) for array in pair_of]
+    weights = [array for pair_of in zip(own, others) for array in pair_of]
     done, terms0 = call(
         step_zero_kernel,
         "step_zero",
@@ -383,7 +390,7 @@
         operands=5,
     )(grad, routes, positions, table, done)
     came = relay(rows, -1)
-    shifted, rows = lax.optimization_barrier((grad, rows))
+    shifted, _ = lax.optimization_barrier((grad, across(terms0)))
     shifted = relay(shifted, -1)
     sends = call(merge_kernel, "merge", [wide] * (E_FLY - 1), operands=1, cost=COST2)(came)
     came = [came] + [along(send, k + 1) for k, send in enumerate(sends)]
@@ -396,13 +403,15 @@
         cost=COST1,
     )(*came, factors, terms0, *weights)
     back = along_all(back)
-    base = call(
-        base_kernel,
-        "base_sums",
-        pltpu.VMEM((tokens, features), BF16),
-        [pltpu.VMEM((PAIRS, features), F32)],
-        operands=5,
-    )(shifted, *came)
+    own_rows, takes = call(
+        own_kernel,
+        "own_rows",
+        [
+            jax.ShapeDtypeStruct((PAIRS, features), F32),
+            jax.ShapeDtypeStruct((STEPS * PAIRS, tokens), BF16),
+        ],
+        operands=6,
+    )(routes, positions, *came)
     result, prob = call(
         final_kernel,
         "final_sums",
@@ -410,9 +419,15 @@
             jax.ShapeDtypeStruct((tokens, features), BF16),
             jax.ShapeDtypeStruct((STEPS, 2, tokens), F32),
         ],
-        [row_scratch],
-        operands=7,
-    )(base, routes, positions, *back)
+        [
+            row_scratch,
+            pltpu.VMEM((tokens, features), BF16),
+            pltpu.VMEM((STEPS, 2, tokens), F32),
+            pltpu.SemaphoreType.DMA((1 + features // OUT,)),
+        ],
+        operands=9,
+        out_specs=[pl.BlockSpec(memory_space=pl.ANY)] * 2,
+    )(shifted, own_rows, takes, routes, positions, *back)
     return result[None], prob.transpose(0, 2, 1)[None]
 
 

time: 44.3 us -> 42.9 us (0.968)
  Pallas kernels: 8.74 us -> 7.52 us
    ppermute x4, waiting for transfers between devices: 1.21 us -> 0.01 us  [across(): return lax.ppermute(block, 'expert', [(i, i ^ 1) for i in range(devices)])]
    ppermute x9, waiting for transfers between devices: 6.12 us -> 7.18 us  [along(): lax.ppermute(block, 'expert', [(i, i ^ 2 * k) for i in range(devices)])]
    pallas_call x1, Pallas kernels: 2.34 us -> 1.55 us  [local_chip(): call(pick_kernel, 'pick_rows', [pltpu.VMEM(pair.shape, BF16)] * E_FLY + [...]
  transfers between devices with their start and end apart: 16 -> 16, of which waited for: 8 -> 6; matrix products, arithmetic and copies ran while one was open for 0% -> 0% of each run, Pallas kernels for 16% -> 14%
where the time goes in v5:
time: 42.9 us; the launch traced here: 42.7 us
  starting transfers between devices  20.4 us (48%)
  waiting for transfers between devices  14 us (33%)
  Pallas kernels  7.52 us (18%)
  between operations  0.76 us (2%)
    ppermute x9, starting transfers between devices, along(): lax.ppermute(block, 'expert', [(i, i ^ 2 * k) for i in range(devices)])  14.6 us
    ppermute x9, waiting for transfers between devices, along(): lax.ppermute(block, 'expert', [(i, i ^ 2 * k) for i in range(devices)])  7.18 us
    ppermute x3, waiting for transfers between devices, relay(): return lax.ppermute(block, 'pipe', route)  6.83 us
    ppermute x3, starting transfers between devices, relay(): return lax.ppermute(block, 'pipe', route)  4.66 us
    pallas_call x1, Pallas kernels, local_chip(): call(step_one_kernel, 'step_one', [pair] * E_FLY, [pltpu.VMEM((PAIRS, pie...  2.09 us
    pallas_call x1, Pallas kernels, local_chip(): call(step_zero_kernel, 'step_zero', [jax.ShapeDtypeStruct((PAIRS, feature...  1.9 us
    pallas_call x1, Pallas kernels, local_chip(): call(pick_kernel, 'pick_rows', [pltpu.VMEM(pair.shape, BF16)] * E_FLY + [...  1.55 us
    pallas_call x1, Pallas kernels, local_chip(): call(final_kernel, 'final_sums', [jax.ShapeDtypeStruct((tokens, features)...  1.39 us
  transfers between devices with their start and end apart: 16, of which 6 were waited for; matrix products, arithmetic and copies ran while one was open for 0% of the time, Pallas kernels for 14%

profile of v5, /device:TPU:0, one launch (start us, length us, event | category | flops | bytes accessed | tf_op | source)
XLA Modules:
  0.0 42.7 jit_solution(8310691184788280555)
XLA Ops:
  0.6 0.0 copy-start.2
  0.6 0.5 %collective-permute-start.5 = (bf16[128,3840]{1,0:T(8,128)(2,1)}, bf16[128,3840]{1,0:T(8,128)(2,1)S(1)}, u32[]{:S(2)}, u32[]{:S(2)}) collective-permute-start(bf16[128,3840]{1,0:T(8,128)(2,1)} %bitcast.21), channel_id=1, source_target_pairs={{0,1},{1,0},{2,3},{3,2},{4,5},{5,4},{6,7},{7,6},{8,9},{9,8},{10,11... | collective-permute-start | bytes 2949128 | tf_op jit(solution)/shard_map/ppermute | solution.py:323
  1.2 0.1 collective-permute-start.3
  1.2 1.5 %pick_rows.1 = (bf16[2,3968]{1,0:T(2,128)(2,1)S(1)}, bf16[2,3968]{1,0:T(2,128)(2,1)S(1)}, bf16[2,3968]{1,0:T(2,128)(2,1)S(1)}, bf16[2,3968]{1,0:T(2,128)(2,1)S(1)}, f32[4,128]{1,0:T(4,128)S(1)}) custom-call(s32[2,2,128]{2,1,0:T(2,128)} %bitcast.30, s32[2,2,128]{2,1,0:T(2,128)} %bitcast.34, bf16[2,2,128]{2,1,0:T(2,128)(2,1)} %bitcast.40, ...), custom_call_target="tpu_custom_call" | custom-call | tf_op jit(solution)/shard_map/pick_rows/pallas_call | solution.py:347
  2.8 0.0 copy-done.2
  2.8 0.5 %collective-permute-start.1 = (bf16[3840,128]{1,0:T(8,128)(2,1)S(1)}, bf16[3840,128]{1,0:T(8,128)(2,1)S(1)}, u32[]{:S(2)}, u32[]{:S(2)}) collective-permute-start(bf16[3840,128]{1,0:T(8,128)(2,1)S(1)} %bitcast.24), channel_id=1, source_target_pairs={{0,1},{1,0},{2,3},{3,2},{4,5},{5,4},{6,7},{7,6},{8,9},{9,8},{10,11... | collective-permute-start | bytes 2949128 | tf_op jit(solution)/shard_map/ppermute | solution.py:323
  3.3 0.1 collective-permute-start.8
  3.4 5.0 %collective-permute-start.7 = (bf16[2,3968]{1,0:T(2,128)(2,1)S(1)}, bf16[2,3968]{1,0:T(2,128)(2,1)S(1)}, u32[]{:S(2)}, u32[]{:S(2)}) collective-permute-start(bf16[2,3968]{1,0:T(2,128)(2,1)S(1)} %get-tuple-element.39), channel_id=1, source_target_pairs={{0,6},{1,7},{2,4},{3,5},{4,2},{5,3},{6,0},{7,1},{8,14},{9,15},{10,... | collective-permute-start | bytes 47624 | tf_op jit(solution)/shard_map/ppermute | solution.py:328
  8.4 0.0 collective-permute-done.3.acts_other
  8.4 0.0 collective-permute-start.4
  8.4 0.0 collective-permute-done.5.refs_6_.refs_7_
  8.4 0.0 copy-start.1
  8.4 0.0 copy-start.3
  8.4 0.7 %collective-permute-start.6 = (bf16[2,3968]{1,0:T(2,128)(2,1)S(1)}, bf16[2,3968]{1,0:T(2,128)(2,1)S(1)}, u32[]{:S(2)}, u32[]{:S(2)}) collective-permute-start(bf16[2,3968]{1,0:T(2,128)(2,1)S(1)} %get-tuple-element.38), channel_id=1, source_target_pairs={{0,4},{1,5},{2,6},{3,7},{4,0},{5,1},{6,2},{7,3},{8,12},{9,13},{10,... | collective-permute-start | bytes 47624 | tf_op jit(solution)/shard_map/ppermute | solution.py:328
  9.1 0.0 copy-done.6
  9.1 0.2 factors.1.refs_4_
  9.3 0.0 collective-permute-done.1.refs_8_.refs_9_
  9.3 0.0 copy-start
  9.3 1.6 %collective-permute-start.2 = (f32[4,128]{1,0:T(4,128)S(1)}, f32[4,128]{1,0:T(4,128)S(1)}, u32[]{:S(2)}, u32[]{:S(2)}) collective-permute-start(f32[4,128]{1,0:T(4,128)S(1)} %get-tuple-element.33), channel_id=1, source_target_pairs={{0,8},{8,16},{16,24},{24,0},{1,9},{9,17},{17,25},{25,1},{2,10},{10... | collective-permute-start | bytes 6152 | tf_op jit(solution)/shard_map/ppermute | solution.py:335
  11.0 0.0 collective-permute-done.7.refs_3_
  11.0 1.2 %collective-permute-done.4.refs_1_ = bf16[2,3968]{1,0:T(2,128)(2,1)S(1)} collective-permute-done((bf16[2,3968]{1,0:T(2,128)(2,1)S(1)}, bf16[2,3968]{1,0:T(2,128)(2,1)S(1)}, u32[]{:S(2)}, u32[]{:S(2)}) %collective-permute-start.4) | collective-permute-done | bytes 15904 | tf_op jit(solution)/shard_map/ppermute | solution.py:328
  12.1 0.0 collective-permute-done.8.refs_10_.refs_11_
  12.2 1.1 %collective-permute-done.6.refs_2_ = bf16[2,3968]{1,0:T(2,128)(2,1)S(1)} collective-permute-done((bf16[2,3968]{1,0:T(2,128)(2,1)S(1)}, bf16[2,3968]{1,0:T(2,128)(2,1)S(1)}, u32[]{:S(2)}, u32[]{:S(2)}) %collective-permute-start.6) | collective-permute-done | bytes 15904 | tf_op jit(solution)/shard_map/ppermute | solution.py:328
  13.2 0.0 copy-done.1
  13.2 0.0 copy-done.3
  13.3 1.9 %step_zero.1 = (bf16[8,3840]{1,0:T(8,128)(2,1)S(1)}, f32[8,128]{1,0:T(8,128)S(1)}) custom-call(bf16[2,3968]{1,0:T(2,128)(2,1)S(1)} %get-tuple-element.34.refs_0_, bf16[2,3968]{1,0:T(2,128)(2,1)S(1)} %collective-permute-done.4.refs_1_, bf16[2,3968]{1,0:T(2,128)(2,1)S(1)} %collective-permute-done.6.refs_2_, ...), custom_call_target="tpu_custom_call" | custom-call | flops 20000000000 | tf_op jit(solution)/shard_map/step_zero/pallas_call | solution.py:374
  15.2 0.0 collective-permute-done.2.table
  15.2 0.0 copy-done
  15.2 0.0 copy-done.4
  15.2 0.3 rows_ahead.1
  15.5 2.5 %collective-permute-start.9 = (bf16[8,8064]{1,0:T(8,128)(2,1)S(1)}, bf16[8,8064]{1,0:T(8,128)(2,1)S(1)}, u32[]{:S(2)}, u32[]{:S(2)}) collective-permute-start(bf16[8,8064]{1,0:T(8,128)(2,1)S(1)} %rows_ahead.1), channel_id=1, source_target_pairs={{0,24},{8,0},{16,8},{24,16},{1,25},{9,1},{17,9},{25,17},{2,26},{10... | collective-permute-start | bytes 387080 | tf_op jit(solution)/shard_map/ppermute | solution.py:335
  18.0 0.5 %collective-permute-start = (bf16[128,3840]{1,0:T(8,128)(2,1)S(1)}, bf16[128,3840]{1,0:T(8,128)(2,1)S(1)}, u32[]{:S(2)}, u32[]{:S(2)}) collective-permute-start(bf16[128,3840]{1,0:T(8,128)(2,1)S(1)} %bitcast.20), channel_id=1, source_target_pairs={{0,24},{8,0},{16,8},{24,16},{1,25},{9,1},{17,9},{25,17},{2,26},{10... | collective-permute-start | bytes 2949128 | tf_op jit(solution)/shard_map/ppermute | solution.py:335
  18.6 3.4 %collective-permute-done.9.came.refs_2_.refs_0_ = bf16[8,8064]{1,0:T(8,128)(2,1)S(1)} collective-permute-done((bf16[8,8064]{1,0:T(8,128)(2,1)S(1)}, bf16[8,8064]{1,0:T(8,128)(2,1)S(1)}, u32[]{:S(2)}, u32[]{:S(2)}) %collective-permute-start.9) | collective-permute-done | bytes 129056 | tf_op jit(solution)/shard_map/ppermute | solution.py:335
  22.0 1.9 %collective-permute-start.10 = (bf16[8,4864]{1,0:T(8,128)(2,1)S(1)}, bf16[8,4864]{1,0:T(8,128)(2,1)S(1)}, u32[]{:S(2)}, u32[]{:S(2)}) collective-permute-start(bf16[8,4864]{1,0:T(8,128)(2,1)S(1)} %get-tuple-element.46), channel_id=1, source_target_pairs={{0,2},{1,3},{2,0},{3,1},{4,6},{5,7},{6,4},{7,5},{8,10},{9,11},{10,... | collective-permute-start | bytes 233480 | tf_op jit(solution)/shard_map/ppermute | solution.py:328
  23.9 1.1 %collective-permute-start.11 = (bf16[8,4864]{1,0:T(8,128)(2,1)S(1)}, bf16[8,4864]{1,0:T(8,128)(2,1)S(1)}, u32[]{:S(2)}, u32[]{:S(2)}) collective-permute-start(bf16[8,4864]{1,0:T(8,128)(2,1)S(1)} %get-tuple-element.47), channel_id=1, source_target_pairs={{0,4},{1,5},{2,6},{3,7},{4,0},{5,1},{6,2},{7,3},{8,12},{9,13},{10,... | collective-permute-start | bytes 233480 | tf_op jit(solution)/shard_map/ppermute | solution.py:328
  25.0 1.4 %collective-permute-start.12 = (bf16[8,4864]{1,0:T(8,128)(2,1)S(1)}, bf16[8,4864]{1,0:T(8,128)(2,1)S(1)}, u32[]{:S(2)}, u32[]{:S(2)}) collective-permute-start(bf16[8,4864]{1,0:T(8,128)(2,1)S(1)} %get-tuple-element.48), channel_id=1, source_target_pairs={{0,6},{1,7},{2,4},{3,5},{4,2},{5,3},{6,0},{7,1},{8,14},{9,15},{10,... | collective-permute-start | bytes 233480 | tf_op jit(solution)/shard_map/ppermute | solution.py:328
  26.4 0.0 collective-permute-done.10.refs_3_.refs_1_
  26.4 3.2 %collective-permute-done.11.refs_4_.refs_2_ = bf16[8,4864]{1,0:T(8,128)(2,1)S(1)} collective-permute-done((bf16[8,4864]{1,0:T(8,128)(2,1)S(1)}, bf16[8,4864]{1,0:T(8,128)(2,1)S(1)}, u32[]{:S(2)}, u32[]{:S(2)}) %collective-permute-start.11) | collective-permute-done | bytes 77856 | tf_op jit(solution)/shard_map/ppermute | solution.py:328
  29.6 1.7 %collective-permute-done.12.refs_5_.refs_3_ = bf16[8,4864]{1,0:T(8,128)(2,1)S(1)} collective-permute-done((bf16[8,4864]{1,0:T(8,128)(2,1)S(1)}, bf16[8,4864]{1,0:T(8,128)(2,1)S(1)}, u32[]{:S(2)}, u32[]{:S(2)}) %collective-permute-start.12) | collective-permute-done | bytes 77856 | tf_op jit(solution)/shard_map/ppermute | solution.py:328
  31.3 2.1 %step_one.1 = (bf16[2,3968]{1,0:T(2,128)(2,1)S(1)}, bf16[2,3968]{1,0:T(2,128)(2,1)S(1)}, bf16[2,3968]{1,0:T(2,128)(2,1)S(1)}, bf16[2,3968]{1,0:T(2,128)(2,1)S(1)}) custom-call(bf16[8,8064]{1,0:T(8,128)(2,1)S(1)} %collective-permute-done.9.came.refs_2_.refs_0_, bf16[8,4864]{1,0:T(8,128)(2,1)S(1)} %collective-permute-done.10.refs_3_.refs_1_, ...), custom_call_target="tpu_custom_call" | custom-call | tf_op jit(solution)/shard_map/step_one/pallas_call | solution.py:397
  33.4 0.0 collective-permute-start.13
  33.5 2.0 %collective-permute-start.14 = (bf16[2,3968]{1,0:T(2,128)(2,1)S(1)}, bf16[2,3968]{1,0:T(2,128)(2,1)S(1)}, u32[]{:S(2)}, u32[]{:S(2)}) collective-permute-start(bf16[2,3968]{1,0:T(2,128)(2,1)S(1)} %get-tuple-element.54), channel_id=1, source_target_pairs={{0,4},{1,5},{2,6},{3,7},{4,0},{5,1},{6,2},{7,3},{8,12},{9,13},{10,... | collective-permute-start | bytes 47624 | tf_op jit(solution)/shard_map/ppermute | solution.py:328
  35.5 2.4 %collective-permute-start.15 = (bf16[2,3968]{1,0:T(2,128)(2,1)S(1)}, bf16[2,3968]{1,0:T(2,128)(2,1)S(1)}, u32[]{:S(2)}, u32[]{:S(2)}) collective-permute-start(bf16[2,3968]{1,0:T(2,128)(2,1)S(1)} %get-tuple-element.55), channel_id=1, source_target_pairs={{0,6},{1,7},{2,4},{3,5},{4,2},{5,3},{6,0},{7,1},{8,14},{9,15},{10,... | collective-permute-start | bytes 47624 | tf_op jit(solution)/shard_map/ppermute | solution.py:328
  37.9 3.5 %collective-permute-done.refs_0_ = bf16[128,3840]{1,0:T(8,128)(2,1)S(1)} collective-permute-done((bf16[128,3840]{1,0:T(8,128)(2,1)S(1)}, bf16[128,3840]{1,0:T(8,128)(2,1)S(1)}, u32[]{:S(2)}, u32[]{:S(2)}) %collective-permute-start) | collective-permute-done | bytes 983072 | tf_op jit(solution)/shard_map/ppermute | solution.py:335
  41.3 0.0 collective-permute-done.13.refs_6_
  41.4 0.0 collective-permute-done.14.refs_7_
  41.4 0.0 collective-permute-done.15.refs_8_
  41.4 1.4 %final_sums.1 = (bf16[128,3840]{1,0:T(8,128)(2,1)}, f32[2,2,128]{2,1,0:T(2,128)}) custom-call(bf16[128,3840]{1,0:T(8,128)(2,1)S(1)} %collective-permute-done.refs_0_, f32[8,3840]{1,0:T(8,128)S(1)} %get-tuple-element.49.refs_1_, bf16[16,128]{1,0:T(8,128)(2,1)S(1)} %get-tuple-element.50.refs_2_, s32[2,2,128]{2,1,0:T(2,128)S(1)} %bitcast.33, ...), custom_call_target="tpu_custom_call" | custom-call | tf_op jit(solution)/shard_map/final_sums/pallas_call | solution.py:415
  (6 shorter events, 0.1 us)
Async XLA Ops:
  0.6 2.2 %copy-start.2 = (bf16[1,3840,128]{2,1,0:T(8,128)(2,1)S(1)}, bf16[1,3840,128]{2,1,0:T(8,128)(2,1)}, u32[]{:S(2)}) copy-start(bf16[1,3840,128]{2,1,0:T(8,128)(2,1)} %param.13) | copy-start | bytes 2949124
  0.6 7.8 %collective-permute-start.5 = (bf16[128,3840]{1,0:T(8,128)(2,1)}, bf16[128,3840]{1,0:T(8,128)(2,1)S(1)}, u32[]{:S(2)}, u32[]{:S(2)}) collective-permute-start(bf16[128,3840]{1,0:T(8,128)(2,1)} %bitcast.21), channel_id=1, source_target_pairs={{0,1},{1,0},{2,3},{3,2},{4,5},{5,4},{6,7},{7,6},{8,9},{9,8},{10,11... | collective-permute-start | bytes 2949128 | tf_op jit(solution)/shard_map/ppermute | solution.py:323
  1.2 7.3 %collective-permute-start.3 = (bf16[2,16,2,128]{3,2,1,0:T(2,128)(2,1)}, bf16[2,16,2,128]{3,2,1,0:T(2,128)(2,1)S(1)}, u32[]{:S(2)}, u32[]{:S(2)}) collective-permute-start(bf16[2,16,2,128]{3,2,1,0:T(2,128)(2,1)} %bitcast.38), channel_id=1, source_target_pairs={{0,1},{1,0},{2,3},{3,2},{4,5},{5,4},{6,7},{7,6},{8,9},{9,8},{10,11... | collective-permute-start | bytes 49160 | tf_op jit(solution)/shard_map/ppermute | solution.py:323
  1.2 7.9 %copy-start.6 = (bf16[1,2,16,2,128]{4,3,2,1,0:T(2,128)(2,1)S(1)}, bf16[1,2,16,2,128]{4,3,2,1,0:T(2,128)(2,1)}, u32[]{:S(2)}) copy-start(bf16[1,2,16,2,128]{4,3,2,1,0:T(2,128)(2,1)} %param.12) | copy-start | bytes 49156
  2.8 6.5 %collective-permute-start.1 = (bf16[3840,128]{1,0:T(8,128)(2,1)S(1)}, bf16[3840,128]{1,0:T(8,128)(2,1)S(1)}, u32[]{:S(2)}, u32[]{:S(2)}) collective-permute-start(bf16[3840,128]{1,0:T(8,128)(2,1)S(1)} %bitcast.24), channel_id=1, source_target_pairs={{0,1},{1,0},{2,3},{3,2},{4,5},{5,4},{6,7},{7,6},{8,9},{9,8},{10,11... | collective-permute-start | bytes 2949128 | tf_op jit(solution)/shard_map/ppermute | solution.py:323
  3.3 8.8 %collective-permute-start.8 = (bf16[3840,128]{1,0:T(8,128)(2,1)}, bf16[3840,128]{1,0:T(8,128)(2,1)S(1)}, u32[]{:S(2)}, u32[]{:S(2)}) collective-permute-start(bf16[3840,128]{1,0:T(8,128)(2,1)} %bitcast.27), channel_id=1, source_target_pairs={{0,1},{1,0},{2,3},{3,2},{4,5},{5,4},{6,7},{7,6},{8,9},{9,8},{10,11... | collective-permute-start | bytes 2949128 | tf_op jit(solution)/shard_map/ppermute | solution.py:323
  3.4 7.6 %collective-permute-start.7 = (bf16[2,3968]{1,0:T(2,128)(2,1)S(1)}, bf16[2,3968]{1,0:T(2,128)(2,1)S(1)}, u32[]{:S(2)}, u32[]{:S(2)}) collective-permute-start(bf16[2,3968]{1,0:T(2,128)(2,1)S(1)} %get-tuple-element.39), channel_id=1, source_target_pairs={{0,6},{1,7},{2,4},{3,5},{4,2},{5,3},{6,0},{7,1},{8,14},{9,15},{10,... | collective-permute-start | bytes 47624 | tf_op jit(solution)/shard_map/ppermute | solution.py:328
  8.4 3.7 %collective-permute-start.4 = (bf16[2,3968]{1,0:T(2,128)(2,1)S(1)}, bf16[2,3968]{1,0:T(2,128)(2,1)S(1)}, u32[]{:S(2)}, u32[]{:S(2)}) collective-permute-start(bf16[2,3968]{1,0:T(2,128)(2,1)S(1)} %get-tuple-element.36), channel_id=1, source_target_pairs={{0,2},{1,3},{2,0},{3,1},{4,6},{5,7},{6,4},{7,5},{8,10},{9,11},{10,... | collective-permute-start | bytes 47624 | tf_op jit(solution)/shard_map/ppermute | solution.py:328
  8.4 4.8 %copy-start.1 = (bf16[1,128,3840]{2,1,0:T(8,128)(2,1)S(1)}, bf16[1,128,3840]{2,1,0:T(8,128)(2,1)}, u32[]{:S(2)}) copy-start(bf16[1,128,3840]{2,1,0:T(8,128)(2,1)} %param.15) | copy-start | bytes 2949124
  8.4 4.8 %copy-start.3 = (bf16[1,3840,128]{2,1,0:T(8,128)(2,1)S(1)}, bf16[1,3840,128]{2,1,0:T(8,128)(2,1)}, u32[]{:S(2)}) copy-start(bf16[1,3840,128]{2,1,0:T(8,128)(2,1)} %param.14) | copy-start | bytes 2949124
  8.4 4.8 %collective-permute-start.6 = (bf16[2,3968]{1,0:T(2,128)(2,1)S(1)}, bf16[2,3968]{1,0:T(2,128)(2,1)S(1)}, u32[]{:S(2)}, u32[]{:S(2)}) collective-permute-start(bf16[2,3968]{1,0:T(2,128)(2,1)S(1)} %get-tuple-element.38), channel_id=1, source_target_pairs={{0,4},{1,5},{2,6},{3,7},{4,0},{5,1},{6,2},{7,3},{8,12},{9,13},{10,... | collective-permute-start | bytes 47624 | tf_op jit(solution)/shard_map/ppermute | solution.py:328
  9.3 5.8 %copy-start = (bf16[1,128,3840]{2,1,0:T(8,128)(2,1)S(1)}, bf16[1,128,3840]{2,1,0:T(8,128)(2,1)}, u32[]{:S(2)}) copy-start(bf16[1,128,3840]{2,1,0:T(8,128)(2,1)} %param.8) | copy-start | bytes 2949124
  9.3 5.8 %collective-permute-start.2 = (f32[4,128]{1,0:T(4,128)S(1)}, f32[4,128]{1,0:T(4,128)S(1)}, u32[]{:S(2)}, u32[]{:S(2)}) collective-permute-start(f32[4,128]{1,0:T(4,128)S(1)} %get-tuple-element.33), channel_id=1, source_target_pairs={{0,8},{8,16},{16,24},{24,0},{1,9},{9,17},{17,25},{25,1},{2,10},{10... | collective-permute-start | bytes 6152 | tf_op jit(solution)/shard_map/ppermute | solution.py:335
  13.2 1.9 %copy-start.4 = (s32[1,2,128,2]{2,3,1,0:T(2,128)S(1)}, s32[1,2,128,2]{2,3,1,0:T(2,128)}, u32[]{:S(2)}) copy-start(s32[1,2,128,2]{2,3,1,0:T(2,128)} %param.9) | copy-start | bytes 6148
  13.2 1.9 %copy-start.5 = (s32[1,2,128,2]{2,3,1,0:T(2,128)S(1)}, s32[1,2,128,2]{2,3,1,0:T(2,128)}, u32[]{:S(2)}) copy-start(s32[1,2,128,2]{2,3,1,0:T(2,128)} %param.10) | copy-start | bytes 6148
  15.5 6.4 %collective-permute-start.9 = (bf16[8,8064]{1,0:T(8,128)(2,1)S(1)}, bf16[8,8064]{1,0:T(8,128)(2,1)S(1)}, u32[]{:S(2)}, u32[]{:S(2)}) collective-permute-start(bf16[8,8064]{1,0:T(8,128)(2,1)S(1)} %rows_ahead.1), channel_id=1, source_target_pairs={{0,24},{8,0},{16,8},{24,16},{1,25},{9,1},{17,9},{25,17},{2,26},{10... | collective-permute-start | bytes 387080 | tf_op jit(solution)/shard_map/ppermute | solution.py:335
  18.0 23.3 %collective-permute-start = (bf16[128,3840]{1,0:T(8,128)(2,1)S(1)}, bf16[128,3840]{1,0:T(8,128)(2,1)S(1)}, u32[]{:S(2)}, u32[]{:S(2)}) collective-permute-start(bf16[128,3840]{1,0:T(8,128)(2,1)S(1)} %bitcast.20), channel_id=1, source_target_pairs={{0,24},{8,0},{16,8},{24,16},{1,25},{9,1},{17,9},{25,17},{2,26},{10... | collective-permute-start | bytes 2949128 | tf_op jit(solution)/shard_map/ppermute | solution.py:335
  22.0 4.5 %collective-permute-start.10 = (bf16[8,4864]{1,0:T(8,128)(2,1)S(1)}, bf16[8,4864]{1,0:T(8,128)(2,1)S(1)}, u32[]{:S(2)}, u32[]{:S(2)}) collective-permute-start(bf16[8,4864]{1,0:T(8,128)(2,1)S(1)} %get-tuple-element.46), channel_id=1, source_target_pairs={{0,2},{1,3},{2,0},{3,1},{4,6},{5,7},{6,4},{7,5},{8,10},{9,11},{10,... | collective-permute-start | bytes 233480 | tf_op jit(solution)/shard_map/ppermute | solution.py:328
  23.9 5.7 %collective-permute-start.11 = (bf16[8,4864]{1,0:T(8,128)(2,1)S(1)}, bf16[8,4864]{1,0:T(8,128)(2,1)S(1)}, u32[]{:S(2)}, u32[]{:S(2)}) collective-permute-start(bf16[8,4864]{1,0:T(8,128)(2,1)S(1)} %get-tuple-element.47), channel_id=1, source_target_pairs={{0,4},{1,5},{2,6},{3,7},{4,0},{5,1},{6,2},{7,3},{8,12},{9,13},{10,... | collective-permute-start | bytes 233480 | tf_op jit(solution)/shard_map/ppermute | solution.py:328
  25.0 6.3 %collective-permute-start.12 = (bf16[8,4864]{1,0:T(8,128)(2,1)S(1)}, bf16[8,4864]{1,0:T(8,128)(2,1)S(1)}, u32[]{:S(2)}, u32[]{:S(2)}) collective-permute-start(bf16[8,4864]{1,0:T(8,128)(2,1)S(1)} %get-tuple-element.48), channel_id=1, source_target_pairs={{0,6},{1,7},{2,4},{3,5},{4,2},{5,3},{6,0},{7,1},{8,14},{9,15},{10,... | collective-permute-start | bytes 233480 | tf_op jit(solution)/shard_map/ppermute | solution.py:328
  33.4 7.9 %collective-permute-start.13 = (bf16[2,3968]{1,0:T(2,128)(2,1)S(1)}, bf16[2,3968]{1,0:T(2,128)(2,1)S(1)}, u32[]{:S(2)}, u32[]{:S(2)}) collective-permute-start(bf16[2,3968]{1,0:T(2,128)(2,1)S(1)} %get-tuple-element.53), channel_id=1, source_target_pairs={{0,2},{1,3},{2,0},{3,1},{4,6},{5,7},{6,4},{7,5},{8,10},{9,11},{10,... | collective-permute-start | bytes 47624 | tf_op jit(solution)/shard_map/ppermute | solution.py:328
  33.5 7.9 %collective-permute-start.14 = (bf16[2,3968]{1,0:T(2,128)(2,1)S(1)}, bf16[2,3968]{1,0:T(2,128)(2,1)S(1)}, u32[]{:S(2)}, u32[]{:S(2)}) collective-permute-start(bf16[2,3968]{1,0:T(2,128)(2,1)S(1)} %get-tuple-element.54), channel_id=1, source_target_pairs={{0,4},{1,5},{2,6},{3,7},{4,0},{5,1},{6,2},{7,3},{8,12},{9,13},{10,... | collective-permute-start | bytes 47624 | tf_op jit(solution)/shard_map/ppermute | solution.py:328
  35.5 5.9 %collective-permute-start.15 = (bf16[2,3968]{1,0:T(2,128)(2,1)S(1)}, bf16[2,3968]{1,0:T(2,128)(2,1)S(1)}, u32[]{:S(2)}, u32[]{:S(2)}) collective-permute-start(bf16[2,3968]{1,0:T(2,128)(2,1)S(1)} %get-tuple-element.55), channel_id=1, source_target_pairs={{0,6},{1,7},{2,4},{3,5},{4,2},{5,3},{6,0},{7,1},{8,14},{9,15},{10,... | collective-permute-start | bytes 47624 | tf_op jit(solution)/shard_map/ppermute | solution.py:328

commit v6 on v5

--- a/solution.py
+++ b/solution.py
@@ -12,9 +12,9 @@
 STEPS = 2
 PAIRS = E_FLY * MOST
 META = 128
-CHUNK = 256
+CHUNK = 384
 SPAN = 1024
-OUT = 1280
+OUT = 768
 COST0 = 20_000_000_000
 COST1 = 0
 COST2 = 20_000_000_000
@@ -278,16 +278,7 @@
     features = out.shape[1]
     label = labels(PAIRS, lambda k: z ^ k)
     take_rows(back_at, got)
-    meta = back_at[:, features:]
-    for step in range(STEPS):
-        first = 3 * (STEPS - 1 - step)
-        terms = meta[:, first:first + 1] + (meta[:, first + 1:first + 2] + meta[:, first + 2:first + 3])
-        for choice, hit in enumerate(hits(keys_of(routes, positions, step), label)):
-            prob_at[step, choice:choice + 1] = jnp.sum(
-                jnp.where(hit, terms, 0.0), axis=0, keepdims=True
-            )
-    copies = [pltpu.make_async_copy(prob_at, prob_out, sems.at[0])]
-    copies[0].start()
+    copies = []
     last = p == lax.axis_size("pipe") - 1
     for at in range(0, features, CHUNK):
         part = slice(at, at + CHUNK)
@@ -303,6 +294,16 @@
                 )
             )
             copies[-1].start()
+    meta = back_at[:, features:]
+    for step in range(STEPS):
+        first = 3 * (STEPS - 1 - step)
+        terms = meta[:, first:first + 1] + (meta[:, first + 1:first + 2] + meta[:, first + 2:first + 3])
+        for choice, hit in enumerate(hits(keys_of(routes, positions, step), label)):
+            prob_at[step, choice:choice + 1] = jnp.sum(
+                jnp.where(hit, terms, 0.0), axis=0, keepdims=True
+            )
+    copies.append(pltpu.make_async_copy(prob_at, prob_out, sems.at[len(copies)]))
+    copies[-1].start()
     for copy in copies:
         copy.wait()
 
@@ -393,7 +394,7 @@
     shifted, _ = lax.optimization_barrier((grad, across(terms0)))
     shifted = relay(shifted, -1)
     sends = call(merge_kernel, "merge", [wide] * (E_FLY - 1), operands=1, cost=COST2)(came)
-    came = [came] + [along(send, k + 1) for k, send in enumerate(sends)]
+    came = along_all([came, *sends])
     back = call(
         step_one_kernel,
         "step_one",

time: 42.9 us -> 42.8 us (level)
  transfers between devices with their start and end apart: 16 -> 16, of which waited for: 6 -> 6; matrix products, arithmetic and copies ran while one was open for 0% -> 0% of each run, Pallas kernels for 14% -> 13%
where the time goes in v6:
time: 42.8 us; the launch traced here: 42.6 us
  starting transfers between devices  20.4 us (48%)
  waiting for transfers between devices  14.1 us (33%)
  Pallas kernels  7.34 us (17%)
  between operations  0.76 us (2%)
    ppermute x9, starting transfers between devices, along(): lax.ppermute(block, 'expert', [(i, i ^ 2 * k) for i in range(devices)])  14.6 us
    ppermute x9, waiting for transfers between devices, along(): lax.ppermute(block, 'expert', [(i, i ^ 2 * k) for i in range(devices)])  7.21 us
    ppermute x3, waiting for transfers between devices, relay(): return lax.ppermute(block, 'pipe', route)  6.84 us
    ppermute x3, starting transfers between devices, relay(): return lax.ppermute(block, 'pipe', route)  4.66 us
    pallas_call x1, Pallas kernels, local_chip(): call(step_one_kernel, 'step_one', [pair] * E_FLY, [pltpu.VMEM((PAIRS, pie...  2.06 us
    pallas_call x1, Pallas kernels, local_chip(): call(step_zero_kernel, 'step_zero', [jax.ShapeDtypeStruct((PAIRS, feature...  1.88 us
    pallas_call x1, Pallas kernels, local_chip(): call(pick_kernel, 'pick_rows', [pltpu.VMEM(pair.shape, BF16)] * E_FLY + [...  1.55 us
    pallas_call x1, Pallas kernels, local_chip(): call(final_kernel, 'final_sums', [jax.ShapeDtypeStruct((tokens, features)...  1.26 us
  transfers between devices with their start and end apart: 16, of which 6 were waited for; matrix products, arithmetic and copies ran while one was open for 0% of the time, Pallas kernels for 13%

profile of v6, /device:TPU:0, one launch (start us, length us, event | category | flops | bytes accessed | tf_op | source)
XLA Modules:
  0.0 42.6 jit_solution(5094290143134469784)
XLA Ops:
  0.6 0.0 copy-start.2
  0.6 0.5 %collective-permute-start.5 = (bf16[128,3840]{1,0:T(8,128)(2,1)}, bf16[128,3840]{1,0:T(8,128)(2,1)S(1)}, u32[]{:S(2)}, u32[]{:S(2)}) collective-permute-start(bf16[128,3840]{1,0:T(8,128)(2,1)} %bitcast.21), channel_id=1, source_target_pairs={{0,1},{1,0},{2,3},{3,2},{4,5},{5,4},{6,7},{7,6},{8,9},{9,8},{10,11... | collective-permute-start | bytes 2949128 | tf_op jit(solution)/shard_map/ppermute | solution.py:324
  1.2 0.1 collective-permute-start.3
  1.2 1.5 %pick_rows.1 = (bf16[2,3968]{1,0:T(2,128)(2,1)S(1)}, bf16[2,3968]{1,0:T(2,128)(2,1)S(1)}, bf16[2,3968]{1,0:T(2,128)(2,1)S(1)}, bf16[2,3968]{1,0:T(2,128)(2,1)S(1)}, f32[4,128]{1,0:T(4,128)S(1)}) custom-call(s32[2,2,128]{2,1,0:T(2,128)} %bitcast.30, s32[2,2,128]{2,1,0:T(2,128)} %bitcast.34, bf16[2,2,128]{2,1,0:T(2,128)(2,1)} %bitcast.40, ...), custom_call_target="tpu_custom_call" | custom-call | tf_op jit(solution)/shard_map/pick_rows/pallas_call | solution.py:348
  2.8 0.0 copy-done.2
  2.8 0.5 %collective-permute-start.1 = (bf16[3840,128]{1,0:T(8,128)(2,1)S(1)}, bf16[3840,128]{1,0:T(8,128)(2,1)S(1)}, u32[]{:S(2)}, u32[]{:S(2)}) collective-permute-start(bf16[3840,128]{1,0:T(8,128)(2,1)S(1)} %bitcast.24), channel_id=1, source_target_pairs={{0,1},{1,0},{2,3},{3,2},{4,5},{5,4},{6,7},{7,6},{8,9},{9,8},{10,11... | collective-permute-start | bytes 2949128 | tf_op jit(solution)/shard_map/ppermute | solution.py:324
  3.3 0.1 collective-permute-start.8
  3.4 5.0 %collective-permute-start.7 = (bf16[2,3968]{1,0:T(2,128)(2,1)S(1)}, bf16[2,3968]{1,0:T(2,128)(2,1)S(1)}, u32[]{:S(2)}, u32[]{:S(2)}) collective-permute-start(bf16[2,3968]{1,0:T(2,128)(2,1)S(1)} %get-tuple-element.39), channel_id=1, source_target_pairs={{0,6},{1,7},{2,4},{3,5},{4,2},{5,3},{6,0},{7,1},{8,14},{9,15},{10,... | collective-permute-start | bytes 47624 | tf_op jit(solution)/shard_map/ppermute | solution.py:329
  8.4 0.0 collective-permute-done.3.acts_other
  8.4 0.0 collective-permute-start.4
  8.4 0.0 collective-permute-done.5.refs_6_.refs_7_
  8.4 0.0 copy-start.1
  8.4 0.0 copy-start.3
  8.4 0.7 %collective-permute-start.6 = (bf16[2,3968]{1,0:T(2,128)(2,1)S(1)}, bf16[2,3968]{1,0:T(2,128)(2,1)S(1)}, u32[]{:S(2)}, u32[]{:S(2)}) collective-permute-start(bf16[2,3968]{1,0:T(2,128)(2,1)S(1)} %get-tuple-element.38), channel_id=1, source_target_pairs={{0,4},{1,5},{2,6},{3,7},{4,0},{5,1},{6,2},{7,3},{8,12},{9,13},{10,... | collective-permute-start | bytes 47624 | tf_op jit(solution)/shard_map/ppermute | solution.py:329
  9.1 0.0 copy-done.6
  9.1 0.2 factors.1.refs_4_
  9.3 0.0 collective-permute-done.1.refs_8_.refs_9_
  9.3 0.0 copy-start
  9.3 1.6 %collective-permute-start.2 = (f32[4,128]{1,0:T(4,128)S(1)}, f32[4,128]{1,0:T(4,128)S(1)}, u32[]{:S(2)}, u32[]{:S(2)}) collective-permute-start(f32[4,128]{1,0:T(4,128)S(1)} %get-tuple-element.33), channel_id=1, source_target_pairs={{0,8},{8,16},{16,24},{24,0},{1,9},{9,17},{17,25},{25,1},{2,10},{10... | collective-permute-start | bytes 6152 | tf_op jit(solution)/shard_map/ppermute | solution.py:336
  11.0 0.0 collective-permute-done.7.refs_3_
  11.0 1.2 %collective-permute-done.4.refs_1_ = bf16[2,3968]{1,0:T(2,128)(2,1)S(1)} collective-permute-done((bf16[2,3968]{1,0:T(2,128)(2,1)S(1)}, bf16[2,3968]{1,0:T(2,128)(2,1)S(1)}, u32[]{:S(2)}, u32[]{:S(2)}) %collective-permute-start.4) | collective-permute-done | bytes 15904 | tf_op jit(solution)/shard_map/ppermute | solution.py:329
  12.1 0.0 collective-permute-done.8.refs_10_.refs_11_
  12.2 1.1 %collective-permute-done.6.refs_2_ = bf16[2,3968]{1,0:T(2,128)(2,1)S(1)} collective-permute-done((bf16[2,3968]{1,0:T(2,128)(2,1)S(1)}, bf16[2,3968]{1,0:T(2,128)(2,1)S(1)}, u32[]{:S(2)}, u32[]{:S(2)}) %collective-permute-start.6) | collective-permute-done | bytes 15904 | tf_op jit(solution)/shard_map/ppermute | solution.py:329
  13.2 0.0 copy-done.1
  13.2 0.0 copy-done.3
  13.3 1.9 %step_zero.1 = (bf16[8,3840]{1,0:T(8,128)(2,1)S(1)}, f32[8,128]{1,0:T(8,128)S(1)}) custom-call(bf16[2,3968]{1,0:T(2,128)(2,1)S(1)} %get-tuple-element.34.refs_0_, bf16[2,3968]{1,0:T(2,128)(2,1)S(1)} %collective-permute-done.4.refs_1_, bf16[2,3968]{1,0:T(2,128)(2,1)S(1)} %collective-permute-done.6.refs_2_, ...), custom_call_target="tpu_custom_call" | custom-call | flops 20000000000 | tf_op jit(solution)/shard_map/step_zero/pallas_call | solution.py:375
  15.1 0.0 collective-permute-done.2.table
  15.1 0.0 copy-done
  15.1 0.0 copy-done.4
  15.2 0.3 rows_ahead.1
  15.5 2.5 %collective-permute-start.9 = (bf16[8,8064]{1,0:T(8,128)(2,1)S(1)}, bf16[8,8064]{1,0:T(8,128)(2,1)S(1)}, u32[]{:S(2)}, u32[]{:S(2)}) collective-permute-start(bf16[8,8064]{1,0:T(8,128)(2,1)S(1)} %rows_ahead.1), channel_id=1, source_target_pairs={{0,24},{8,0},{16,8},{24,16},{1,25},{9,1},{17,9},{25,17},{2,26},{10... | collective-permute-start | bytes 387080 | tf_op jit(solution)/shard_map/ppermute | solution.py:336
  18.0 0.5 %collective-permute-start = (bf16[128,3840]{1,0:T(8,128)(2,1)S(1)}, bf16[128,3840]{1,0:T(8,128)(2,1)S(1)}, u32[]{:S(2)}, u32[]{:S(2)}) collective-permute-start(bf16[128,3840]{1,0:T(8,128)(2,1)S(1)} %bitcast.20), channel_id=1, source_target_pairs={{0,24},{8,0},{16,8},{24,16},{1,25},{9,1},{17,9},{25,17},{2,26},{10... | collective-permute-start | bytes 2949128 | tf_op jit(solution)/shard_map/ppermute | solution.py:336
  18.6 3.4 %collective-permute-done.9.came.refs_2_.refs_0_ = bf16[8,8064]{1,0:T(8,128)(2,1)S(1)} collective-permute-done((bf16[8,8064]{1,0:T(8,128)(2,1)S(1)}, bf16[8,8064]{1,0:T(8,128)(2,1)S(1)}, u32[]{:S(2)}, u32[]{:S(2)}) %collective-permute-start.9) | collective-permute-done | bytes 129056 | tf_op jit(solution)/shard_map/ppermute | solution.py:336
  22.0 1.9 %collective-permute-start.10 = (bf16[8,4864]{1,0:T(8,128)(2,1)S(1)}, bf16[8,4864]{1,0:T(8,128)(2,1)S(1)}, u32[]{:S(2)}, u32[]{:S(2)}) collective-permute-start(bf16[8,4864]{1,0:T(8,128)(2,1)S(1)} %get-tuple-element.46), channel_id=1, source_target_pairs={{0,2},{1,3},{2,0},{3,1},{4,6},{5,7},{6,4},{7,5},{8,10},{9,11},{10,... | collective-permute-start | bytes 233480 | tf_op jit(solution)/shard_map/ppermute | solution.py:329
  23.9 1.1 %collective-permute-start.11 = (bf16[8,4864]{1,0:T(8,128)(2,1)S(1)}, bf16[8,4864]{1,0:T(8,128)(2,1)S(1)}, u32[]{:S(2)}, u32[]{:S(2)}) collective-permute-start(bf16[8,4864]{1,0:T(8,128)(2,1)S(1)} %get-tuple-element.47), channel_id=1, source_target_pairs={{0,4},{1,5},{2,6},{3,7},{4,0},{5,1},{6,2},{7,3},{8,12},{9,13},{10,... | collective-permute-start | bytes 233480 | tf_op jit(solution)/shard_map/ppermute | solution.py:329
  25.0 1.4 %collective-permute-start.12 = (bf16[8,4864]{1,0:T(8,128)(2,1)S(1)}, bf16[8,4864]{1,0:T(8,128)(2,1)S(1)}, u32[]{:S(2)}, u32[]{:S(2)}) collective-permute-start(bf16[8,4864]{1,0:T(8,128)(2,1)S(1)} %get-tuple-element.48), channel_id=1, source_target_pairs={{0,6},{1,7},{2,4},{3,5},{4,2},{5,3},{6,0},{7,1},{8,14},{9,15},{10,... | collective-permute-start | bytes 233480 | tf_op jit(solution)/shard_map/ppermute | solution.py:329
  26.4 0.0 collective-permute-done.10.refs_3_.refs_1_
  26.4 3.2 %collective-permute-done.11.refs_4_.refs_2_ = bf16[8,4864]{1,0:T(8,128)(2,1)S(1)} collective-permute-done((bf16[8,4864]{1,0:T(8,128)(2,1)S(1)}, bf16[8,4864]{1,0:T(8,128)(2,1)S(1)}, u32[]{:S(2)}, u32[]{:S(2)}) %collective-permute-start.11) | collective-permute-done | bytes 77856 | tf_op jit(solution)/shard_map/ppermute | solution.py:329
  29.6 1.7 %collective-permute-done.12.refs_5_.refs_3_ = bf16[8,4864]{1,0:T(8,128)(2,1)S(1)} collective-permute-done((bf16[8,4864]{1,0:T(8,128)(2,1)S(1)}, bf16[8,4864]{1,0:T(8,128)(2,1)S(1)}, u32[]{:S(2)}, u32[]{:S(2)}) %collective-permute-start.12) | collective-permute-done | bytes 77856 | tf_op jit(solution)/shard_map/ppermute | solution.py:329
  31.3 2.1 %step_one.1 = (bf16[2,3968]{1,0:T(2,128)(2,1)S(1)}, bf16[2,3968]{1,0:T(2,128)(2,1)S(1)}, bf16[2,3968]{1,0:T(2,128)(2,1)S(1)}, bf16[2,3968]{1,0:T(2,128)(2,1)S(1)}) custom-call(bf16[8,8064]{1,0:T(8,128)(2,1)S(1)} %collective-permute-done.9.came.refs_2_.refs_0_, bf16[8,4864]{1,0:T(8,128)(2,1)S(1)} %collective-permute-done.10.refs_3_.refs_1_, ...), custom_call_target="tpu_custom_call" | custom-call | tf_op jit(solution)/shard_map/step_one/pallas_call | solution.py:398
  33.4 0.0 collective-permute-start.13
  33.5 2.0 %collective-permute-start.14 = (bf16[2,3968]{1,0:T(2,128)(2,1)S(1)}, bf16[2,3968]{1,0:T(2,128)(2,1)S(1)}, u32[]{:S(2)}, u32[]{:S(2)}) collective-permute-start(bf16[2,3968]{1,0:T(2,128)(2,1)S(1)} %get-tuple-element.54), channel_id=1, source_target_pairs={{0,4},{1,5},{2,6},{3,7},{4,0},{5,1},{6,2},{7,3},{8,12},{9,13},{10,... | collective-permute-start | bytes 47624 | tf_op jit(solution)/shard_map/ppermute | solution.py:329
  35.5 2.4 %collective-permute-start.15 = (bf16[2,3968]{1,0:T(2,128)(2,1)S(1)}, bf16[2,3968]{1,0:T(2,128)(2,1)S(1)}, u32[]{:S(2)}, u32[]{:S(2)}) collective-permute-start(bf16[2,3968]{1,0:T(2,128)(2,1)S(1)} %get-tuple-element.55), channel_id=1, source_target_pairs={{0,6},{1,7},{2,4},{3,5},{4,2},{5,3},{6,0},{7,1},{8,14},{9,15},{10,... | collective-permute-start | bytes 47624 | tf_op jit(solution)/shard_map/ppermute | solution.py:329
  37.9 3.5 %collective-permute-done.refs_0_ = bf16[128,3840]{1,0:T(8,128)(2,1)S(1)} collective-permute-done((bf16[128,3840]{1,0:T(8,128)(2,1)S(1)}, bf16[128,3840]{1,0:T(8,128)(2,1)S(1)}, u32[]{:S(2)}, u32[]{:S(2)}) %collective-permute-start) | collective-permute-done | bytes 983072 | tf_op jit(solution)/shard_map/ppermute | solution.py:336
  41.3 0.0 collective-permute-done.13.refs_6_
  41.3 0.0 collective-permute-done.14.refs_7_
  41.3 0.0 collective-permute-done.15.refs_8_
  41.4 1.3 %final_sums.1 = (bf16[128,3840]{1,0:T(8,128)(2,1)}, f32[2,2,128]{2,1,0:T(2,128)}) custom-call(bf16[128,3840]{1,0:T(8,128)(2,1)S(1)} %collective-permute-done.refs_0_, f32[8,3840]{1,0:T(8,128)S(1)} %get-tuple-element.49.refs_1_, bf16[16,128]{1,0:T(8,128)(2,1)S(1)} %get-tuple-element.50.refs_2_, s32[2,2,128]{2,1,0:T(2,128)S(1)} %bitcast.33, ...), custom_call_target="tpu_custom_call" | custom-call | tf_op jit(solution)/shard_map/final_sums/pallas_call | solution.py:416
  (6 shorter events, 0.1 us)
Async XLA Ops:
  0.6 2.2 %copy-start.2 = (bf16[1,3840,128]{2,1,0:T(8,128)(2,1)S(1)}, bf16[1,3840,128]{2,1,0:T(8,128)(2,1)}, u32[]{:S(2)}) copy-start(bf16[1,3840,128]{2,1,0:T(8,128)(2,1)} %param.13) | copy-start | bytes 2949124
  0.6 7.8 %collective-permute-start.5 = (bf16[128,3840]{1,0:T(8,128)(2,1)}, bf16[128,3840]{1,0:T(8,128)(2,1)S(1)}, u32[]{:S(2)}, u32[]{:S(2)}) collective-permute-start(bf16[128,3840]{1,0:T(8,128)(2,1)} %bitcast.21), channel_id=1, source_target_pairs={{0,1},{1,0},{2,3},{3,2},{4,5},{5,4},{6,7},{7,6},{8,9},{9,8},{10,11... | collective-permute-start | bytes 2949128 | tf_op jit(solution)/shard_map/ppermute | solution.py:324
  1.2 7.3 %collective-permute-start.3 = (bf16[2,16,2,128]{3,2,1,0:T(2,128)(2,1)}, bf16[2,16,2,128]{3,2,1,0:T(2,128)(2,1)S(1)}, u32[]{:S(2)}, u32[]{:S(2)}) collective-permute-start(bf16[2,16,2,128]{3,2,1,0:T(2,128)(2,1)} %bitcast.38), channel_id=1, source_target_pairs={{0,1},{1,0},{2,3},{3,2},{4,5},{5,4},{6,7},{7,6},{8,9},{9,8},{10,11... | collective-permute-start | bytes 49160 | tf_op jit(solution)/shard_map/ppermute | solution.py:324
  1.2 7.9 %copy-start.6 = (bf16[1,2,16,2,128]{4,3,2,1,0:T(2,128)(2,1)S(1)}, bf16[1,2,16,2,128]{4,3,2,1,0:T(2,128)(2,1)}, u32[]{:S(2)}) copy-start(bf16[1,2,16,2,128]{4,3,2,1,0:T(2,128)(2,1)} %param.12) | copy-start | bytes 49156
  2.8 6.5 %collective-permute-start.1 = (bf16[3840,128]{1,0:T(8,128)(2,1)S(1)}, bf16[3840,128]{1,0:T(8,128)(2,1)S(1)}, u32[]{:S(2)}, u32[]{:S(2)}) collective-permute-start(bf16[3840,128]{1,0:T(8,128)(2,1)S(1)} %bitcast.24), channel_id=1, source_target_pairs={{0,1},{1,0},{2,3},{3,2},{4,5},{5,4},{6,7},{7,6},{8,9},{9,8},{10,11... | collective-permute-start | bytes 2949128 | tf_op jit(solution)/shard_map/ppermute | solution.py:324
  3.3 8.8 %collective-permute-start.8 = (bf16[3840,128]{1,0:T(8,128)(2,1)}, bf16[3840,128]{1,0:T(8,128)(2,1)S(1)}, u32[]{:S(2)}, u32[]{:S(2)}) collective-permute-start(bf16[3840,128]{1,0:T(8,128)(2,1)} %bitcast.27), channel_id=1, source_target_pairs={{0,1},{1,0},{2,3},{3,2},{4,5},{5,4},{6,7},{7,6},{8,9},{9,8},{10,11... | collective-permute-start | bytes 2949128 | tf_op jit(solution)/shard_map/ppermute | solution.py:324
  3.4 7.6 %collective-permute-start.7 = (bf16[2,3968]{1,0:T(2,128)(2,1)S(1)}, bf16[2,3968]{1,0:T(2,128)(2,1)S(1)}, u32[]{:S(2)}, u32[]{:S(2)}) collective-permute-start(bf16[2,3968]{1,0:T(2,128)(2,1)S(1)} %get-tuple-element.39), channel_id=1, source_target_pairs={{0,6},{1,7},{2,4},{3,5},{4,2},{5,3},{6,0},{7,1},{8,14},{9,15},{10,... | collective-permute-start | bytes 47624 | tf_op jit(solution)/shard_map/ppermute | solution.py:329
  8.4 3.7 %collective-permute-start.4 = (bf16[2,3968]{1,0:T(2,128)(2,1)S(1)}, bf16[2,3968]{1,0:T(2,128)(2,1)S(1)}, u32[]{:S(2)}, u32[]{:S(2)}) collective-permute-start(bf16[2,3968]{1,0:T(2,128)(2,1)S(1)} %get-tuple-element.36), channel_id=1, source_target_pairs={{0,2},{1,3},{2,0},{3,1},{4,6},{5,7},{6,4},{7,5},{8,10},{9,11},{10,... | collective-permute-start | bytes 47624 | tf_op jit(solution)/shard_map/ppermute | solution.py:329
  8.4 4.8 %copy-start.1 = (bf16[1,128,3840]{2,1,0:T(8,128)(2,1)S(1)}, bf16[1,128,3840]{2,1,0:T(8,128)(2,1)}, u32[]{:S(2)}) copy-start(bf16[1,128,3840]{2,1,0:T(8,128)(2,1)} %param.15) | copy-start | bytes 2949124
  8.4 4.8 %copy-start.3 = (bf16[1,3840,128]{2,1,0:T(8,128)(2,1)S(1)}, bf16[1,3840,128]{2,1,0:T(8,128)(2,1)}, u32[]{:S(2)}) copy-start(bf16[1,3840,128]{2,1,0:T(8,128)(2,1)} %param.14) | copy-start | bytes 2949124
  8.4 4.8 %collective-permute-start.6 = (bf16[2,3968]{1,0:T(2,128)(2,1)S(1)}, bf16[2,3968]{1,0:T(2,128)(2,1)S(1)}, u32[]{:S(2)}, u32[]{:S(2)}) collective-permute-start(bf16[2,3968]{1,0:T(2,128)(2,1)S(1)} %get-tuple-element.38), channel_id=1, source_target_pairs={{0,4},{1,5},{2,6},{3,7},{4,0},{5,1},{6,2},{7,3},{8,12},{9,13},{10,... | collective-permute-start | bytes 47624 | tf_op jit(solution)/shard_map/ppermute | solution.py:329
  9.3 5.8 %copy-start = (bf16[1,128,3840]{2,1,0:T(8,128)(2,1)S(1)}, bf16[1,128,3840]{2,1,0:T(8,128)(2,1)}, u32[]{:S(2)}) copy-start(bf16[1,128,3840]{2,1,0:T(8,128)(2,1)} %param.8) | copy-start | bytes 2949124
  9.3 5.8 %collective-permute-start.2 = (f32[4,128]{1,0:T(4,128)S(1)}, f32[4,128]{1,0:T(4,128)S(1)}, u32[]{:S(2)}, u32[]{:S(2)}) collective-permute-start(f32[4,128]{1,0:T(4,128)S(1)} %get-tuple-element.33), channel_id=1, source_target_pairs={{0,8},{8,16},{16,24},{24,0},{1,9},{9,17},{17,25},{25,1},{2,10},{10... | collective-permute-start | bytes 6152 | tf_op jit(solution)/shard_map/ppermute | solution.py:336
  13.2 1.9 %copy-start.4 = (s32[1,2,128,2]{2,3,1,0:T(2,128)S(1)}, s32[1,2,128,2]{2,3,1,0:T(2,128)}, u32[]{:S(2)}) copy-start(s32[1,2,128,2]{2,3,1,0:T(2,128)} %param.9) | copy-start | bytes 6148
  13.2 1.9 %copy-start.5 = (s32[1,2,128,2]{2,3,1,0:T(2,128)S(1)}, s32[1,2,128,2]{2,3,1,0:T(2,128)}, u32[]{:S(2)}) copy-start(s32[1,2,128,2]{2,3,1,0:T(2,128)} %param.10) | copy-start | bytes 6148
  15.5 6.4 %collective-permute-start.9 = (bf16[8,8064]{1,0:T(8,128)(2,1)S(1)}, bf16[8,8064]{1,0:T(8,128)(2,1)S(1)}, u32[]{:S(2)}, u32[]{:S(2)}) collective-permute-start(bf16[8,8064]{1,0:T(8,128)(2,1)S(1)} %rows_ahead.1), channel_id=1, source_target_pairs={{0,24},{8,0},{16,8},{24,16},{1,25},{9,1},{17,9},{25,17},{2,26},{10... | collective-permute-start | bytes 387080 | tf_op jit(solution)/shard_map/ppermute | solution.py:336
  18.0 23.3 %collective-permute-start = (bf16[128,3840]{1,0:T(8,128)(2,1)S(1)}, bf16[128,3840]{1,0:T(8,128)(2,1)S(1)}, u32[]{:S(2)}, u32[]{:S(2)}) collective-permute-start(bf16[128,3840]{1,0:T(8,128)(2,1)S(1)} %bitcast.20), channel_id=1, source_target_pairs={{0,24},{8,0},{16,8},{24,16},{1,25},{9,1},{17,9},{25,17},{2,26},{10... | collective-permute-start | bytes 2949128 | tf_op jit(solution)/shard_map/ppermute | solution.py:336
  22.0 4.5 %collective-permute-start.10 = (bf16[8,4864]{1,0:T(8,128)(2,1)S(1)}, bf16[8,4864]{1,0:T(8,128)(2,1)S(1)}, u32[]{:S(2)}, u32[]{:S(2)}) collective-permute-start(bf16[8,4864]{1,0:T(8,128)(2,1)S(1)} %get-tuple-element.46), channel_id=1, source_target_pairs={{0,2},{1,3},{2,0},{3,1},{4,6},{5,7},{6,4},{7,5},{8,10},{9,11},{10,... | collective-permute-start | bytes 233480 | tf_op jit(solution)/shard_map/ppermute | solution.py:329
  23.9 5.8 %collective-permute-start.11 = (bf16[8,4864]{1,0:T(8,128)(2,1)S(1)}, bf16[8,4864]{1,0:T(8,128)(2,1)S(1)}, u32[]{:S(2)}, u32[]{:S(2)}) collective-permute-start(bf16[8,4864]{1,0:T(8,128)(2,1)S(1)} %get-tuple-element.47), channel_id=1, source_target_pairs={{0,4},{1,5},{2,6},{3,7},{4,0},{5,1},{6,2},{7,3},{8,12},{9,13},{10,... | collective-permute-start | bytes 233480 | tf_op jit(solution)/shard_map/ppermute | solution.py:329
  25.0 6.4 %collective-permute-start.12 = (bf16[8,4864]{1,0:T(8,128)(2,1)S(1)}, bf16[8,4864]{1,0:T(8,128)(2,1)S(1)}, u32[]{:S(2)}, u32[]{:S(2)}) collective-permute-start(bf16[8,4864]{1,0:T(8,128)(2,1)S(1)} %get-tuple-element.48), channel_id=1, source_target_pairs={{0,6},{1,7},{2,4},{3,5},{4,2},{5,3},{6,0},{7,1},{8,14},{9,15},{10,... | collective-permute-start | bytes 233480 | tf_op jit(solution)/shard_map/ppermute | solution.py:329
  33.4 7.9 %collective-permute-start.13 = (bf16[2,3968]{1,0:T(2,128)(2,1)S(1)}, bf16[2,3968]{1,0:T(2,128)(2,1)S(1)}, u32[]{:S(2)}, u32[]{:S(2)}) collective-permute-start(bf16[2,3968]{1,0:T(2,128)(2,1)S(1)} %get-tuple-element.53), channel_id=1, source_target_pairs={{0,2},{1,3},{2,0},{3,1},{4,6},{5,7},{6,4},{7,5},{8,10},{9,11},{10,... | collective-permute-start | bytes 47624 | tf_op jit(solution)/shard_map/ppermute | solution.py:329
  33.5 7.9 %collective-permute-start.14 = (bf16[2,3968]{1,0:T(2,128)(2,1)S(1)}, bf16[2,3968]{1,0:T(2,128)(2,1)S(1)}, u32[]{:S(2)}, u32[]{:S(2)}) collective-permute-start(bf16[2,3968]{1,0:T(2,128)(2,1)S(1)} %get-tuple-element.54), channel_id=1, source_target_pairs={{0,4},{1,5},{2,6},{3,7},{4,0},{5,1},{6,2},{7,3},{8,12},{9,13},{10,... | collective-permute-start | bytes 47624 | tf_op jit(solution)/shard_map/ppermute | solution.py:329
  35.5 5.9 %collective-permute-start.15 = (bf16[2,3968]{1,0:T(2,128)(2,1)S(1)}, bf16[2,3968]{1,0:T(2,128)(2,1)S(1)}, u32[]{:S(2)}, u32[]{:S(2)}) collective-permute-start(bf16[2,3968]{1,0:T(2,128)(2,1)S(1)} %get-tuple-element.55), channel_id=1, source_target_pairs={{0,6},{1,7},{2,4},{3,5},{4,2},{5,3},{6,0},{7,1},{8,14},{9,15},{10,... | collective-permute-start | bytes 47624 | tf_op jit(solution)/shard_map/ppermute | solution.py:329

commit v7 on v6

--- a/solution.py
+++ b/solution.py
@@ -391,8 +391,7 @@
         operands=5,
     )(grad, routes, positions, table, done)
     came = relay(rows, -1)
-    shifted, _ = lax.optimization_barrier((grad, across(terms0)))
-    shifted = relay(shifted, -1)
+    shifted = relay(grad, -1)
     sends = call(merge_kernel, "merge", [wide] * (E_FLY - 1), operands=1, cost=COST2)(came)
     came = along_all([came, *sends])
     back = call(

time: 42.8 us -> 42.8 us (level)
  no operation moved by 1% of the time
where the time goes in v7:
time: 42.8 us; the launch traced here: 42.6 us
  starting transfers between devices  20.4 us (48%)
  waiting for transfers between devices  14.1 us (33%)
  Pallas kernels  7.34 us (17%)
  between operations  0.76 us (2%)
    ppermute x9, starting transfers between devices, along(): lax.ppermute(block, 'expert', [(i, i ^ 2 * k) for i in range(devices)])  14.6 us
    ppermute x9, waiting for transfers between devices, along(): lax.ppermute(block, 'expert', [(i, i ^ 2 * k) for i in range(devices)])  7.21 us
    ppermute x3, waiting for transfers between devices, relay(): return lax.ppermute(block, 'pipe', route)  6.84 us
    ppermute x3, starting transfers between devices, relay(): return lax.ppermute(block, 'pipe', route)  4.66 us
    pallas_call x1, Pallas kernels, local_chip(): call(step_one_kernel, 'step_one', [pair] * E_FLY, [pltpu.VMEM((PAIRS, pie...  2.06 us
    pallas_call x1, Pallas kernels, local_chip(): call(step_zero_kernel, 'step_zero', [jax.ShapeDtypeStruct((PAIRS, feature...  1.88 us
    pallas_call x1, Pallas kernels, local_chip(): call(pick_kernel, 'pick_rows', [pltpu.VMEM(pair.shape, BF16)] * E_FLY + [...  1.55 us
    pallas_call x1, Pallas kernels, local_chip(): call(final_kernel, 'final_sums', [jax.ShapeDtypeStruct((tokens, features)...  1.26 us
  transfers between devices with their start and end apart: 16, of which 6 were waited for; matrix products, arithmetic and copies ran while one was open for 0% of the time, Pallas kernels for 13%

profile of v7, /device:TPU:0, one launch (start us, length us, event | category | flops | bytes accessed | tf_op | source)
XLA Modules:
  0.0 42.6 jit_solution(5094290143134469784)
XLA Ops:
  0.6 0.0 copy-start.2
  0.6 0.5 %collective-permute-start.5 = (bf16[128,3840]{1,0:T(8,128)(2,1)}, bf16[128,3840]{1,0:T(8,128)(2,1)S(1)}, u32[]{:S(2)}, u32[]{:S(2)}) collective-permute-start(bf16[128,3840]{1,0:T(8,128)(2,1)} %bitcast.21), channel_id=1, source_target_pairs={{0,1},{1,0},{2,3},{3,2},{4,5},{5,4},{6,7},{7,6},{8,9},{9,8},{10,11... | collective-permute-start | bytes 2949128 | tf_op jit(solution)/shard_map/ppermute | solution.py:324
  1.2 0.1 collective-permute-start.3
  1.2 1.5 %pick_rows.1 = (bf16[2,3968]{1,0:T(2,128)(2,1)S(1)}, bf16[2,3968]{1,0:T(2,128)(2,1)S(1)}, bf16[2,3968]{1,0:T(2,128)(2,1)S(1)}, bf16[2,3968]{1,0:T(2,128)(2,1)S(1)}, f32[4,128]{1,0:T(4,128)S(1)}) custom-call(s32[2,2,128]{2,1,0:T(2,128)} %bitcast.30, s32[2,2,128]{2,1,0:T(2,128)} %bitcast.34, bf16[2,2,128]{2,1,0:T(2,128)(2,1)} %bitcast.40, ...), custom_call_target="tpu_custom_call" | custom-call | tf_op jit(solution)/shard_map/pick_rows/pallas_call | solution.py:348
  2.8 0.0 copy-done.2
  2.8 0.5 %collective-permute-start.1 = (bf16[3840,128]{1,0:T(8,128)(2,1)S(1)}, bf16[3840,128]{1,0:T(8,128)(2,1)S(1)}, u32[]{:S(2)}, u32[]{:S(2)}) collective-permute-start(bf16[3840,128]{1,0:T(8,128)(2,1)S(1)} %bitcast.24), channel_id=1, source_target_pairs={{0,1},{1,0},{2,3},{3,2},{4,5},{5,4},{6,7},{7,6},{8,9},{9,8},{10,11... | collective-permute-start | bytes 2949128 | tf_op jit(solution)/shard_map/ppermute | solution.py:324
  3.3 0.1 collective-permute-start.8
  3.4 5.0 %collective-permute-start.7 = (bf16[2,3968]{1,0:T(2,128)(2,1)S(1)}, bf16[2,3968]{1,0:T(2,128)(2,1)S(1)}, u32[]{:S(2)}, u32[]{:S(2)}) collective-permute-start(bf16[2,3968]{1,0:T(2,128)(2,1)S(1)} %get-tuple-element.39), channel_id=1, source_target_pairs={{0,6},{1,7},{2,4},{3,5},{4,2},{5,3},{6,0},{7,1},{8,14},{9,15},{10,... | collective-permute-start | bytes 47624 | tf_op jit(solution)/shard_map/ppermute | solution.py:329
  8.4 0.0 collective-permute-done.3.acts_other
  8.4 0.0 collective-permute-start.4
  8.4 0.0 collective-permute-done.5.refs_6_.refs_7_
  8.4 0.0 copy-start.1
  8.4 0.0 copy-start.3
  8.4 0.7 %collective-permute-start.6 = (bf16[2,3968]{1,0:T(2,128)(2,1)S(1)}, bf16[2,3968]{1,0:T(2,128)(2,1)S(1)}, u32[]{:S(2)}, u32[]{:S(2)}) collective-permute-start(bf16[2,3968]{1,0:T(2,128)(2,1)S(1)} %get-tuple-element.38), channel_id=1, source_target_pairs={{0,4},{1,5},{2,6},{3,7},{4,0},{5,1},{6,2},{7,3},{8,12},{9,13},{10,... | collective-permute-start | bytes 47624 | tf_op jit(solution)/shard_map/ppermute | solution.py:329
  9.1 0.0 copy-done.6
  9.1 0.2 factors.1.refs_4_
  9.3 0.0 collective-permute-done.1.refs_8_.refs_9_
  9.3 0.0 copy-start
  9.3 1.6 %collective-permute-start.2 = (f32[4,128]{1,0:T(4,128)S(1)}, f32[4,128]{1,0:T(4,128)S(1)}, u32[]{:S(2)}, u32[]{:S(2)}) collective-permute-start(f32[4,128]{1,0:T(4,128)S(1)} %get-tuple-element.33), channel_id=1, source_target_pairs={{0,8},{8,16},{16,24},{24,0},{1,9},{9,17},{17,25},{25,1},{2,10},{10... | collective-permute-start | bytes 6152 | tf_op jit(solution)/shard_map/ppermute | solution.py:336
  11.0 0.0 collective-permute-done.7.refs_3_
  11.0 1.2 %collective-permute-done.4.refs_1_ = bf16[2,3968]{1,0:T(2,128)(2,1)S(1)} collective-permute-done((bf16[2,3968]{1,0:T(2,128)(2,1)S(1)}, bf16[2,3968]{1,0:T(2,128)(2,1)S(1)}, u32[]{:S(2)}, u32[]{:S(2)}) %collective-permute-start.4) | collective-permute-done | bytes 15904 | tf_op jit(solution)/shard_map/ppermute | solution.py:329
  12.1 0.0 collective-permute-done.8.refs_10_.refs_11_
  12.2 1.1 %collective-permute-done.6.refs_2_ = bf16[2,3968]{1,0:T(2,128)(2,1)S(1)} collective-permute-done((bf16[2,3968]{1,0:T(2,128)(2,1)S(1)}, bf16[2,3968]{1,0:T(2,128)(2,1)S(1)}, u32[]{:S(2)}, u32[]{:S(2)}) %collective-permute-start.6) | collective-permute-done | bytes 15904 | tf_op jit(solution)/shard_map/ppermute | solution.py:329
  13.2 0.0 copy-done.1
  13.2 0.0 copy-done.3
  13.3 1.9 %step_zero.1 = (bf16[8,3840]{1,0:T(8,128)(2,1)S(1)}, f32[8,128]{1,0:T(8,128)S(1)}) custom-call(bf16[2,3968]{1,0:T(2,128)(2,1)S(1)} %get-tuple-element.34.refs_0_, bf16[2,3968]{1,0:T(2,128)(2,1)S(1)} %collective-permute-done.4.refs_1_, bf16[2,3968]{1,0:T(2,128)(2,1)S(1)} %collective-permute-done.6.refs_2_, ...), custom_call_target="tpu_custom_call" | custom-call | flops 20000000000 | tf_op jit(solution)/shard_map/step_zero/pallas_call | solution.py:375
  15.1 0.0 collective-permute-done.2.table
  15.1 0.0 copy-done
  15.1 0.0 copy-done.4
  15.2 0.3 rows_ahead.1
  15.5 2.5 %collective-permute-start.9 = (bf16[8,8064]{1,0:T(8,128)(2,1)S(1)}, bf16[8,8064]{1,0:T(8,128)(2,1)S(1)}, u32[]{:S(2)}, u32[]{:S(2)}) collective-permute-start(bf16[8,8064]{1,0:T(8,128)(2,1)S(1)} %rows_ahead.1), channel_id=1, source_target_pairs={{0,24},{8,0},{16,8},{24,16},{1,25},{9,1},{17,9},{25,17},{2,26},{10... | collective-permute-start | bytes 387080 | tf_op jit(solution)/shard_map/ppermute | solution.py:336
  18.0 0.5 %collective-permute-start = (bf16[128,3840]{1,0:T(8,128)(2,1)S(1)}, bf16[128,3840]{1,0:T(8,128)(2,1)S(1)}, u32[]{:S(2)}, u32[]{:S(2)}) collective-permute-start(bf16[128,3840]{1,0:T(8,128)(2,1)S(1)} %bitcast.20), channel_id=1, source_target_pairs={{0,24},{8,0},{16,8},{24,16},{1,25},{9,1},{17,9},{25,17},{2,26},{10... | collective-permute-start | bytes 2949128 | tf_op jit(solution)/shard_map/ppermute | solution.py:336
  18.6 3.4 %collective-permute-done.9.came.refs_2_.refs_0_ = bf16[8,8064]{1,0:T(8,128)(2,1)S(1)} collective-permute-done((bf16[8,8064]{1,0:T(8,128)(2,1)S(1)}, bf16[8,8064]{1,0:T(8,128)(2,1)S(1)}, u32[]{:S(2)}, u32[]{:S(2)}) %collective-permute-start.9) | collective-permute-done | bytes 129056 | tf_op jit(solution)/shard_map/ppermute | solution.py:336
  22.0 1.9 %collective-permute-start.10 = (bf16[8,4864]{1,0:T(8,128)(2,1)S(1)}, bf16[8,4864]{1,0:T(8,128)(2,1)S(1)}, u32[]{:S(2)}, u32[]{:S(2)}) collective-permute-start(bf16[8,4864]{1,0:T(8,128)(2,1)S(1)} %get-tuple-element.46), channel_id=1, source_target_pairs={{0,2},{1,3},{2,0},{3,1},{4,6},{5,7},{6,4},{7,5},{8,10},{9,11},{10,... | collective-permute-start | bytes 233480 | tf_op jit(solution)/shard_map/ppermute | solution.py:329
  23.9 1.1 %collective-permute-start.11 = (bf16[8,4864]{1,0:T(8,128)(2,1)S(1)}, bf16[8,4864]{1,0:T(8,128)(2,1)S(1)}, u32[]{:S(2)}, u32[]{:S(2)}) collective-permute-start(bf16[8,4864]{1,0:T(8,128)(2,1)S(1)} %get-tuple-element.47), channel_id=1, source_target_pairs={{0,4},{1,5},{2,6},{3,7},{4,0},{5,1},{6,2},{7,3},{8,12},{9,13},{10,... | collective-permute-start | bytes 233480 | tf_op jit(solution)/shard_map/ppermute | solution.py:329
  25.0 1.4 %collective-permute-start.12 = (bf16[8,4864]{1,0:T(8,128)(2,1)S(1)}, bf16[8,4864]{1,0:T(8,128)(2,1)S(1)}, u32[]{:S(2)}, u32[]{:S(2)}) collective-permute-start(bf16[8,4864]{1,0:T(8,128)(2,1)S(1)} %get-tuple-element.48), channel_id=1, source_target_pairs={{0,6},{1,7},{2,4},{3,5},{4,2},{5,3},{6,0},{7,1},{8,14},{9,15},{10,... | collective-permute-start | bytes 233480 | tf_op jit(solution)/shard_map/ppermute | solution.py:329
  26.4 0.0 collective-permute-done.10.refs_3_.refs_1_
  26.4 3.2 %collective-permute-done.11.refs_4_.refs_2_ = bf16[8,4864]{1,0:T(8,128)(2,1)S(1)} collective-permute-done((bf16[8,4864]{1,0:T(8,128)(2,1)S(1)}, bf16[8,4864]{1,0:T(8,128)(2,1)S(1)}, u32[]{:S(2)}, u32[]{:S(2)}) %collective-permute-start.11) | collective-permute-done | bytes 77856 | tf_op jit(solution)/shard_map/ppermute | solution.py:329
  29.6 1.7 %collective-permute-done.12.refs_5_.refs_3_ = bf16[8,4864]{1,0:T(8,128)(2,1)S(1)} collective-permute-done((bf16[8,4864]{1,0:T(8,128)(2,1)S(1)}, bf16[8,4864]{1,0:T(8,128)(2,1)S(1)}, u32[]{:S(2)}, u32[]{:S(2)}) %collective-permute-start.12) | collective-permute-done | bytes 77856 | tf_op jit(solution)/shard_map/ppermute | solution.py:329
  31.3 2.1 %step_one.1 = (bf16[2,3968]{1,0:T(2,128)(2,1)S(1)}, bf16[2,3968]{1,0:T(2,128)(2,1)S(1)}, bf16[2,3968]{1,0:T(2,128)(2,1)S(1)}, bf16[2,3968]{1,0:T(2,128)(2,1)S(1)}) custom-call(bf16[8,8064]{1,0:T(8,128)(2,1)S(1)} %collective-permute-done.9.came.refs_2_.refs_0_, bf16[8,4864]{1,0:T(8,128)(2,1)S(1)} %collective-permute-done.10.refs_3_.refs_1_, ...), custom_call_target="tpu_custom_call" | custom-call | tf_op jit(solution)/shard_map/step_one/pallas_call | solution.py:397
  33.4 0.0 collective-permute-start.13
  33.5 2.0 %collective-permute-start.14 = (bf16[2,3968]{1,0:T(2,128)(2,1)S(1)}, bf16[2,3968]{1,0:T(2,128)(2,1)S(1)}, u32[]{:S(2)}, u32[]{:S(2)}) collective-permute-start(bf16[2,3968]{1,0:T(2,128)(2,1)S(1)} %get-tuple-element.54), channel_id=1, source_target_pairs={{0,4},{1,5},{2,6},{3,7},{4,0},{5,1},{6,2},{7,3},{8,12},{9,13},{10,... | collective-permute-start | bytes 47624 | tf_op jit(solution)/shard_map/ppermute | solution.py:329
  35.5 2.4 %collective-permute-start.15 = (bf16[2,3968]{1,0:T(2,128)(2,1)S(1)}, bf16[2,3968]{1,0:T(2,128)(2,1)S(1)}, u32[]{:S(2)}, u32[]{:S(2)}) collective-permute-start(bf16[2,3968]{1,0:T(2,128)(2,1)S(1)} %get-tuple-element.55), channel_id=1, source_target_pairs={{0,6},{1,7},{2,4},{3,5},{4,2},{5,3},{6,0},{7,1},{8,14},{9,15},{10,... | collective-permute-start | bytes 47624 | tf_op jit(solution)/shard_map/ppermute | solution.py:329
  37.9 3.5 %collective-permute-done.refs_0_ = bf16[128,3840]{1,0:T(8,128)(2,1)S(1)} collective-permute-done((bf16[128,3840]{1,0:T(8,128)(2,1)S(1)}, bf16[128,3840]{1,0:T(8,128)(2,1)S(1)}, u32[]{:S(2)}, u32[]{:S(2)}) %collective-permute-start) | collective-permute-done | bytes 983072 | tf_op jit(solution)/shard_map/ppermute | solution.py:336
  41.3 0.0 collective-permute-done.13.refs_6_
  41.3 0.0 collective-permute-done.14.refs_7_
  41.3 0.0 collective-permute-done.15.refs_8_
  41.4 1.3 %final_sums.1 = (bf16[128,3840]{1,0:T(8,128)(2,1)}, f32[2,2,128]{2,1,0:T(2,128)}) custom-call(bf16[128,3840]{1,0:T(8,128)(2,1)S(1)} %collective-permute-done.refs_0_, f32[8,3840]{1,0:T(8,128)S(1)} %get-tuple-element.49.refs_1_, bf16[16,128]{1,0:T(8,128)(2,1)S(1)} %get-tuple-element.50.refs_2_, s32[2,2,128]{2,1,0:T(2,128)S(1)} %bitcast.33, ...), custom_call_target="tpu_custom_call" | custom-call | tf_op jit(solution)/shard_map/final_sums/pallas_call | solution.py:415
  (6 shorter events, 0.1 us)
Async XLA Ops:
  0.6 2.2 %copy-start.2 = (bf16[1,3840,128]{2,1,0:T(8,128)(2,1)S(1)}, bf16[1,3840,128]{2,1,0:T(8,128)(2,1)}, u32[]{:S(2)}) copy-start(bf16[1,3840,128]{2,1,0:T(8,128)(2,1)} %param.13) | copy-start | bytes 2949124
  0.6 7.8 %collective-permute-start.5 = (bf16[128,3840]{1,0:T(8,128)(2,1)}, bf16[128,3840]{1,0:T(8,128)(2,1)S(1)}, u32[]{:S(2)}, u32[]{:S(2)}) collective-permute-start(bf16[128,3840]{1,0:T(8,128)(2,1)} %bitcast.21), channel_id=1, source_target_pairs={{0,1},{1,0},{2,3},{3,2},{4,5},{5,4},{6,7},{7,6},{8,9},{9,8},{10,11... | collective-permute-start | bytes 2949128 | tf_op jit(solution)/shard_map/ppermute | solution.py:324
  1.2 7.3 %collective-permute-start.3 = (bf16[2,16,2,128]{3,2,1,0:T(2,128)(2,1)}, bf16[2,16,2,128]{3,2,1,0:T(2,128)(2,1)S(1)}, u32[]{:S(2)}, u32[]{:S(2)}) collective-permute-start(bf16[2,16,2,128]{3,2,1,0:T(2,128)(2,1)} %bitcast.38), channel_id=1, source_target_pairs={{0,1},{1,0},{2,3},{3,2},{4,5},{5,4},{6,7},{7,6},{8,9},{9,8},{10,11... | collective-permute-start | bytes 49160 | tf_op jit(solution)/shard_map/ppermute | solution.py:324
  1.2 7.9 %copy-start.6 = (bf16[1,2,16,2,128]{4,3,2,1,0:T(2,128)(2,1)S(1)}, bf16[1,2,16,2,128]{4,3,2,1,0:T(2,128)(2,1)}, u32[]{:S(2)}) copy-start(bf16[1,2,16,2,128]{4,3,2,1,0:T(2,128)(2,1)} %param.12) | copy-start | bytes 49156
  2.8 6.5 %collective-permute-start.1 = (bf16[3840,128]{1,0:T(8,128)(2,1)S(1)}, bf16[3840,128]{1,0:T(8,128)(2,1)S(1)}, u32[]{:S(2)}, u32[]{:S(2)}) collective-permute-start(bf16[3840,128]{1,0:T(8,128)(2,1)S(1)} %bitcast.24), channel_id=1, source_target_pairs={{0,1},{1,0},{2,3},{3,2},{4,5},{5,4},{6,7},{7,6},{8,9},{9,8},{10,11... | collective-permute-start | bytes 2949128 | tf_op jit(solution)/shard_map/ppermute | solution.py:324
  3.3 8.8 %collective-permute-start.8 = (bf16[3840,128]{1,0:T(8,128)(2,1)}, bf16[3840,128]{1,0:T(8,128)(2,1)S(1)}, u32[]{:S(2)}, u32[]{:S(2)}) collective-permute-start(bf16[3840,128]{1,0:T(8,128)(2,1)} %bitcast.27), channel_id=1, source_target_pairs={{0,1},{1,0},{2,3},{3,2},{4,5},{5,4},{6,7},{7,6},{8,9},{9,8},{10,11... | collective-permute-start | bytes 2949128 | tf_op jit(solution)/shard_map/ppermute | solution.py:324
  3.4 7.6 %collective-permute-start.7 = (bf16[2,3968]{1,0:T(2,128)(2,1)S(1)}, bf16[2,3968]{1,0:T(2,128)(2,1)S(1)}, u32[]{:S(2)}, u32[]{:S(2)}) collective-permute-start(bf16[2,3968]{1,0:T(2,128)(2,1)S(1)} %get-tuple-element.39), channel_id=1, source_target_pairs={{0,6},{1,7},{2,4},{3,5},{4,2},{5,3},{6,0},{7,1},{8,14},{9,15},{10,... | collective-permute-start | bytes 47624 | tf_op jit(solution)/shard_map/ppermute | solution.py:329
  8.4 3.7 %collective-permute-start.4 = (bf16[2,3968]{1,0:T(2,128)(2,1)S(1)}, bf16[2,3968]{1,0:T(2,128)(2,1)S(1)}, u32[]{:S(2)}, u32[]{:S(2)}) collective-permute-start(bf16[2,3968]{1,0:T(2,128)(2,1)S(1)} %get-tuple-element.36), channel_id=1, source_target_pairs={{0,2},{1,3},{2,0},{3,1},{4,6},{5,7},{6,4},{7,5},{8,10},{9,11},{10,... | collective-permute-start | bytes 47624 | tf_op jit(solution)/shard_map/ppermute | solution.py:329
  8.4 4.8 %copy-start.1 = (bf16[1,128,3840]{2,1,0:T(8,128)(2,1)S(1)}, bf16[1,128,3840]{2,1,0:T(8,128)(2,1)}, u32[]{:S(2)}) copy-start(bf16[1,128,3840]{2,1,0:T(8,128)(2,1)} %param.15) | copy-start | bytes 2949124
  8.4 4.8 %copy-start.3 = (bf16[1,3840,128]{2,1,0:T(8,128)(2,1)S(1)}, bf16[1,3840,128]{2,1,0:T(8,128)(2,1)}, u32[]{:S(2)}) copy-start(bf16[1,3840,128]{2,1,0:T(8,128)(2,1)} %param.14) | copy-start | bytes 2949124
  8.4 4.8 %collective-permute-start.6 = (bf16[2,3968]{1,0:T(2,128)(2,1)S(1)}, bf16[2,3968]{1,0:T(2,128)(2,1)S(1)}, u32[]{:S(2)}, u32[]{:S(2)}) collective-permute-start(bf16[2,3968]{1,0:T(2,128)(2,1)S(1)} %get-tuple-element.38), channel_id=1, source_target_pairs={{0,4},{1,5},{2,6},{3,7},{4,0},{5,1},{6,2},{7,3},{8,12},{9,13},{10,... | collective-permute-start | bytes 47624 | tf_op jit(solution)/shard_map/ppermute | solution.py:329
  9.3 5.8 %copy-start = (bf16[1,128,3840]{2,1,0:T(8,128)(2,1)S(1)}, bf16[1,128,3840]{2,1,0:T(8,128)(2,1)}, u32[]{:S(2)}) copy-start(bf16[1,128,3840]{2,1,0:T(8,128)(2,1)} %param.8) | copy-start | bytes 2949124
  9.3 5.8 %collective-permute-start.2 = (f32[4,128]{1,0:T(4,128)S(1)}, f32[4,128]{1,0:T(4,128)S(1)}, u32[]{:S(2)}, u32[]{:S(2)}) collective-permute-start(f32[4,128]{1,0:T(4,128)S(1)} %get-tuple-element.33), channel_id=1, source_target_pairs={{0,8},{8,16},{16,24},{24,0},{1,9},{9,17},{17,25},{25,1},{2,10},{10... | collective-permute-start | bytes 6152 | tf_op jit(solution)/shard_map/ppermute | solution.py:336
  13.2 1.9 %copy-start.4 = (s32[1,2,128,2]{2,3,1,0:T(2,128)S(1)}, s32[1,2,128,2]{2,3,1,0:T(2,128)}, u32[]{:S(2)}) copy-start(s32[1,2,128,2]{2,3,1,0:T(2,128)} %param.9) | copy-start | bytes 6148
  13.2 1.9 %copy-start.5 = (s32[1,2,128,2]{2,3,1,0:T(2,128)S(1)}, s32[1,2,128,2]{2,3,1,0:T(2,128)}, u32[]{:S(2)}) copy-start(s32[1,2,128,2]{2,3,1,0:T(2,128)} %param.10) | copy-start | bytes 6148
  15.5 6.4 %collective-permute-start.9 = (bf16[8,8064]{1,0:T(8,128)(2,1)S(1)}, bf16[8,8064]{1,0:T(8,128)(2,1)S(1)}, u32[]{:S(2)}, u32[]{:S(2)}) collective-permute-start(bf16[8,8064]{1,0:T(8,128)(2,1)S(1)} %rows_ahead.1), channel_id=1, source_target_pairs={{0,24},{8,0},{16,8},{24,16},{1,25},{9,1},{17,9},{25,17},{2,26},{10... | collective-permute-start | bytes 387080 | tf_op jit(solution)/shard_map/ppermute | solution.py:336
  18.0 23.3 %collective-permute-start = (bf16[128,3840]{1,0:T(8,128)(2,1)S(1)}, bf16[128,3840]{1,0:T(8,128)(2,1)S(1)}, u32[]{:S(2)}, u32[]{:S(2)}) collective-permute-start(bf16[128,3840]{1,0:T(8,128)(2,1)S(1)} %bitcast.20), channel_id=1, source_target_pairs={{0,24},{8,0},{16,8},{24,16},{1,25},{9,1},{17,9},{25,17},{2,26},{10... | collective-permute-start | bytes 2949128 | tf_op jit(solution)/shard_map/ppermute | solution.py:336
  22.0 4.5 %collective-permute-start.10 = (bf16[8,4864]{1,0:T(8,128)(2,1)S(1)}, bf16[8,4864]{1,0:T(8,128)(2,1)S(1)}, u32[]{:S(2)}, u32[]{:S(2)}) collective-permute-start(bf16[8,4864]{1,0:T(8,128)(2,1)S(1)} %get-tuple-element.46), channel_id=1, source_target_pairs={{0,2},{1,3},{2,0},{3,1},{4,6},{5,7},{6,4},{7,5},{8,10},{9,11},{10,... | collective-permute-start | bytes 233480 | tf_op jit(solution)/shard_map/ppermute | solution.py:329
  23.9 5.8 %collective-permute-start.11 = (bf16[8,4864]{1,0:T(8,128)(2,1)S(1)}, bf16[8,4864]{1,0:T(8,128)(2,1)S(1)}, u32[]{:S(2)}, u32[]{:S(2)}) collective-permute-start(bf16[8,4864]{1,0:T(8,128)(2,1)S(1)} %get-tuple-element.47), channel_id=1, source_target_pairs={{0,4},{1,5},{2,6},{3,7},{4,0},{5,1},{6,2},{7,3},{8,12},{9,13},{10,... | collective-permute-start | bytes 233480 | tf_op jit(solution)/shard_map/ppermute | solution.py:329
  25.0 6.4 %collective-permute-start.12 = (bf16[8,4864]{1,0:T(8,128)(2,1)S(1)}, bf16[8,4864]{1,0:T(8,128)(2,1)S(1)}, u32[]{:S(2)}, u32[]{:S(2)}) collective-permute-start(bf16[8,4864]{1,0:T(8,128)(2,1)S(1)} %get-tuple-element.48), channel_id=1, source_target_pairs={{0,6},{1,7},{2,4},{3,5},{4,2},{5,3},{6,0},{7,1},{8,14},{9,15},{10,... | collective-permute-start | bytes 233480 | tf_op jit(solution)/shard_map/ppermute | solution.py:329
  33.4 7.9 %collective-permute-start.13 = (bf16[2,3968]{1,0:T(2,128)(2,1)S(1)}, bf16[2,3968]{1,0:T(2,128)(2,1)S(1)}, u32[]{:S(2)}, u32[]{:S(2)}) collective-permute-start(bf16[2,3968]{1,0:T(2,128)(2,1)S(1)} %get-tuple-element.53), channel_id=1, source_target_pairs={{0,2},{1,3},{2,0},{3,1},{4,6},{5,7},{6,4},{7,5},{8,10},{9,11},{10,... | collective-permute-start | bytes 47624 | tf_op jit(solution)/shard_map/ppermute | solution.py:329
  33.5 7.9 %collective-permute-start.14 = (bf16[2,3968]{1,0:T(2,128)(2,1)S(1)}, bf16[2,3968]{1,0:T(2,128)(2,1)S(1)}, u32[]{:S(2)}, u32[]{:S(2)}) collective-permute-start(bf16[2,3968]{1,0:T(2,128)(2,1)S(1)} %get-tuple-element.54), channel_id=1, source_target_pairs={{0,4},{1,5},{2,6},{3,7},{4,0},{5,1},{6,2},{7,3},{8,12},{9,13},{10,... | collective-permute-start | bytes 47624 | tf_op jit(solution)/shard_map/ppermute | solution.py:329
  35.5 5.9 %collective-permute-start.15 = (bf16[2,3968]{1,0:T(2,128)(2,1)S(1)}, bf16[2,3968]{1,0:T(2,128)(2,1)S(1)}, u32[]{:S(2)}, u32[]{:S(2)}) collective-permute-start(bf16[2,3968]{1,0:T(2,128)(2,1)S(1)} %get-tuple-element.55), channel_id=1, source_target_pairs={{0,6},{1,7},{2,4},{3,5},{4,2},{5,3},{6,0},{7,1},{8,14},{9,15},{10,... | collective-permute-start | bytes 47624 | tf_op jit(solution)/shard_map/ppermute | solution.py:329

commit v8 on v7

--- a/solution.py
+++ b/solution.py
@@ -358,8 +358,7 @@
     )(*small)
     *own, picked[0] = lax.optimization_barrier((*own, picked[0]))
     others += [across(array) for array in own[1:]]
-    others[0], picked[2] = lax.optimization_barrier((others[0], picked[2]))
-    acts_other, picked[1] = lax.optimization_barrier((acts_other, picked[1]))
+    others[0], picked[1] = lax.optimization_barrier((others[0], picked[1]))
     got = along_all(picked)
     table, others[1] = lax.optimization_barrier((table, others[1]))
     table = relay(table, 1)

time: 42.8 us -> 42.6 us (level)
    ppermute x9, waiting for transfers between devices: 7.21 us -> 6.66 us  [along(): lax.ppermute(block, 'expert', [(i, i ^ 2 * k) for i in range(devices)])]
    ppermute x3, waiting for transfers between devices: 6.84 us -> 7.33 us  [relay(): return lax.ppermute(block, 'pipe', route)]
  transfers between devices with their start and end apart: 16 -> 16, of which waited for: 6 -> 6; matrix products, arithmetic and copies ran while one was open for 0% -> 0% of each run, Pallas kernels for 13% -> 14%
where the time goes in v8:
time: 42.6 us; the launch traced here: 42.4 us
  starting transfers between devices  20.3 us (48%)
  waiting for transfers between devices  14 us (33%)
  Pallas kernels  7.34 us (17%)
  between operations  0.76 us (2%)
    ppermute x9, starting transfers between devices, along(): lax.ppermute(block, 'expert', [(i, i ^ 2 * k) for i in range(devices)])  14.5 us
    ppermute x3, waiting for transfers between devices, relay(): return lax.ppermute(block, 'pipe', route)  7.33 us
    ppermute x9, waiting for transfers between devices, along(): lax.ppermute(block, 'expert', [(i, i ^ 2 * k) for i in range(devices)])  6.66 us
    ppermute x3, starting transfers between devices, relay(): return lax.ppermute(block, 'pipe', route)  4.57 us
    pallas_call x1, Pallas kernels, local_chip(): call(step_one_kernel, 'step_one', [pair] * E_FLY, [pltpu.VMEM((PAIRS, pie...  2.07 us
    pallas_call x1, Pallas kernels, local_chip(): call(step_zero_kernel, 'step_zero', [jax.ShapeDtypeStruct((PAIRS, feature...  1.88 us
    pallas_call x1, Pallas kernels, local_chip(): call(pick_kernel, 'pick_rows', [pltpu.VMEM(pair.shape, BF16)] * E_FLY + [...  1.55 us
    pallas_call x1, Pallas kernels, local_chip(): call(final_kernel, 'final_sums', [jax.ShapeDtypeStruct((tokens, features)...  1.26 us
  transfers between devices with their start and end apart: 16, of which 6 were waited for; matrix products, arithmetic and copies ran while one was open for 0% of the time, Pallas kernels for 14%

profile of v8, /device:TPU:0, one launch (start us, length us, event | category | flops | bytes accessed | tf_op | source)
XLA Modules:
  0.0 42.4 jit_solution(6296252114147189436)
XLA Ops:
  0.6 0.0 copy-start.2
  0.6 0.5 %collective-permute-start.3 = (bf16[128,3840]{1,0:T(8,128)(2,1)}, bf16[128,3840]{1,0:T(8,128)(2,1)S(1)}, u32[]{:S(2)}, u32[]{:S(2)}) collective-permute-start(bf16[128,3840]{1,0:T(8,128)(2,1)} %bitcast.21), channel_id=1, source_target_pairs={{0,1},{1,0},{2,3},{3,2},{4,5},{5,4},{6,7},{7,6},{8,9},{9,8},{10,11... | collective-permute-start | bytes 2949128 | tf_op jit(solution)/shard_map/ppermute | solution.py:324
  1.2 0.1 collective-permute-start.7
  1.2 1.5 %pick_rows.1 = (bf16[2,3968]{1,0:T(2,128)(2,1)S(1)}, bf16[2,3968]{1,0:T(2,128)(2,1)S(1)}, bf16[2,3968]{1,0:T(2,128)(2,1)S(1)}, bf16[2,3968]{1,0:T(2,128)(2,1)S(1)}, f32[4,128]{1,0:T(4,128)S(1)}) custom-call(s32[2,2,128]{2,1,0:T(2,128)} %bitcast.30, s32[2,2,128]{2,1,0:T(2,128)} %bitcast.34, bf16[2,2,128]{2,1,0:T(2,128)(2,1)} %bitcast.40, ...), custom_call_target="tpu_custom_call" | custom-call | tf_op jit(solution)/shard_map/pick_rows/pallas_call | solution.py:348
  2.8 0.0 copy-done.2
  2.8 0.5 %collective-permute-start.1 = (bf16[3840,128]{1,0:T(8,128)(2,1)S(1)}, bf16[3840,128]{1,0:T(8,128)(2,1)S(1)}, u32[]{:S(2)}, u32[]{:S(2)}) collective-permute-start(bf16[3840,128]{1,0:T(8,128)(2,1)S(1)} %bitcast.24), channel_id=1, source_target_pairs={{0,1},{1,0},{2,3},{3,2},{4,5},{5,4},{6,7},{7,6},{8,9},{9,8},{10,11... | collective-permute-start | bytes 2949128 | tf_op jit(solution)/shard_map/ppermute | solution.py:324
  3.3 0.1 collective-permute-start.8
  3.4 4.0 %collective-permute-start.5 = (bf16[2,3968]{1,0:T(2,128)(2,1)S(1)}, bf16[2,3968]{1,0:T(2,128)(2,1)S(1)}, u32[]{:S(2)}, u32[]{:S(2)}) collective-permute-start(bf16[2,3968]{1,0:T(2,128)(2,1)S(1)} %get-tuple-element.35), channel_id=1, source_target_pairs={{0,4},{1,5},{2,6},{3,7},{4,0},{5,1},{6,2},{7,3},{8,12},{9,13},{10,... | collective-permute-start | bytes 47624 | tf_op jit(solution)/shard_map/ppermute | solution.py:329
  7.4 0.0 collective-permute-done.3.refs_6_.refs_7_
  7.4 1.3 %collective-permute-start.6 = (bf16[2,3968]{1,0:T(2,128)(2,1)S(1)}, bf16[2,3968]{1,0:T(2,128)(2,1)S(1)}, u32[]{:S(2)}, u32[]{:S(2)}) collective-permute-start(bf16[2,3968]{1,0:T(2,128)(2,1)S(1)} %get-tuple-element.36), channel_id=1, source_target_pairs={{0,6},{1,7},{2,4},{3,5},{4,2},{5,3},{6,0},{7,1},{8,14},{9,15},{10,... | collective-permute-start | bytes 47624 | tf_op jit(solution)/shard_map/ppermute | solution.py:329
  8.8 0.0 collective-permute-done.7.acts_other
  8.8 0.3 collective-permute-start.4
  9.1 0.0 copy-done.6
  9.1 0.2 factors.1.refs_4_
  9.3 0.0 collective-permute-done.1.refs_8_.refs_9_
  9.3 0.0 copy-start
  9.3 1.5 %collective-permute-start.2 = (f32[4,128]{1,0:T(4,128)S(1)}, f32[4,128]{1,0:T(4,128)S(1)}, u32[]{:S(2)}, u32[]{:S(2)}) collective-permute-start(f32[4,128]{1,0:T(4,128)S(1)} %get-tuple-element.31), channel_id=1, source_target_pairs={{0,8},{8,16},{16,24},{24,0},{1,9},{9,17},{17,25},{25,1},{2,10},{10... | collective-permute-start | bytes 6152 | tf_op jit(solution)/shard_map/ppermute | solution.py:336
  10.8 0.0 collective-permute-done.5.refs_2_
  10.8 2.1 %collective-permute-done.6.refs_3_ = bf16[2,3968]{1,0:T(2,128)(2,1)S(1)} collective-permute-done((bf16[2,3968]{1,0:T(2,128)(2,1)S(1)}, bf16[2,3968]{1,0:T(2,128)(2,1)S(1)}, u32[]{:S(2)}, u32[]{:S(2)}) %collective-permute-start.6) | collective-permute-done | bytes 15904 | tf_op jit(solution)/shard_map/ppermute | solution.py:329
  12.9 0.0 collective-permute-done.8.refs_10_.refs_11_
  12.9 0.0 collective-permute-done.4.refs_1_
  12.9 0.0 copy-done.1
  12.9 0.0 copy-done.3
  13.0 0.0 copy-start.4
  13.0 0.0 copy-start.5
  13.0 1.9 %step_zero.1 = (bf16[8,3840]{1,0:T(8,128)(2,1)S(1)}, f32[8,128]{1,0:T(8,128)S(1)}) custom-call(bf16[2,3968]{1,0:T(2,128)(2,1)S(1)} %get-tuple-element.32.refs_0_, bf16[2,3968]{1,0:T(2,128)(2,1)S(1)} %collective-permute-done.4.refs_1_, bf16[2,3968]{1,0:T(2,128)(2,1)S(1)} %collective-permute-done.5.refs_2_, ...), custom_call_target="tpu_custom_call" | custom-call | flops 20000000000 | tf_op jit(solution)/shard_map/step_zero/pallas_call | solution.py:374
  14.9 0.0 collective-permute-done.2.table
  14.9 0.0 copy-done.4
  14.9 0.0 copy-done.5
  14.9 0.3 rows_ahead.1
  15.2 2.5 %collective-permute-start.9 = (bf16[8,8064]{1,0:T(8,128)(2,1)S(1)}, bf16[8,8064]{1,0:T(8,128)(2,1)S(1)}, u32[]{:S(2)}, u32[]{:S(2)}) collective-permute-start(bf16[8,8064]{1,0:T(8,128)(2,1)S(1)} %rows_ahead.1), channel_id=1, source_target_pairs={{0,24},{8,0},{16,8},{24,16},{1,25},{9,1},{17,9},{25,17},{2,26},{10... | collective-permute-start | bytes 387080 | tf_op jit(solution)/shard_map/ppermute | solution.py:336
  17.7 0.5 %collective-permute-start = (bf16[128,3840]{1,0:T(8,128)(2,1)S(1)}, bf16[128,3840]{1,0:T(8,128)(2,1)S(1)}, u32[]{:S(2)}, u32[]{:S(2)}) collective-permute-start(bf16[128,3840]{1,0:T(8,128)(2,1)S(1)} %bitcast.20), channel_id=1, source_target_pairs={{0,24},{8,0},{16,8},{24,16},{1,25},{9,1},{17,9},{25,17},{2,26},{10... | collective-permute-start | bytes 2949128 | tf_op jit(solution)/shard_map/ppermute | solution.py:336
  18.3 3.4 %collective-permute-done.9.came.refs_2_.refs_0_ = bf16[8,8064]{1,0:T(8,128)(2,1)S(1)} collective-permute-done((bf16[8,8064]{1,0:T(8,128)(2,1)S(1)}, bf16[8,8064]{1,0:T(8,128)(2,1)S(1)}, u32[]{:S(2)}, u32[]{:S(2)}) %collective-permute-start.9) | collective-permute-done | bytes 129056 | tf_op jit(solution)/shard_map/ppermute | solution.py:336
  21.7 0.7 %collective-permute-start.10 = (bf16[8,4864]{1,0:T(8,128)(2,1)S(1)}, bf16[8,4864]{1,0:T(8,128)(2,1)S(1)}, u32[]{:S(2)}, u32[]{:S(2)}) collective-permute-start(bf16[8,4864]{1,0:T(8,128)(2,1)S(1)} %get-tuple-element.42), channel_id=1, source_target_pairs={{0,2},{1,3},{2,0},{3,1},{4,6},{5,7},{6,4},{7,5},{8,10},{9,11},{10,... | collective-permute-start | bytes 233480 | tf_op jit(solution)/shard_map/ppermute | solution.py:329
  22.4 1.9 %collective-permute-start.11 = (bf16[8,4864]{1,0:T(8,128)(2,1)S(1)}, bf16[8,4864]{1,0:T(8,128)(2,1)S(1)}, u32[]{:S(2)}, u32[]{:S(2)}) collective-permute-start(bf16[8,4864]{1,0:T(8,128)(2,1)S(1)} %get-tuple-element.43), channel_id=1, source_target_pairs={{0,4},{1,5},{2,6},{3,7},{4,0},{5,1},{6,2},{7,3},{8,12},{9,13},{10,... | collective-permute-start | bytes 233480 | tf_op jit(solution)/shard_map/ppermute | solution.py:329
  24.3 1.8 %collective-permute-start.12 = (bf16[8,4864]{1,0:T(8,128)(2,1)S(1)}, bf16[8,4864]{1,0:T(8,128)(2,1)S(1)}, u32[]{:S(2)}, u32[]{:S(2)}) collective-permute-start(bf16[8,4864]{1,0:T(8,128)(2,1)S(1)} %get-tuple-element.44), channel_id=1, source_target_pairs={{0,6},{1,7},{2,4},{3,5},{4,2},{5,3},{6,0},{7,1},{8,14},{9,15},{10,... | collective-permute-start | bytes 233480 | tf_op jit(solution)/shard_map/ppermute | solution.py:329
  26.1 0.1 collective-permute-done.10.refs_3_.refs_1_
  26.2 1.4 %collective-permute-done.11.refs_4_.refs_2_ = bf16[8,4864]{1,0:T(8,128)(2,1)S(1)} collective-permute-done((bf16[8,4864]{1,0:T(8,128)(2,1)S(1)}, bf16[8,4864]{1,0:T(8,128)(2,1)S(1)}, u32[]{:S(2)}, u32[]{:S(2)}) %collective-permute-start.11) | collective-permute-done | bytes 77856 | tf_op jit(solution)/shard_map/ppermute | solution.py:329
  27.7 3.0 %collective-permute-done.12.refs_5_.refs_3_ = bf16[8,4864]{1,0:T(8,128)(2,1)S(1)} collective-permute-done((bf16[8,4864]{1,0:T(8,128)(2,1)S(1)}, bf16[8,4864]{1,0:T(8,128)(2,1)S(1)}, u32[]{:S(2)}, u32[]{:S(2)}) %collective-permute-start.12) | collective-permute-done | bytes 77856 | tf_op jit(solution)/shard_map/ppermute | solution.py:329
  30.7 2.1 %step_one.1 = (bf16[2,3968]{1,0:T(2,128)(2,1)S(1)}, bf16[2,3968]{1,0:T(2,128)(2,1)S(1)}, bf16[2,3968]{1,0:T(2,128)(2,1)S(1)}, bf16[2,3968]{1,0:T(2,128)(2,1)S(1)}) custom-call(bf16[8,8064]{1,0:T(8,128)(2,1)S(1)} %collective-permute-done.9.came.refs_2_.refs_0_, bf16[8,4864]{1,0:T(8,128)(2,1)S(1)} %collective-permute-done.10.refs_3_.refs_1_, ...), custom_call_target="tpu_custom_call" | custom-call | tf_op jit(solution)/shard_map/step_one/pallas_call | solution.py:396
  32.7 0.0 collective-permute-start.13
  32.8 2.4 %collective-permute-start.14 = (bf16[2,3968]{1,0:T(2,128)(2,1)S(1)}, bf16[2,3968]{1,0:T(2,128)(2,1)S(1)}, u32[]{:S(2)}, u32[]{:S(2)}) collective-permute-start(bf16[2,3968]{1,0:T(2,128)(2,1)S(1)} %get-tuple-element.50), channel_id=1, source_target_pairs={{0,4},{1,5},{2,6},{3,7},{4,0},{5,1},{6,2},{7,3},{8,12},{9,13},{10,... | collective-permute-start | bytes 47624 | tf_op jit(solution)/shard_map/ppermute | solution.py:329
  35.2 2.0 %collective-permute-start.15 = (bf16[2,3968]{1,0:T(2,128)(2,1)S(1)}, bf16[2,3968]{1,0:T(2,128)(2,1)S(1)}, u32[]{:S(2)}, u32[]{:S(2)}) collective-permute-start(bf16[2,3968]{1,0:T(2,128)(2,1)S(1)} %get-tuple-element.51), channel_id=1, source_target_pairs={{0,6},{1,7},{2,4},{3,5},{4,2},{5,3},{6,0},{7,1},{8,14},{9,15},{10,... | collective-permute-start | bytes 47624 | tf_op jit(solution)/shard_map/ppermute | solution.py:329
  37.2 4.0 %collective-permute-done.refs_0_ = bf16[128,3840]{1,0:T(8,128)(2,1)S(1)} collective-permute-done((bf16[128,3840]{1,0:T(8,128)(2,1)S(1)}, bf16[128,3840]{1,0:T(8,128)(2,1)S(1)}, u32[]{:S(2)}, u32[]{:S(2)}) %collective-permute-start) | collective-permute-done | bytes 983072 | tf_op jit(solution)/shard_map/ppermute | solution.py:336
  41.2 0.0 collective-permute-done.13.refs_6_
  41.2 0.0 collective-permute-done.14.refs_7_
  41.2 0.0 collective-permute-done.15.refs_8_
  41.2 1.3 %final_sums.1 = (bf16[128,3840]{1,0:T(8,128)(2,1)}, f32[2,2,128]{2,1,0:T(2,128)}) custom-call(bf16[128,3840]{1,0:T(8,128)(2,1)S(1)} %collective-permute-done.refs_0_, f32[8,3840]{1,0:T(8,128)S(1)} %get-tuple-element.45.refs_1_, bf16[16,128]{1,0:T(8,128)(2,1)S(1)} %get-tuple-element.46.refs_2_, s32[2,2,128]{2,1,0:T(2,128)S(1)} %bitcast.33, ...), custom_call_target="tpu_custom_call" | custom-call | tf_op jit(solution)/shard_map/final_sums/pallas_call | solution.py:414
  (6 shorter events, 0.1 us)
Async XLA Ops:
  0.6 2.2 %copy-start.2 = (bf16[1,3840,128]{2,1,0:T(8,128)(2,1)S(1)}, bf16[1,3840,128]{2,1,0:T(8,128)(2,1)}, u32[]{:S(2)}) copy-start(bf16[1,3840,128]{2,1,0:T(8,128)(2,1)} %param.13) | copy-start | bytes 2949124
  0.6 6.8 %collective-permute-start.3 = (bf16[128,3840]{1,0:T(8,128)(2,1)}, bf16[128,3840]{1,0:T(8,128)(2,1)S(1)}, u32[]{:S(2)}, u32[]{:S(2)}) collective-permute-start(bf16[128,3840]{1,0:T(8,128)(2,1)} %bitcast.21), channel_id=1, source_target_pairs={{0,1},{1,0},{2,3},{3,2},{4,5},{5,4},{6,7},{7,6},{8,9},{9,8},{10,11... | collective-permute-start | bytes 2949128 | tf_op jit(solution)/shard_map/ppermute | solution.py:324
  1.2 7.6 %collective-permute-start.7 = (bf16[2,16,2,128]{3,2,1,0:T(2,128)(2,1)}, bf16[2,16,2,128]{3,2,1,0:T(2,128)(2,1)S(1)}, u32[]{:S(2)}, u32[]{:S(2)}) collective-permute-start(bf16[2,16,2,128]{3,2,1,0:T(2,128)(2,1)} %bitcast.38), channel_id=1, source_target_pairs={{0,1},{1,0},{2,3},{3,2},{4,5},{5,4},{6,7},{7,6},{8,9},{9,8},{10,11... | collective-permute-start | bytes 49160 | tf_op jit(solution)/shard_map/ppermute | solution.py:324
  1.2 7.8 %copy-start.6 = (bf16[1,2,16,2,128]{4,3,2,1,0:T(2,128)(2,1)S(1)}, bf16[1,2,16,2,128]{4,3,2,1,0:T(2,128)(2,1)}, u32[]{:S(2)}) copy-start(bf16[1,2,16,2,128]{4,3,2,1,0:T(2,128)(2,1)} %param.12) | copy-start | bytes 49156
  2.8 6.5 %collective-permute-start.1 = (bf16[3840,128]{1,0:T(8,128)(2,1)S(1)}, bf16[3840,128]{1,0:T(8,128)(2,1)S(1)}, u32[]{:S(2)}, u32[]{:S(2)}) collective-permute-start(bf16[3840,128]{1,0:T(8,128)(2,1)S(1)} %bitcast.24), channel_id=1, source_target_pairs={{0,1},{1,0},{2,3},{3,2},{4,5},{5,4},{6,7},{7,6},{8,9},{9,8},{10,11... | collective-permute-start | bytes 2949128 | tf_op jit(solution)/shard_map/ppermute | solution.py:324
  3.3 9.6 %collective-permute-start.8 = (bf16[3840,128]{1,0:T(8,128)(2,1)}, bf16[3840,128]{1,0:T(8,128)(2,1)S(1)}, u32[]{:S(2)}, u32[]{:S(2)}) collective-permute-start(bf16[3840,128]{1,0:T(8,128)(2,1)} %bitcast.27), channel_id=1, source_target_pairs={{0,1},{1,0},{2,3},{3,2},{4,5},{5,4},{6,7},{7,6},{8,9},{9,8},{10,11... | collective-permute-start | bytes 2949128 | tf_op jit(solution)/shard_map/ppermute | solution.py:324
  3.4 7.4 %collective-permute-start.5 = (bf16[2,3968]{1,0:T(2,128)(2,1)S(1)}, bf16[2,3968]{1,0:T(2,128)(2,1)S(1)}, u32[]{:S(2)}, u32[]{:S(2)}) collective-permute-start(bf16[2,3968]{1,0:T(2,128)(2,1)S(1)} %get-tuple-element.35), channel_id=1, source_target_pairs={{0,4},{1,5},{2,6},{3,7},{4,0},{5,1},{6,2},{7,3},{8,12},{9,13},{10,... | collective-permute-start | bytes 47624 | tf_op jit(solution)/shard_map/ppermute | solution.py:329
  7.4 5.5 %collective-permute-start.6 = (bf16[2,3968]{1,0:T(2,128)(2,1)S(1)}, bf16[2,3968]{1,0:T(2,128)(2,1)S(1)}, u32[]{:S(2)}, u32[]{:S(2)}) collective-permute-start(bf16[2,3968]{1,0:T(2,128)(2,1)S(1)} %get-tuple-element.36), channel_id=1, source_target_pairs={{0,6},{1,7},{2,4},{3,5},{4,2},{5,3},{6,0},{7,1},{8,14},{9,15},{10,... | collective-permute-start | bytes 47624 | tf_op jit(solution)/shard_map/ppermute | solution.py:329
  8.7 4.2 %copy-start.1 = (bf16[1,128,3840]{2,1,0:T(8,128)(2,1)S(1)}, bf16[1,128,3840]{2,1,0:T(8,128)(2,1)}, u32[]{:S(2)}) copy-start(bf16[1,128,3840]{2,1,0:T(8,128)(2,1)} %param.15) | copy-start | bytes 2949124
  8.8 4.2 %copy-start.3 = (bf16[1,3840,128]{2,1,0:T(8,128)(2,1)S(1)}, bf16[1,3840,128]{2,1,0:T(8,128)(2,1)}, u32[]{:S(2)}) copy-start(bf16[1,3840,128]{2,1,0:T(8,128)(2,1)} %param.14) | copy-start | bytes 2949124
  8.8 4.2 %collective-permute-start.4 = (bf16[2,3968]{1,0:T(2,128)(2,1)S(1)}, bf16[2,3968]{1,0:T(2,128)(2,1)S(1)}, u32[]{:S(2)}, u32[]{:S(2)}) collective-permute-start(bf16[2,3968]{1,0:T(2,128)(2,1)S(1)} %get-tuple-element.34), channel_id=1, source_target_pairs={{0,2},{1,3},{2,0},{3,1},{4,6},{5,7},{6,4},{7,5},{8,10},{9,11},{10,... | collective-permute-start | bytes 47624 | tf_op jit(solution)/shard_map/ppermute | solution.py:329
  9.3 5.6 %copy-start = (bf16[1,128,3840]{2,1,0:T(8,128)(2,1)S(1)}, bf16[1,128,3840]{2,1,0:T(8,128)(2,1)}, u32[]{:S(2)}) copy-start(bf16[1,128,3840]{2,1,0:T(8,128)(2,1)} %param.8) | copy-start | bytes 2949124
  9.3 5.6 %collective-permute-start.2 = (f32[4,128]{1,0:T(4,128)S(1)}, f32[4,128]{1,0:T(4,128)S(1)}, u32[]{:S(2)}, u32[]{:S(2)}) collective-permute-start(f32[4,128]{1,0:T(4,128)S(1)} %get-tuple-element.31), channel_id=1, source_target_pairs={{0,8},{8,16},{16,24},{24,0},{1,9},{9,17},{17,25},{25,1},{2,10},{10... | collective-permute-start | bytes 6152 | tf_op jit(solution)/shard_map/ppermute | solution.py:336
  13.0 1.9 %copy-start.4 = (s32[1,2,128,2]{2,3,1,0:T(2,128)S(1)}, s32[1,2,128,2]{2,3,1,0:T(2,128)}, u32[]{:S(2)}) copy-start(s32[1,2,128,2]{2,3,1,0:T(2,128)} %param.9) | copy-start | bytes 6148
  13.0 1.9 %copy-start.5 = (s32[1,2,128,2]{2,3,1,0:T(2,128)S(1)}, s32[1,2,128,2]{2,3,1,0:T(2,128)}, u32[]{:S(2)}) copy-start(s32[1,2,128,2]{2,3,1,0:T(2,128)} %param.10) | copy-start | bytes 6148
  15.2 6.4 %collective-permute-start.9 = (bf16[8,8064]{1,0:T(8,128)(2,1)S(1)}, bf16[8,8064]{1,0:T(8,128)(2,1)S(1)}, u32[]{:S(2)}, u32[]{:S(2)}) collective-permute-start(bf16[8,8064]{1,0:T(8,128)(2,1)S(1)} %rows_ahead.1), channel_id=1, source_target_pairs={{0,24},{8,0},{16,8},{24,16},{1,25},{9,1},{17,9},{25,17},{2,26},{10... | collective-permute-start | bytes 387080 | tf_op jit(solution)/shard_map/ppermute | solution.py:336
  17.7 23.4 %collective-permute-start = (bf16[128,3840]{1,0:T(8,128)(2,1)S(1)}, bf16[128,3840]{1,0:T(8,128)(2,1)S(1)}, u32[]{:S(2)}, u32[]{:S(2)}) collective-permute-start(bf16[128,3840]{1,0:T(8,128)(2,1)S(1)} %bitcast.20), channel_id=1, source_target_pairs={{0,24},{8,0},{16,8},{24,16},{1,25},{9,1},{17,9},{25,17},{2,26},{10... | collective-permute-start | bytes 2949128 | tf_op jit(solution)/shard_map/ppermute | solution.py:336
  21.7 4.5 %collective-permute-start.10 = (bf16[8,4864]{1,0:T(8,128)(2,1)S(1)}, bf16[8,4864]{1,0:T(8,128)(2,1)S(1)}, u32[]{:S(2)}, u32[]{:S(2)}) collective-permute-start(bf16[8,4864]{1,0:T(8,128)(2,1)S(1)} %get-tuple-element.42), channel_id=1, source_target_pairs={{0,2},{1,3},{2,0},{3,1},{4,6},{5,7},{6,4},{7,5},{8,10},{9,11},{10,... | collective-permute-start | bytes 233480 | tf_op jit(solution)/shard_map/ppermute | solution.py:329
  22.4 5.3 %collective-permute-start.11 = (bf16[8,4864]{1,0:T(8,128)(2,1)S(1)}, bf16[8,4864]{1,0:T(8,128)(2,1)S(1)}, u32[]{:S(2)}, u32[]{:S(2)}) collective-permute-start(bf16[8,4864]{1,0:T(8,128)(2,1)S(1)} %get-tuple-element.43), channel_id=1, source_target_pairs={{0,4},{1,5},{2,6},{3,7},{4,0},{5,1},{6,2},{7,3},{8,12},{9,13},{10,... | collective-permute-start | bytes 233480 | tf_op jit(solution)/shard_map/ppermute | solution.py:329
  24.3 6.4 %collective-permute-start.12 = (bf16[8,4864]{1,0:T(8,128)(2,1)S(1)}, bf16[8,4864]{1,0:T(8,128)(2,1)S(1)}, u32[]{:S(2)}, u32[]{:S(2)}) collective-permute-start(bf16[8,4864]{1,0:T(8,128)(2,1)S(1)} %get-tuple-element.44), channel_id=1, source_target_pairs={{0,6},{1,7},{2,4},{3,5},{4,2},{5,3},{6,0},{7,1},{8,14},{9,15},{10,... | collective-permute-start | bytes 233480 | tf_op jit(solution)/shard_map/ppermute | solution.py:329
  32.7 8.4 %collective-permute-start.13 = (bf16[2,3968]{1,0:T(2,128)(2,1)S(1)}, bf16[2,3968]{1,0:T(2,128)(2,1)S(1)}, u32[]{:S(2)}, u32[]{:S(2)}) collective-permute-start(bf16[2,3968]{1,0:T(2,128)(2,1)S(1)} %get-tuple-element.49), channel_id=1, source_target_pairs={{0,2},{1,3},{2,0},{3,1},{4,6},{5,7},{6,4},{7,5},{8,10},{9,11},{10,... | collective-permute-start | bytes 47624 | tf_op jit(solution)/shard_map/ppermute | solution.py:329
  32.8 8.4 %collective-permute-start.14 = (bf16[2,3968]{1,0:T(2,128)(2,1)S(1)}, bf16[2,3968]{1,0:T(2,128)(2,1)S(1)}, u32[]{:S(2)}, u32[]{:S(2)}) collective-permute-start(bf16[2,3968]{1,0:T(2,128)(2,1)S(1)} %get-tuple-element.50), channel_id=1, source_target_pairs={{0,4},{1,5},{2,6},{3,7},{4,0},{5,1},{6,2},{7,3},{8,12},{9,13},{10,... | collective-permute-start | bytes 47624 | tf_op jit(solution)/shard_map/ppermute | solution.py:329
  35.2 6.0 %collective-permute-start.15 = (bf16[2,3968]{1,0:T(2,128)(2,1)S(1)}, bf16[2,3968]{1,0:T(2,128)(2,1)S(1)}, u32[]{:S(2)}, u32[]{:S(2)}) collective-permute-start(bf16[2,3968]{1,0:T(2,128)(2,1)S(1)} %get-tuple-element.51), channel_id=1, source_target_pairs={{0,6},{1,7},{2,4},{3,5},{4,2},{5,3},{6,0},{7,1},{8,14},{9,15},{10,... | collective-permute-start | bytes 47624 | tf_op jit(solution)/shard_map/ppermute | solution.py:329

commit v9 on v8

--- a/solution.py
+++ b/solution.py
@@ -356,7 +356,6 @@
         operands=4,
         limit=LIMIT,
     )(*small)
-    *own, picked[0] = lax.optimization_barrier((*own, picked[0]))
     others += [across(array) for array in own[1:]]
     others[0], picked[1] = lax.optimization_barrier((others[0], picked[1]))
     got = along_all(picked)

time: 42.6 us -> 42.3 us (level)
  no operation moved by 1% of the time
where the time goes in v9:
time: 42.3 us; the launch traced here: 42.2 us
  starting transfers between devices  20 us (47%)
  waiting for transfers between devices  13.9 us (33%)
  Pallas kernels  7.37 us (17%)
  between operations  0.78 us (2%)
    ppermute x9, starting transfers between devices, along(): lax.ppermute(block, 'expert', [(i, i ^ 2 * k) for i in range(devices)])  14.4 us
    ppermute x3, waiting for transfers between devices, relay(): return lax.ppermute(block, 'pipe', route)  7.51 us
    ppermute x9, waiting for transfers between devices, along(): lax.ppermute(block, 'expert', [(i, i ^ 2 * k) for i in range(devices)])  6.42 us
    ppermute x3, starting transfers between devices, relay(): return lax.ppermute(block, 'pipe', route)  4.59 us
    pallas_call x1, Pallas kernels, local_chip(): call(step_one_kernel, 'step_one', [pair] * E_FLY, [pltpu.VMEM((PAIRS, pie...  2.08 us
    pallas_call x1, Pallas kernels, local_chip(): call(step_zero_kernel, 'step_zero', [jax.ShapeDtypeStruct((PAIRS, feature...  1.89 us
    pallas_call x1, Pallas kernels, local_chip(): call(pick_kernel, 'pick_rows', [pltpu.VMEM(pair.shape, BF16)] * E_FLY + [...  1.55 us
    pallas_call x1, Pallas kernels, local_chip(): call(final_kernel, 'final_sums', [jax.ShapeDtypeStruct((tokens, features)...  1.26 us
  transfers between devices with their start and end apart: 16, of which 6 were waited for; matrix products, arithmetic and copies ran while one was open for 0% of the time, Pallas kernels for 14%

profile of v9, /device:TPU:0, one launch (start us, length us, event | category | flops | bytes accessed | tf_op | source)
XLA Modules:
  0.0 42.2 jit_solution(3626135958734704132)
XLA Ops:
  0.6 0.0 copy-start.3
  0.6 0.5 %collective-permute-start.3 = (bf16[128,3840]{1,0:T(8,128)(2,1)}, bf16[128,3840]{1,0:T(8,128)(2,1)S(1)}, u32[]{:S(2)}, u32[]{:S(2)}) collective-permute-start(bf16[128,3840]{1,0:T(8,128)(2,1)} %bitcast.21), channel_id=1, source_target_pairs={{0,1},{1,0},{2,3},{3,2},{4,5},{5,4},{6,7},{7,6},{8,9},{9,8},{10,11... | collective-permute-start | bytes 2949128 | tf_op jit(solution)/shard_map/ppermute | solution.py:324
  1.2 0.1 collective-permute-start.7
  1.2 0.4 %collective-permute-start.1 = (bf16[3840,128]{1,0:T(8,128)(2,1)}, bf16[3840,128]{1,0:T(8,128)(2,1)S(1)}, u32[]{:S(2)}, u32[]{:S(2)}) collective-permute-start(bf16[3840,128]{1,0:T(8,128)(2,1)} %bitcast.24), channel_id=1, source_target_pairs={{0,1},{1,0},{2,3},{3,2},{4,5},{5,4},{6,7},{7,6},{8,9},{9,8},{10,11... | collective-permute-start | bytes 2949128 | tf_op jit(solution)/shard_map/ppermute | solution.py:324
  1.7 1.5 %pick_rows.1 = (bf16[2,3968]{1,0:T(2,128)(2,1)S(1)}, bf16[2,3968]{1,0:T(2,128)(2,1)S(1)}, bf16[2,3968]{1,0:T(2,128)(2,1)S(1)}, bf16[2,3968]{1,0:T(2,128)(2,1)S(1)}, f32[4,128]{1,0:T(4,128)S(1)}) custom-call(s32[2,2,128]{2,1,0:T(2,128)} %bitcast.30, s32[2,2,128]{2,1,0:T(2,128)} %bitcast.34, bf16[2,2,128]{2,1,0:T(2,128)(2,1)} %bitcast.40, ...), custom_call_target="tpu_custom_call" | custom-call | tf_op jit(solution)/shard_map/pick_rows/pallas_call | solution.py:348
  3.2 3.7 %collective-permute-start.5 = (bf16[2,3968]{1,0:T(2,128)(2,1)S(1)}, bf16[2,3968]{1,0:T(2,128)(2,1)S(1)}, u32[]{:S(2)}, u32[]{:S(2)}) collective-permute-start(bf16[2,3968]{1,0:T(2,128)(2,1)S(1)} %get-tuple-element.29), channel_id=1, source_target_pairs={{0,4},{1,5},{2,6},{3,7},{4,0},{5,1},{6,2},{7,3},{8,12},{9,13},{10,... | collective-permute-start | bytes 47624 | tf_op jit(solution)/shard_map/ppermute | solution.py:329
  7.0 1.3 %collective-permute-start.6 = (bf16[2,3968]{1,0:T(2,128)(2,1)S(1)}, bf16[2,3968]{1,0:T(2,128)(2,1)S(1)}, u32[]{:S(2)}, u32[]{:S(2)}) collective-permute-start(bf16[2,3968]{1,0:T(2,128)(2,1)S(1)} %get-tuple-element.30), channel_id=1, source_target_pairs={{0,6},{1,7},{2,4},{3,5},{4,2},{5,3},{6,0},{7,1},{8,14},{9,15},{10,... | collective-permute-start | bytes 47624 | tf_op jit(solution)/shard_map/ppermute | solution.py:329
  8.3 0.0 collective-permute-done.3.refs_6_.refs_7_
  8.3 0.0 copy-done.3
  8.3 0.0 collective-permute-start.8
  8.3 0.0 copy-start.1
  8.3 0.0 copy-start.2
  8.3 0.0 collective-permute-done.7.acts_other
  8.4 0.5 %collective-permute-start.4 = (bf16[2,3968]{1,0:T(2,128)(2,1)S(1)}, bf16[2,3968]{1,0:T(2,128)(2,1)S(1)}, u32[]{:S(2)}, u32[]{:S(2)}) collective-permute-start(bf16[2,3968]{1,0:T(2,128)(2,1)S(1)} %get-tuple-element.28), channel_id=1, source_target_pairs={{0,2},{1,3},{2,0},{3,1},{4,6},{5,7},{6,4},{7,5},{8,10},{9,11},{10,... | collective-permute-start | bytes 47624 | tf_op jit(solution)/shard_map/ppermute | solution.py:329
  8.8 0.0 copy-done.6
  8.8 0.2 factors.1.refs_4_
  9.0 0.0 collective-permute-done.1.refs_8_.refs_9_
  9.0 1.5 %collective-permute-start.2 = (f32[4,128]{1,0:T(4,128)S(1)}, f32[4,128]{1,0:T(4,128)S(1)}, u32[]{:S(2)}, u32[]{:S(2)}) collective-permute-start(f32[4,128]{1,0:T(4,128)S(1)} %get-tuple-element.25), channel_id=1, source_target_pairs={{0,8},{8,16},{16,24},{24,0},{1,9},{9,17},{17,25},{25,1},{2,10},{10... | collective-permute-start | bytes 6152 | tf_op jit(solution)/shard_map/ppermute | solution.py:336
  10.6 0.0 collective-permute-done.5.refs_2_
  10.6 1.9 %collective-permute-done.6.refs_3_ = bf16[2,3968]{1,0:T(2,128)(2,1)S(1)} collective-permute-done((bf16[2,3968]{1,0:T(2,128)(2,1)S(1)}, bf16[2,3968]{1,0:T(2,128)(2,1)S(1)}, u32[]{:S(2)}, u32[]{:S(2)}) %collective-permute-start.6) | collective-permute-done | bytes 15904 | tf_op jit(solution)/shard_map/ppermute | solution.py:329
  12.5 0.0 collective-permute-done.8.refs_10_.refs_11_
  12.5 0.0 collective-permute-done.4.refs_1_
  12.5 0.0 copy-done.1
  12.5 0.0 copy-start
  12.5 0.0 copy-start.4
  12.5 0.0 copy-start.5
  12.5 1.9 %step_zero.1 = (bf16[8,3840]{1,0:T(8,128)(2,1)S(1)}, f32[8,128]{1,0:T(8,128)S(1)}) custom-call(bf16[2,3968]{1,0:T(2,128)(2,1)S(1)} %get-tuple-element.26.refs_0_, bf16[2,3968]{1,0:T(2,128)(2,1)S(1)} %collective-permute-done.4.refs_1_, bf16[2,3968]{1,0:T(2,128)(2,1)S(1)} %collective-permute-done.5.refs_2_, ...), custom_call_target="tpu_custom_call" | custom-call | flops 20000000000 | tf_op jit(solution)/shard_map/step_zero/pallas_call | solution.py:373
  14.4 0.0 collective-permute-done.2.table
  14.4 0.0 copy-done.4
  14.5 0.3 rows_ahead.1
  14.8 2.5 %collective-permute-start.9 = (bf16[8,8064]{1,0:T(8,128)(2,1)S(1)}, bf16[8,8064]{1,0:T(8,128)(2,1)S(1)}, u32[]{:S(2)}, u32[]{:S(2)}) collective-permute-start(bf16[8,8064]{1,0:T(8,128)(2,1)S(1)} %rows_ahead.1), channel_id=1, source_target_pairs={{0,24},{8,0},{16,8},{24,16},{1,25},{9,1},{17,9},{25,17},{2,26},{10... | collective-permute-start | bytes 387080 | tf_op jit(solution)/shard_map/ppermute | solution.py:336
  17.3 0.5 %collective-permute-start = (bf16[128,3840]{1,0:T(8,128)(2,1)S(1)}, bf16[128,3840]{1,0:T(8,128)(2,1)S(1)}, u32[]{:S(2)}, u32[]{:S(2)}) collective-permute-start(bf16[128,3840]{1,0:T(8,128)(2,1)S(1)} %bitcast.20), channel_id=1, source_target_pairs={{0,24},{8,0},{16,8},{24,16},{1,25},{9,1},{17,9},{25,17},{2,26},{10... | collective-permute-start | bytes 2949128 | tf_op jit(solution)/shard_map/ppermute | solution.py:336
  17.9 3.4 %collective-permute-done.9.came.refs_2_.refs_0_ = bf16[8,8064]{1,0:T(8,128)(2,1)S(1)} collective-permute-done((bf16[8,8064]{1,0:T(8,128)(2,1)S(1)}, bf16[8,8064]{1,0:T(8,128)(2,1)S(1)}, u32[]{:S(2)}, u32[]{:S(2)}) %collective-permute-start.9) | collective-permute-done | bytes 129056 | tf_op jit(solution)/shard_map/ppermute | solution.py:336
  21.3 0.8 %collective-permute-start.10 = (bf16[8,4864]{1,0:T(8,128)(2,1)S(1)}, bf16[8,4864]{1,0:T(8,128)(2,1)S(1)}, u32[]{:S(2)}, u32[]{:S(2)}) collective-permute-start(bf16[8,4864]{1,0:T(8,128)(2,1)S(1)} %get-tuple-element.34), channel_id=1, source_target_pairs={{0,2},{1,3},{2,0},{3,1},{4,6},{5,7},{6,4},{7,5},{8,10},{9,11},{10,... | collective-permute-start | bytes 233480 | tf_op jit(solution)/shard_map/ppermute | solution.py:329
  22.0 2.0 %collective-permute-start.11 = (bf16[8,4864]{1,0:T(8,128)(2,1)S(1)}, bf16[8,4864]{1,0:T(8,128)(2,1)S(1)}, u32[]{:S(2)}, u32[]{:S(2)}) collective-permute-start(bf16[8,4864]{1,0:T(8,128)(2,1)S(1)} %get-tuple-element.35), channel_id=1, source_target_pairs={{0,4},{1,5},{2,6},{3,7},{4,0},{5,1},{6,2},{7,3},{8,12},{9,13},{10,... | collective-permute-start | bytes 233480 | tf_op jit(solution)/shard_map/ppermute | solution.py:329
  24.0 1.7 %collective-permute-start.12 = (bf16[8,4864]{1,0:T(8,128)(2,1)S(1)}, bf16[8,4864]{1,0:T(8,128)(2,1)S(1)}, u32[]{:S(2)}, u32[]{:S(2)}) collective-permute-start(bf16[8,4864]{1,0:T(8,128)(2,1)S(1)} %get-tuple-element.36), channel_id=1, source_target_pairs={{0,6},{1,7},{2,4},{3,5},{4,2},{5,3},{6,0},{7,1},{8,14},{9,15},{10,... | collective-permute-start | bytes 233480 | tf_op jit(solution)/shard_map/ppermute | solution.py:329
  25.7 0.9 %collective-permute-done.10.refs_3_.refs_1_ = bf16[8,4864]{1,0:T(8,128)(2,1)S(1)} collective-permute-done((bf16[8,4864]{1,0:T(8,128)(2,1)S(1)}, bf16[8,4864]{1,0:T(8,128)(2,1)S(1)}, u32[]{:S(2)}, u32[]{:S(2)}) %collective-permute-start.10) | collective-permute-done | bytes 77856 | tf_op jit(solution)/shard_map/ppermute | solution.py:329
  26.6 0.8 %collective-permute-done.11.refs_4_.refs_2_ = bf16[8,4864]{1,0:T(8,128)(2,1)S(1)} collective-permute-done((bf16[8,4864]{1,0:T(8,128)(2,1)S(1)}, bf16[8,4864]{1,0:T(8,128)(2,1)S(1)}, u32[]{:S(2)}, u32[]{:S(2)}) %collective-permute-start.11) | collective-permute-done | bytes 77856 | tf_op jit(solution)/shard_map/ppermute | solution.py:329
  27.4 2.8 %collective-permute-done.12.refs_5_.refs_3_ = bf16[8,4864]{1,0:T(8,128)(2,1)S(1)} collective-permute-done((bf16[8,4864]{1,0:T(8,128)(2,1)S(1)}, bf16[8,4864]{1,0:T(8,128)(2,1)S(1)}, u32[]{:S(2)}, u32[]{:S(2)}) %collective-permute-start.12) | collective-permute-done | bytes 77856 | tf_op jit(solution)/shard_map/ppermute | solution.py:329
  30.2 2.1 %step_one.1 = (bf16[2,3968]{1,0:T(2,128)(2,1)S(1)}, bf16[2,3968]{1,0:T(2,128)(2,1)S(1)}, bf16[2,3968]{1,0:T(2,128)(2,1)S(1)}, bf16[2,3968]{1,0:T(2,128)(2,1)S(1)}) custom-call(bf16[8,8064]{1,0:T(8,128)(2,1)S(1)} %collective-permute-done.9.came.refs_2_.refs_0_, bf16[8,4864]{1,0:T(8,128)(2,1)S(1)} %collective-permute-done.10.refs_3_.refs_1_, ...), custom_call_target="tpu_custom_call" | custom-call | tf_op jit(solution)/shard_map/step_one/pallas_call | solution.py:395
  32.3 0.0 collective-permute-start.13
  32.3 2.4 %collective-permute-start.14 = (bf16[2,3968]{1,0:T(2,128)(2,1)S(1)}, bf16[2,3968]{1,0:T(2,128)(2,1)S(1)}, u32[]{:S(2)}, u32[]{:S(2)}) collective-permute-start(bf16[2,3968]{1,0:T(2,128)(2,1)S(1)} %get-tuple-element.42), channel_id=1, source_target_pairs={{0,4},{1,5},{2,6},{3,7},{4,0},{5,1},{6,2},{7,3},{8,12},{9,13},{10,... | collective-permute-start | bytes 47624 | tf_op jit(solution)/shard_map/ppermute | solution.py:329
  34.7 2.0 %collective-permute-start.15 = (bf16[2,3968]{1,0:T(2,128)(2,1)S(1)}, bf16[2,3968]{1,0:T(2,128)(2,1)S(1)}, u32[]{:S(2)}, u32[]{:S(2)}) collective-permute-start(bf16[2,3968]{1,0:T(2,128)(2,1)S(1)} %get-tuple-element.43), channel_id=1, source_target_pairs={{0,6},{1,7},{2,4},{3,5},{4,2},{5,3},{6,0},{7,1},{8,14},{9,15},{10,... | collective-permute-start | bytes 47624 | tf_op jit(solution)/shard_map/ppermute | solution.py:329
  36.7 4.1 %collective-permute-done.refs_0_ = bf16[128,3840]{1,0:T(8,128)(2,1)S(1)} collective-permute-done((bf16[128,3840]{1,0:T(8,128)(2,1)S(1)}, bf16[128,3840]{1,0:T(8,128)(2,1)S(1)}, u32[]{:S(2)}, u32[]{:S(2)}) %collective-permute-start) | collective-permute-done | bytes 983072 | tf_op jit(solution)/shard_map/ppermute | solution.py:336
  40.9 0.0 collective-permute-done.13.refs_6_
  40.9 0.0 collective-permute-done.14.refs_7_
  40.9 0.0 collective-permute-done.15.refs_8_
  40.9 1.3 %final_sums.1 = (bf16[128,3840]{1,0:T(8,128)(2,1)}, f32[2,2,128]{2,1,0:T(2,128)}) custom-call(bf16[128,3840]{1,0:T(8,128)(2,1)S(1)} %collective-permute-done.refs_0_, f32[8,3840]{1,0:T(8,128)S(1)} %get-tuple-element.37.refs_1_, bf16[16,128]{1,0:T(8,128)(2,1)S(1)} %get-tuple-element.38.refs_2_, s32[2,2,128]{2,1,0:T(2,128)S(1)} %bitcast.33, ...), custom_call_target="tpu_custom_call" | custom-call | tf_op jit(solution)/shard_map/final_sums/pallas_call | solution.py:413
  (6 shorter events, 0.1 us)
Async XLA Ops:
  0.6 7.7 %copy-start.3 = (bf16[1,3840,128]{2,1,0:T(8,128)(2,1)S(1)}, bf16[1,3840,128]{2,1,0:T(8,128)(2,1)}, u32[]{:S(2)}) copy-start(bf16[1,3840,128]{2,1,0:T(8,128)(2,1)} %param.14) | copy-start | bytes 2949124
  0.6 7.7 %collective-permute-start.3 = (bf16[128,3840]{1,0:T(8,128)(2,1)}, bf16[128,3840]{1,0:T(8,128)(2,1)S(1)}, u32[]{:S(2)}, u32[]{:S(2)}) collective-permute-start(bf16[128,3840]{1,0:T(8,128)(2,1)} %bitcast.21), channel_id=1, source_target_pairs={{0,1},{1,0},{2,3},{3,2},{4,5},{5,4},{6,7},{7,6},{8,9},{9,8},{10,11... | collective-permute-start | bytes 2949128 | tf_op jit(solution)/shard_map/ppermute | solution.py:324
  1.2 7.2 %collective-permute-start.7 = (bf16[2,16,2,128]{3,2,1,0:T(2,128)(2,1)}, bf16[2,16,2,128]{3,2,1,0:T(2,128)(2,1)S(1)}, u32[]{:S(2)}, u32[]{:S(2)}) collective-permute-start(bf16[2,16,2,128]{3,2,1,0:T(2,128)(2,1)} %bitcast.38), channel_id=1, source_target_pairs={{0,1},{1,0},{2,3},{3,2},{4,5},{5,4},{6,7},{7,6},{8,9},{9,8},{10,11... | collective-permute-start | bytes 49160 | tf_op jit(solution)/shard_map/ppermute | solution.py:324
  1.2 7.8 %collective-permute-start.1 = (bf16[3840,128]{1,0:T(8,128)(2,1)}, bf16[3840,128]{1,0:T(8,128)(2,1)S(1)}, u32[]{:S(2)}, u32[]{:S(2)}) collective-permute-start(bf16[3840,128]{1,0:T(8,128)(2,1)} %bitcast.24), channel_id=1, source_target_pairs={{0,1},{1,0},{2,3},{3,2},{4,5},{5,4},{6,7},{7,6},{8,9},{9,8},{10,11... | collective-permute-start | bytes 2949128 | tf_op jit(solution)/shard_map/ppermute | solution.py:324
  1.7 7.1 %copy-start.6 = (bf16[1,2,16,2,128]{4,3,2,1,0:T(2,128)(2,1)S(1)}, bf16[1,2,16,2,128]{4,3,2,1,0:T(2,128)(2,1)}, u32[]{:S(2)}) copy-start(bf16[1,2,16,2,128]{4,3,2,1,0:T(2,128)(2,1)} %param.12) | copy-start | bytes 49156
  3.2 7.3 %collective-permute-start.5 = (bf16[2,3968]{1,0:T(2,128)(2,1)S(1)}, bf16[2,3968]{1,0:T(2,128)(2,1)S(1)}, u32[]{:S(2)}, u32[]{:S(2)}) collective-permute-start(bf16[2,3968]{1,0:T(2,128)(2,1)S(1)} %get-tuple-element.29), channel_id=1, source_target_pairs={{0,4},{1,5},{2,6},{3,7},{4,0},{5,1},{6,2},{7,3},{8,12},{9,13},{10,... | collective-permute-start | bytes 47624 | tf_op jit(solution)/shard_map/ppermute | solution.py:329
  7.0 5.5 %collective-permute-start.6 = (bf16[2,3968]{1,0:T(2,128)(2,1)S(1)}, bf16[2,3968]{1,0:T(2,128)(2,1)S(1)}, u32[]{:S(2)}, u32[]{:S(2)}) collective-permute-start(bf16[2,3968]{1,0:T(2,128)(2,1)S(1)} %get-tuple-element.30), channel_id=1, source_target_pairs={{0,6},{1,7},{2,4},{3,5},{4,2},{5,3},{6,0},{7,1},{8,14},{9,15},{10,... | collective-permute-start | bytes 47624 | tf_op jit(solution)/shard_map/ppermute | solution.py:329
  8.3 4.2 %collective-permute-start.8 = (bf16[3840,128]{1,0:T(8,128)(2,1)S(1)}, bf16[3840,128]{1,0:T(8,128)(2,1)S(1)}, u32[]{:S(2)}, u32[]{:S(2)}) collective-permute-start(bf16[3840,128]{1,0:T(8,128)(2,1)S(1)} %bitcast.27), channel_id=1, source_target_pairs={{0,1},{1,0},{2,3},{3,2},{4,5},{5,4},{6,7},{7,6},{8,9},{9,8},{10,11... | collective-permute-start | bytes 2949128 | tf_op jit(solution)/shard_map/ppermute | solution.py:324
  8.3 4.2 %copy-start.1 = (bf16[1,128,3840]{2,1,0:T(8,128)(2,1)S(1)}, bf16[1,128,3840]{2,1,0:T(8,128)(2,1)}, u32[]{:S(2)}) copy-start(bf16[1,128,3840]{2,1,0:T(8,128)(2,1)} %param.15) | copy-start | bytes 2949124
  8.3 4.2 %copy-start.2 = (bf16[1,3840,128]{2,1,0:T(8,128)(2,1)S(1)}, bf16[1,3840,128]{2,1,0:T(8,128)(2,1)}, u32[]{:S(2)}) copy-start(bf16[1,3840,128]{2,1,0:T(8,128)(2,1)} %param.13) | copy-start | bytes 2949124
  8.4 4.1 %collective-permute-start.4 = (bf16[2,3968]{1,0:T(2,128)(2,1)S(1)}, bf16[2,3968]{1,0:T(2,128)(2,1)S(1)}, u32[]{:S(2)}, u32[]{:S(2)}) collective-permute-start(bf16[2,3968]{1,0:T(2,128)(2,1)S(1)} %get-tuple-element.28), channel_id=1, source_target_pairs={{0,2},{1,3},{2,0},{3,1},{4,6},{5,7},{6,4},{7,5},{8,10},{9,11},{10,... | collective-permute-start | bytes 47624 | tf_op jit(solution)/shard_map/ppermute | solution.py:329
  9.0 5.4 %collective-permute-start.2 = (f32[4,128]{1,0:T(4,128)S(1)}, f32[4,128]{1,0:T(4,128)S(1)}, u32[]{:S(2)}, u32[]{:S(2)}) collective-permute-start(f32[4,128]{1,0:T(4,128)S(1)} %get-tuple-element.25), channel_id=1, source_target_pairs={{0,8},{8,16},{16,24},{24,0},{1,9},{9,17},{17,25},{25,1},{2,10},{10... | collective-permute-start | bytes 6152 | tf_op jit(solution)/shard_map/ppermute | solution.py:336
  12.5 1.9 %copy-start = (bf16[1,128,3840]{2,1,0:T(8,128)(2,1)S(1)}, bf16[1,128,3840]{2,1,0:T(8,128)(2,1)}, u32[]{:S(2)}) copy-start(bf16[1,128,3840]{2,1,0:T(8,128)(2,1)} %param.8) | copy-start | bytes 2949124
  12.5 1.9 %copy-start.4 = (s32[1,2,128,2]{2,3,1,0:T(2,128)S(1)}, s32[1,2,128,2]{2,3,1,0:T(2,128)}, u32[]{:S(2)}) copy-start(s32[1,2,128,2]{2,3,1,0:T(2,128)} %param.9) | copy-start | bytes 6148
  12.5 1.9 %copy-start.5 = (s32[1,2,128,2]{2,3,1,0:T(2,128)S(1)}, s32[1,2,128,2]{2,3,1,0:T(2,128)}, u32[]{:S(2)}) copy-start(s32[1,2,128,2]{2,3,1,0:T(2,128)} %param.10) | copy-start | bytes 6148
  14.8 6.4 %collective-permute-start.9 = (bf16[8,8064]{1,0:T(8,128)(2,1)S(1)}, bf16[8,8064]{1,0:T(8,128)(2,1)S(1)}, u32[]{:S(2)}, u32[]{:S(2)}) collective-permute-start(bf16[8,8064]{1,0:T(8,128)(2,1)S(1)} %rows_ahead.1), channel_id=1, source_target_pairs={{0,24},{8,0},{16,8},{24,16},{1,25},{9,1},{17,9},{25,17},{2,26},{10... | collective-permute-start | bytes 387080 | tf_op jit(solution)/shard_map/ppermute | solution.py:336
  17.3 23.6 %collective-permute-start = (bf16[128,3840]{1,0:T(8,128)(2,1)S(1)}, bf16[128,3840]{1,0:T(8,128)(2,1)S(1)}, u32[]{:S(2)}, u32[]{:S(2)}) collective-permute-start(bf16[128,3840]{1,0:T(8,128)(2,1)S(1)} %bitcast.20), channel_id=1, source_target_pairs={{0,24},{8,0},{16,8},{24,16},{1,25},{9,1},{17,9},{25,17},{2,26},{10... | collective-permute-start | bytes 2949128 | tf_op jit(solution)/shard_map/ppermute | solution.py:336
  21.3 5.3 %collective-permute-start.10 = (bf16[8,4864]{1,0:T(8,128)(2,1)S(1)}, bf16[8,4864]{1,0:T(8,128)(2,1)S(1)}, u32[]{:S(2)}, u32[]{:S(2)}) collective-permute-start(bf16[8,4864]{1,0:T(8,128)(2,1)S(1)} %get-tuple-element.34), channel_id=1, source_target_pairs={{0,2},{1,3},{2,0},{3,1},{4,6},{5,7},{6,4},{7,5},{8,10},{9,11},{10,... | collective-permute-start | bytes 233480 | tf_op jit(solution)/shard_map/ppermute | solution.py:329
  22.0 5.4 %collective-permute-start.11 = (bf16[8,4864]{1,0:T(8,128)(2,1)S(1)}, bf16[8,4864]{1,0:T(8,128)(2,1)S(1)}, u32[]{:S(2)}, u32[]{:S(2)}) collective-permute-start(bf16[8,4864]{1,0:T(8,128)(2,1)S(1)} %get-tuple-element.35), channel_id=1, source_target_pairs={{0,4},{1,5},{2,6},{3,7},{4,0},{5,1},{6,2},{7,3},{8,12},{9,13},{10,... | collective-permute-start | bytes 233480 | tf_op jit(solution)/shard_map/ppermute | solution.py:329
  24.0 6.2 %collective-permute-start.12 = (bf16[8,4864]{1,0:T(8,128)(2,1)S(1)}, bf16[8,4864]{1,0:T(8,128)(2,1)S(1)}, u32[]{:S(2)}, u32[]{:S(2)}) collective-permute-start(bf16[8,4864]{1,0:T(8,128)(2,1)S(1)} %get-tuple-element.36), channel_id=1, source_target_pairs={{0,6},{1,7},{2,4},{3,5},{4,2},{5,3},{6,0},{7,1},{8,14},{9,15},{10,... | collective-permute-start | bytes 233480 | tf_op jit(solution)/shard_map/ppermute | solution.py:329
  32.3 8.6 %collective-permute-start.13 = (bf16[2,3968]{1,0:T(2,128)(2,1)S(1)}, bf16[2,3968]{1,0:T(2,128)(2,1)S(1)}, u32[]{:S(2)}, u32[]{:S(2)}) collective-permute-start(bf16[2,3968]{1,0:T(2,128)(2,1)S(1)} %get-tuple-element.41), channel_id=1, source_target_pairs={{0,2},{1,3},{2,0},{3,1},{4,6},{5,7},{6,4},{7,5},{8,10},{9,11},{10,... | collective-permute-start | bytes 47624 | tf_op jit(solution)/shard_map/ppermute | solution.py:329
  32.3 8.6 %collective-permute-start.14 = (bf16[2,3968]{1,0:T(2,128)(2,1)S(1)}, bf16[2,3968]{1,0:T(2,128)(2,1)S(1)}, u32[]{:S(2)}, u32[]{:S(2)}) collective-permute-start(bf16[2,3968]{1,0:T(2,128)(2,1)S(1)} %get-tuple-element.42), channel_id=1, source_target_pairs={{0,4},{1,5},{2,6},{3,7},{4,0},{5,1},{6,2},{7,3},{8,12},{9,13},{10,... | collective-permute-start | bytes 47624 | tf_op jit(solution)/shard_map/ppermute | solution.py:329
  34.7 6.2 %collective-permute-start.15 = (bf16[2,3968]{1,0:T(2,128)(2,1)S(1)}, bf16[2,3968]{1,0:T(2,128)(2,1)S(1)}, u32[]{:S(2)}, u32[]{:S(2)}) collective-permute-start(bf16[2,3968]{1,0:T(2,128)(2,1)S(1)} %get-tuple-element.43), channel_id=1, source_target_pairs={{0,6},{1,7},{2,4},{3,5},{4,2},{5,3},{6,0},{7,1},{8,14},{9,15},{10,... | collective-permute-start | bytes 47624 | tf_op jit(solution)/shard_map/ppermute | solution.py:329
